TPU v7x, 32 devices: a whole 2x2x4 slice. The times are simulated.
32 devices in a mesh: ccd: 4 (over z), patch: 8 (over y, x, core).
Axes of the slice: x: 2, y: 2, z: 4, core: 2. Of those that a mesh axis runs over, the one named last changes fastest.
Arguments:
- pixel_counts: bfloat16 [4, 1024, 4096], P('ccd', 'patch'), may hold values from -1.5 to 14
- pixel_weights: bfloat16 [4, 1024, 4096], P('ccd', 'patch'), may hold values from 0.5 to 2
- wave_profile: bfloat16 [4, 8, 64, 128, 128], P('ccd', 'patch'), may hold values from 0 to 1.65
- cross_profile: bfloat16 [4, 128, 16], P('ccd', 'patch'), may hold values from 0 to 1.5
- trace_columns: int32 [4, 128, 16], P('ccd', 'patch'), may hold values from -8 to 1031, as said below
- throughput: float32 [4], P('ccd'), may hold values from 0.8 to 3.75
- sky_fibres: int32 [4, 16], P('ccd'), may hold values from 0 to 127, as said below
- fibre_mask: int32 [4, 128], P('ccd'), may hold values 0 or 1
Outputs:
- calibrated: float32 [4, 128, 4096], P('ccd', None, 'patch')
- sky_model: float32 [4096], P('patch')
Inputs may be any that keep to these rules, and one draw needn't show every extreme that they name: trace_columns[c, f] lists 16 consecutive pixel columns in rising order, numbered from the camera's first column; each lies within 8 columns of the columns 8 * 16 * g to 8 * 16 * (g + 1) - 1 of the fibre's bundle g = f // 16. `sky_fibres`: each row holds 16 different fibre numbers.
All inputs are finite; a program needn't handle non-finite values. No bound on the sum of `fibre_mask` on one device may be relied on, other than what follows from the above.
Results may differ from a plain program's by a relative error of at most 0.0065.
Values may be sent and summed in bfloat16 or wider, within the bound.
No kernel may reach another device: no remote copies, remote signals or barrier semaphores. Data moves between devices by JAX's collectives and lax.ppermute only.
A program may use at most 64 MiB of HBM per device.

v0:
```python
import jax
import jax.numpy as jnp
from jax import lax
from jax.sharding import PartitionSpec as P

LW = 64
ITERS = 10
HALO = 8


RIDGE = 0.1
PRIOR = 1.0


def extended(cells, sides, width):
    for axis, dim in sides:
        count = lax.axis_size(axis)
        ends = count - 1
        head = lax.slice_in_dim(cells, 0, width, axis=dim)
        tail = lax.slice_in_dim(cells, cells.shape[dim] - width, cells.shape[dim], axis=dim)
        cells = jnp.concatenate(
            [
                lax.ppermute(tail, axis, [(i, (i + 1) % count) for i in range(ends)]),
                cells,
                lax.ppermute(head, axis, [((i + 1) % count, i) for i in range(ends)]),
            ],
            axis=dim,
        )
    return cells


def make_windows(pixel_block):
    margin = LW // 2
    patch_count = pixel_block.shape[1] // LW
    padded = jnp.pad(pixel_block, ((0, 0), (margin, margin)))
    pieces = padded.reshape(pixel_block.shape[0], patch_count + 1, LW)
    return jnp.concatenate([pieces[:, :-1], pieces[:, 1:]], axis=2)


def profile_matrix(local_columns, cross_rows, window_width):
    columns = jnp.arange(window_width, dtype=jnp.int32)
    matches = local_columns[:, :, None] == columns[None, None, :]
    summed = jnp.sum(
        jnp.where(matches, cross_rows.astype(jnp.float32)[:, :, None], jnp.float32(0.0)), axis=1
    )
    return summed.T.astype(jnp.bfloat16)


def extract_patches(counts_window, weights_window, profile, wave_rows):
    profile_wide = profile.astype(jnp.float32)
    column_total = jnp.sum(profile_wide, axis=1)
    spread_profile = (profile_wide * column_total[:, None]).astype(jnp.bfloat16)
    wave_wide = wave_rows.astype(jnp.float32)
    row_total = jnp.sum(wave_wide, axis=2)
    spread_wave = (wave_wide * row_total[:, :, None]).astype(jnp.bfloat16)
    mixed_sum = jnp.einsum(
        "cf,cpr->fpr", spread_profile, weights_window, preferred_element_type=jnp.float32
    ).astype(jnp.bfloat16)
    row_weight = (
        jnp.einsum("fpr,prl->fpl", mixed_sum, spread_wave, preferred_element_type=jnp.float32)
        + RIDGE
    )
    first_residual = (
        weights_window.astype(jnp.float32) * counts_window.astype(jnp.float32)
    ).astype(jnp.bfloat16)

    def relax(fluxes, residual):
        folded = jnp.einsum(
            "cf,cpr->fpr", profile, residual, preferred_element_type=jnp.float32
        ).astype(jnp.bfloat16)
        gradient = jnp.einsum("fpr,prl->fpl", folded, wave_rows, preferred_element_type=jnp.float32)
        return fluxes + (gradient - RIDGE * fluxes) / row_weight

    def sweep_step(iteration, fluxes):
        blurred = jnp.einsum(
            "fpl,prl->fpr",
            fluxes.astype(jnp.bfloat16),
            wave_rows,
            preferred_element_type=jnp.float32,
        ).astype(jnp.bfloat16)
        modelled = jnp.einsum("cf,fpr->cpr", profile, blurred, preferred_element_type=jnp.float32)
        residual = (
            weights_window.astype(jnp.float32) * (counts_window.astype(jnp.float32) - modelled)
        ).astype(jnp.bfloat16)
        return relax(fluxes, residual)

    fluxes = relax(jnp.zeros(row_weight.shape, jnp.float32), first_residual)
    fluxes = lax.fori_loop(1, ITERS, sweep_step, fluxes)
    return (fluxes, row_weight)


def per_device(
    pixel_counts,
    pixel_weights,
    wave_profile,
    cross_profile,
    trace_columns,
    throughput,
    sky_fibres,
    fibre_mask,
):
    column_count = pixel_counts.shape[1]
    fibre_count = trace_columns.shape[1]
    wave_count = pixel_counts.shape[2]
    window_width = column_count + 2 * HALO
    bundle_index = lax.axis_index("patch")
    stacked = jnp.stack([pixel_counts[0], pixel_weights[0]])
    widened = extended(stacked, (("patch", 1),), HALO)
    local_columns = trace_columns[0] - (bundle_index * column_count - HALO)
    profile = profile_matrix(local_columns, cross_profile[0], window_width)
    fluxes, row_weight = extract_patches(
        make_windows(widened[0]), make_windows(widened[1]), profile, wave_profile[0, 0]
    )
    margin = LW // 2
    extracted = fluxes[:, :, margin : margin + LW].reshape(fibre_count, wave_count)
    extracted_weight = row_weight[:, :, margin : margin + LW].reshape(fibre_count, wave_count)
    gain = throughput[0]
    mask_all = fibre_mask[0].astype(jnp.float32)
    flux_all, weight_all = (
        lax.all_to_all(extracted, "patch", split_axis=1, concat_axis=0, tiled=True),
        lax.all_to_all(extracted_weight, "patch", split_axis=1, concat_axis=0, tiled=True),
    )
    fibres = jnp.arange(flux_all.shape[0], dtype=jnp.int32)
    is_sky = jnp.any(sky_fibres[0][:, None] == fibres[None, :], axis=0)
    selected = mask_all * is_sky.astype(jnp.float32)
    sky_terms = jnp.sum(selected[:, None] * gain * weight_all * flux_all, axis=0)
    weight_terms = jnp.sum(selected[:, None] * (gain * gain) * weight_all, axis=0)
    sky_total, weight_total = lax.psum((sky_terms, weight_terms), "ccd")
    sky_part = sky_total / (PRIOR + weight_total)
    calibrated = mask_all[:, None] * (flux_all - gain * sky_part[None, :])
    return (calibrated[None], sky_part)


def solution(mesh):
    return jax.shard_map(
        per_device,
        mesh=mesh,
        in_specs=(
            P("ccd", "patch", None),
            P("ccd", "patch", None),
            P("ccd", "patch", None, None, None),
            P("ccd", "patch", None),
            P("ccd", "patch", None),
            P("ccd"),
            P("ccd", None),
            P("ccd", None),
        ),
        out_specs=(P("ccd", None, "patch"), P("patch")),
        check_vma=False,
    )
```

profile of v0, /device:TPU:0, one launch (start us, length us, event | category | flops | bytes accessed | tf_op | source)
XLA Modules:
  0.0 154.3 jit_solution(4973995466646082887)
XLA Ops:
  8.2 3.2 %collective-permute-done.1 = bf16[2,8,4096]{2,1,0:T(8,128)(2,1)S(1)} collective-permute-done((bf16[2,8,4096]{2,1,0:T(8,128)(2,1)S(1)}, bf16[2,8,4096]{2,1,0:T(8,128)(2,1)S(1)}, u32[]{:S(2)}, u32[]{:S(2)}) %collective-permute-start.1) | collective-permute-done | bytes 131104 | tf_op jit(solution)/shard_map/ppermute | solution.py:25
  17.6 3.8 %fusion.50 = (bf16[144,64,64]{2,1,0:T(8,128)(2,1)S(1)}, bf16[144,64,64]{2,1,0:T(8,128)(2,1)S(1)}) fusion(bf16[144,65,64]{2,1,0:T(8,128)(2,1)} %reshape.126), kind=kLoop, calls=%fused_computation.65 | loop fusion | bytes 4718592 | tf_op jit(solution)/shard_map/slice | solution.py:37
  21.4 2.9 %copy.39 = bf16[144,64,64]{2,0,1:T(8,128)(2,1)} copy(bf16[144,64,64]{2,1,0:T(8,128)(2,1)S(1)} %get-tuple-element.62) | data formatting | bytes 2359296
  24.3 2.9 %copy.40 = bf16[144,64,64]{2,0,1:T(8,128)(2,1)} copy(bf16[144,64,64]{2,1,0:T(8,128)(2,1)S(1)} %get-tuple-element.63) | data formatting | bytes 2359296
  27.7 2.8 %reshape.127 = bf16[144,65,64]{2,1,0:T(8,128)(2,1)} reshape(bf16[144,4160]{1,0:T(8,128)(2,1)S(1)} %pad.8) | data formatting | bytes 2396160 | tf_op jit(solution)/shard_map/reshape | solution.py:36
  30.5 3.8 %fusion.49 = (bf16[144,64,64]{2,1,0:T(8,128)(2,1)S(1)}, bf16[144,64,64]{2,1,0:T(8,128)(2,1)S(1)}) fusion(bf16[144,65,64]{2,1,0:T(8,128)(2,1)} %reshape.127), kind=kLoop, calls=%fused_computation.64 | loop fusion | bytes 4718592 | tf_op jit(solution)/shard_map/slice | solution.py:37
  38.2 4.1 %pad_maximum_fusion.1 = (bf16[144,64,128]{2,0,1:T(8,128)(2,1)}, bf16[144,64,128]{2,0,1:T(8,128)(2,1)}) fusion(bf16[144,64,64]{2,0,1:T(8,128)(2,1)S(1)} %copy-done.2, bf16[144,64,64]{2,0,1:T(8,128)(2,1)S(1)} %copy-done.1, bf16[144,64,64]{2,0,1:T(8,128)(2,1)S(1)} %copy.42, bf16[144,64,64]{2,0,1:T(8,128)(2,1)S(1)} %copy.41), kind=kLoop, calls=%fused_computation.21 | loop fusion | flops 9437184 | bytes 9437184 | tf_op jit(solution)/shard_map/concatenate | solution.py:37
  42.3 2.9 %fusion.28 = f32[16,64,128]{2,0,1:T(8,128)S(1)} fusion(f32[64,128]{1,0:T(8,128)S(1)} %convert_reduce_fusion, bf16[144,64,128]{2,0,1:T(8,128)(2,1)} %get-tuple-element.117, f32[144]{0:T(256)S(1)} %convert_reduce_fusion.1, bf16[1,1,64,128,128]{4,3,2,1,0:T(8,128)(2,1)S(1)} %copy-done, bf16[16,144]{1,0:T(8,128)(2,1)S(1)} %select_reduce_fusion), kind=kOutput, calls=%fused_computation.28 | convolution fusion | flops 74717952 | bytes 5018688 | tf_op jit(solution)/shard_map/fpr,prl->fpl/dot_general | solution.py:60
  45.3 3.6 %fusion.24 = f32[16,64,128]{2,0,1:T(8,128)S(1)} fusion(f32[16,64,128]{2,0,1:T(8,128)S(1)} %fusion.28, bf16[144,64,128]{2,0,1:T(8,128)(2,1)} %get-tuple-element.118, bf16[144,64,128]{2,0,1:T(8,128)(2,1)} %get-tuple-element.117, bf16[16,144]{1,0:T(8,128)(2,1)S(1)} %select_reduce_fusion, bf16[1,1,64,128,128]{4,3,2,1,0:T(8,128)(2,1)S(1)} %copy-done), kind=kOutput, calls=%fused_computation.26 | convolution fusion | flops 76283904 | bytes 7868928 | tf_op jit(solution)/shard_map/fpr,prl->fpl/dot_general | solution.py:71
  48.8 66.5 %while.10 = (s32[]{:T(128)}, f32[16,64,128]{2,0,1:T(8,128)S(1)}, bf16[144,64,128]{2,0,1:T(8,128)(2,1)}, bf16[144,64,128]{2,0,1:T(8,128)(2,1)}, bf16[64,128,128]{...) while((s32[]{:T(128)}, f32[16,64,128]{2,0,1:T(8,128)S(1)}, ...), condition=%wide.region_4.5_spmd, body=%wide.region_3.4_spmd.sunk | while | flops 149422080 | bytes 12063317 | solution.py:88
  50.0 4.6 %fusion.79 = bf16[16,64,128]{2,0,1:T(8,128)(2,1)} fusion(bf16[144,64,128]{2,0,1:T(8,128)(2,1)} %get-tuple-element.134, bf16[144,64,128]{2,0,1:T(8,128)(2,1)} %get-tuple-element.133, bf16[16,64,128]{2,0,1:T(8,128)(2,1)S(1)} %fusion.78, bf16[144,16]{0,1:T(8,128)(2,1)S(1)} %get-tuple-element.136), kind=kOutput, calls=%fused_computation.11.clone.1 | convolution fusion | flops 81526784 | bytes 5247488 | tf_op jit(solution)/shard_map/while/body/eval_jaxpr/cf,cpr->fpr/dot_general | solution.py:68
  57.4 4.6 %fusion.79 = bf16[16,64,128]{2,0,1:T(8,128)(2,1)} fusion(bf16[144,64,128]{2,0,1:T(8,128)(2,1)} %get-tuple-element.134, bf16[144,64,128]{2,0,1:T(8,128)(2,1)} %get-tuple-element.133, bf16[16,64,128]{2,0,1:T(8,128)(2,1)S(1)} %fusion.78, bf16[144,16]{0,1:T(8,128)(2,1)S(1)} %get-tuple-element.136), kind=kOutput, calls=%fused_computation.11.clone.1 | convolution fusion | flops 81526784 | bytes 5247488 | tf_op jit(solution)/shard_map/while/body/eval_jaxpr/cf,cpr->fpr/dot_general | solution.py:68
  64.8 4.6 %fusion.79 = bf16[16,64,128]{2,0,1:T(8,128)(2,1)} fusion(bf16[144,64,128]{2,0,1:T(8,128)(2,1)} %get-tuple-element.134, bf16[144,64,128]{2,0,1:T(8,128)(2,1)} %get-tuple-element.133, bf16[16,64,128]{2,0,1:T(8,128)(2,1)S(1)} %fusion.78, bf16[144,16]{0,1:T(8,128)(2,1)S(1)} %get-tuple-element.136), kind=kOutput, calls=%fused_computation.11.clone.1 | convolution fusion | flops 81526784 | bytes 5247488 | tf_op jit(solution)/shard_map/while/body/eval_jaxpr/cf,cpr->fpr/dot_general | solution.py:68
  72.2 4.6 %fusion.79 = bf16[16,64,128]{2,0,1:T(8,128)(2,1)} fusion(bf16[144,64,128]{2,0,1:T(8,128)(2,1)} %get-tuple-element.134, bf16[144,64,128]{2,0,1:T(8,128)(2,1)} %get-tuple-element.133, bf16[16,64,128]{2,0,1:T(8,128)(2,1)S(1)} %fusion.78, bf16[144,16]{0,1:T(8,128)(2,1)S(1)} %get-tuple-element.136), kind=kOutput, calls=%fused_computation.11.clone.1 | convolution fusion | flops 81526784 | bytes 5247488 | tf_op jit(solution)/shard_map/while/body/eval_jaxpr/cf,cpr->fpr/dot_general | solution.py:68
  79.6 4.6 %fusion.79 = bf16[16,64,128]{2,0,1:T(8,128)(2,1)} fusion(bf16[144,64,128]{2,0,1:T(8,128)(2,1)} %get-tuple-element.134, bf16[144,64,128]{2,0,1:T(8,128)(2,1)} %get-tuple-element.133, bf16[16,64,128]{2,0,1:T(8,128)(2,1)S(1)} %fusion.78, bf16[144,16]{0,1:T(8,128)(2,1)S(1)} %get-tuple-element.136), kind=kOutput, calls=%fused_computation.11.clone.1 | convolution fusion | flops 81526784 | bytes 5247488 | tf_op jit(solution)/shard_map/while/body/eval_jaxpr/cf,cpr->fpr/dot_general | solution.py:68
  87.0 4.6 %fusion.79 = bf16[16,64,128]{2,0,1:T(8,128)(2,1)} fusion(bf16[144,64,128]{2,0,1:T(8,128)(2,1)} %get-tuple-element.134, bf16[144,64,128]{2,0,1:T(8,128)(2,1)} %get-tuple-element.133, bf16[16,64,128]{2,0,1:T(8,128)(2,1)S(1)} %fusion.78, bf16[144,16]{0,1:T(8,128)(2,1)S(1)} %get-tuple-element.136), kind=kOutput, calls=%fused_computation.11.clone.1 | convolution fusion | flops 81526784 | bytes 5247488 | tf_op jit(solution)/shard_map/while/body/eval_jaxpr/cf,cpr->fpr/dot_general | solution.py:68
  94.4 4.6 %fusion.79 = bf16[16,64,128]{2,0,1:T(8,128)(2,1)} fusion(bf16[144,64,128]{2,0,1:T(8,128)(2,1)} %get-tuple-element.134, bf16[144,64,128]{2,0,1:T(8,128)(2,1)} %get-tuple-element.133, bf16[16,64,128]{2,0,1:T(8,128)(2,1)S(1)} %fusion.78, bf16[144,16]{0,1:T(8,128)(2,1)S(1)} %get-tuple-element.136), kind=kOutput, calls=%fused_computation.11.clone.1 | convolution fusion | flops 81526784 | bytes 5247488 | tf_op jit(solution)/shard_map/while/body/eval_jaxpr/cf,cpr->fpr/dot_general | solution.py:68
  101.8 4.6 %fusion.79 = bf16[16,64,128]{2,0,1:T(8,128)(2,1)} fusion(bf16[144,64,128]{2,0,1:T(8,128)(2,1)} %get-tuple-element.134, bf16[144,64,128]{2,0,1:T(8,128)(2,1)} %get-tuple-element.133, bf16[16,64,128]{2,0,1:T(8,128)(2,1)S(1)} %fusion.78, bf16[144,16]{0,1:T(8,128)(2,1)S(1)} %get-tuple-element.136), kind=kOutput, calls=%fused_computation.11.clone.1 | convolution fusion | flops 81526784 | bytes 5247488 | tf_op jit(solution)/shard_map/while/body/eval_jaxpr/cf,cpr->fpr/dot_general | solution.py:68
  109.2 4.6 %fusion.79 = bf16[16,64,128]{2,0,1:T(8,128)(2,1)} fusion(bf16[144,64,128]{2,0,1:T(8,128)(2,1)} %get-tuple-element.134, bf16[144,64,128]{2,0,1:T(8,128)(2,1)} %get-tuple-element.133, bf16[16,64,128]{2,0,1:T(8,128)(2,1)S(1)} %fusion.78, bf16[144,16]{0,1:T(8,128)(2,1)S(1)} %get-tuple-element.136), kind=kOutput, calls=%fused_computation.11.clone.1 | convolution fusion | flops 81526784 | bytes 5247488 | tf_op jit(solution)/shard_map/while/body/eval_jaxpr/cf,cpr->fpr/dot_general | solution.py:68
  116.8 6.8 %all-to-all-start = ((f32[16,8,512]{2,0,1:T(8,128)}), f32[16,8,512]{2,0,1:T(8,128)S(1)}, u32[]{:S(2)}, u32[]{:S(2)}) async-start(f32[16,8,512]{2,0,1:T(8,128)} %copy.36), calls=%async_computation | async-start | bytes 524288 | tf_op jit(solution)/shard_map/all_to_all | solution.py:120
  125.1 5.5 %all-to-all-done = f32[16,8,512]{2,0,1:T(8,128)S(1)} async-done(((f32[16,8,512]{2,0,1:T(8,128)}), f32[16,8,512]{2,0,1:T(8,128)S(1)}, u32[]{:S(2)}, u32[]{:S(2)}) %all-to-all-start) | async-done | bytes 262176 | tf_op jit(solution)/shard_map/all_to_all | solution.py:120
  130.5 3.4 %all-to-all-start.1 = ((f32[16,8,512]{2,0,1:T(8,128)}), f32[16,8,512]{2,0,1:T(8,128)S(1)}, u32[]{:S(2)}, u32[]{:S(2)}) async-start(f32[16,8,512]{2,0,1:T(8,128)} %copy.38), calls=%async_computation.1 | async-start | bytes 524288 | tf_op jit(solution)/shard_map/all_to_all | solution.py:121
  134.8 6.0 %all-to-all-done.1 = f32[16,8,512]{2,0,1:T(8,128)S(1)} async-done(((f32[16,8,512]{2,0,1:T(8,128)}), f32[16,8,512]{2,0,1:T(8,128)S(1)}, u32[]{:S(2)}, u32[]{:S(2)}) %all-to-all-start.1) | async-done | bytes 262176 | tf_op jit(solution)/shard_map/all_to_all | solution.py:121
  140.9 12.0 %all-reduce.2 = (f32[512]{0:T(512)S(1)}, f32[512]{0:T(512)S(1)}) all-reduce(f32[512]{0:T(512)S(1)} %get-tuple-element.41, f32[512]{0:T(512)S(1)} %get-tuple-element.40), channel_id=1, replica_groups=mesh['ccd'=4,'patch'=8] {'ccd'}, use_global_device_ids=true, to_apply=%region_7.8 | all-reduce | flops 1024 | bytes 8192 | tf_op jit(solution)/shard_map/psum | solution.py:128
  (73 shorter events, 47.6 us)
Async XLA Ops:
  0.6 1.5 copy-start.5
  0.6 6.7 %copy-start.7 = (bf16[1,16,16]{2,1,0:T(8,128)(2,1)S(1)}, bf16[1,16,16]{2,1,0:T(8,128)(2,1)}, u32[]{:S(2)}) copy-start(bf16[1,16,16]{2,1,0:T(8,128)(2,1)} %param.13) | copy-start | bytes 1540
  0.7 6.7 %copy-start = (bf16[1,1,64,128,128]{4,3,2,1,0:T(8,128)(2,1)S(1)}, bf16[1,1,64,128,128]{4,3,2,1,0:T(8,128)(2,1)}, u32[]{:S(2)}) copy-start(bf16[1,1,64,128,128]{4,3,2,1,0:T(8,128)(2,1)} %param.12) | copy-start | bytes 6291460
  2.2 5.8 %copy-start.6 = (s32[1,16,16]{2,1,0:T(8,128)S(1)}, s32[1,16,16]{2,1,0:T(8,128)}, u32[]{:S(2)}) copy-start(s32[1,16,16]{2,1,0:T(8,128)} %param.14) | copy-start | bytes 3076
  2.3 1.3 copy-start.3
  3.6 4.6 %collective-permute-start = (bf16[2,8,4096]{2,1,0:T(8,128)(2,1)S(1)}, bf16[2,8,4096]{2,1,0:T(8,128)(2,1)S(1)}, u32[]{:S(2)}, u32[]{:S(2)}) collective-permute-start(bf16[2,8,4096]{2,1,0:T(8,128)(2,1)S(1)} %get-tuple-element.66), channel_id=1, source_target_pairs={{0,1},{1,2},{2,3},{3,4},{4,5},{5,6},{6,7},{8,9},{9,10},{10,11},{11... | collective-permute-start | bytes 393224 | tf_op jit(solution)/shard_map/ppermute | solution.py:23
  6.0 5.3 %collective-permute-start.1 = (bf16[2,8,4096]{2,1,0:T(8,128)(2,1)S(1)}, bf16[2,8,4096]{2,1,0:T(8,128)(2,1)S(1)}, u32[]{:S(2)}, u32[]{:S(2)}) collective-permute-start(bf16[2,8,4096]{2,1,0:T(8,128)(2,1)S(1)} %get-tuple-element.67), channel_id=1, source_target_pairs={{1,0},{2,1},{3,2},{4,3},{5,4},{6,5},{7,6},{9,8},{10,9},{11,10},{12... | collective-permute-start | bytes 393224 | tf_op jit(solution)/shard_map/ppermute | solution.py:25
  24.3 2.9 %copy-start.4 = (bf16[144,4096]{1,0:T(8,128)(2,1)S(1)}, bf16[144,4096]{1,0:T(8,128)(2,1)}, u32[]{:S(2)}) copy-start(bf16[144,4096]{1,0:T(8,128)(2,1)} %get-tuple-element.64) | copy-start | bytes 3538948
  35.9 1.7 %copy-start.1 = (bf16[144,64,64]{2,0,1:T(8,128)(2,1)S(1)}, bf16[144,64,64]{2,0,1:T(8,128)(2,1)}, u32[]{:S(2)}) copy-start(bf16[144,64,64]{2,0,1:T(8,128)(2,1)} %copy.39) | copy-start | bytes 3538948
  35.9 2.4 %copy-start.2 = (bf16[144,64,64]{2,0,1:T(8,128)(2,1)S(1)}, bf16[144,64,64]{2,0,1:T(8,128)(2,1)}, u32[]{:S(2)}) copy-start(bf16[144,64,64]{2,0,1:T(8,128)(2,1)} %copy.40) | copy-start | bytes 3538948
  115.4 8.2 %copy-start.8 = (s32[1,16]{1,0:T(1,128)S(1)}, s32[1,16]{1,0:T(1,128)}, u32[]{:S(2)}) copy-start(s32[1,16]{1,0:T(1,128)} %param.16) | copy-start | bytes 196
  115.4 8.3 %copy-start.9 = (s32[1,128]{1,0:T(1,128)S(1)}, s32[1,128]{1,0:T(1,128)}, u32[]{:S(2)}) copy-start(s32[1,128]{1,0:T(1,128)} %param.17) | copy-start | bytes 1540
  116.8 13.7 %all-to-all-start = ((f32[16,8,512]{2,0,1:T(8,128)}), f32[16,8,512]{2,0,1:T(8,128)S(1)}, u32[]{:S(2)}, u32[]{:S(2)}) async-start(f32[16,8,512]{2,0,1:T(8,128)} %copy.36), calls=%async_computation | async-start | bytes 524288 | tf_op jit(solution)/shard_map/all_to_all | solution.py:120
  130.5 10.3 %all-to-all-start.1 = ((f32[16,8,512]{2,0,1:T(8,128)}), f32[16,8,512]{2,0,1:T(8,128)S(1)}, u32[]{:S(2)}, u32[]{:S(2)}) async-start(f32[16,8,512]{2,0,1:T(8,128)} %copy.38), calls=%async_computation.1 | async-start | bytes 524288 | tf_op jit(solution)/shard_map/all_to_all | solution.py:121
where the time goes:
time: 155 us; the launch traced here: 154 us
  matrix products  72.9 us (47%)
  local copies, waits for them, and re-layouts  30.8 us (20%)
  waiting for transfers between devices  14.6 us (9%)
  starting transfers between devices  13.9 us (9%)
  blocking collectives  12 us (8%)
  other arithmetic  8.36 us (5%)
    dot_general x9, matrix products, relax(): jnp.einsum('cf,cpr->fpr', profile, residual, preferred_element_type=jnp.f...  41.4 us
    dot_general x10, matrix products, relax(): jnp.einsum('fpr,prl->fpl', folded, wave_rows, preferred_element_type=jnp....  18 us
    unnamed x25, local copies, waits for them, and re-layouts  12.6 us
    psum x1, blocking collectives, per_device(): sky_total, weight_total = lax.psum((sky_terms, weight_terms), 'ccd')  12 us
    dot_general x9, matrix products, sweep_step(): jnp.einsum('fpl,prl->fpr', fluxes.astype(jnp.bfloat16), wave_rows, prefer...  10.6 us
    slice x2, local copies, waits for them, and re-layouts, make_windows(): return jnp.concatenate([pieces[:, :-1], pieces[:, 1:]], axis=2)  7.54 us
    all_to_all x1, starting transfers between devices, per_device(): lax.all_to_all(extracted, 'patch', split_axis=1, concat_axis=0, tiled=True)  6.81 us
    all_to_all x1, waiting for transfers between devices, per_device(): lax.all_to_all(extracted_weight, 'patch', split_axis=1, concat_axis=0, ti...  6.02 us
  transfers between devices with their start and end apart: 4, of which 3 were waited for; matrix products, arithmetic and copies ran while one was open for 2% of the time, Pallas kernels for 0%

commit v1 on v0

v1 whole, which is shorter than its diff:
```python
import functools
import jax, jax.numpy as jnp
from jax import lax
from jax.sharding import PartitionSpec as P
from jax.experimental import pallas as pl
from jax.experimental.pallas import tpu as pltpu

LW=64; ITERS=10; HALO=8; RIDGE=0.1; PRIOR=1.0
F32=jnp.float32; BF=jnp.bfloat16
NT=(((1,),(1,)),((),()))

def mm(a,b): return jnp.dot(a,b,preferred_element_type=F32)
def mmt(a,b): return lax.dot_general(a,b,NT,preferred_element_type=F32)

def kernel(group, pc, pw, halo, wave, cols, cross, pick, out, wpad, cpad, qt, A, B0, inv, flux, rw, wt):
    g=pl.program_id(0)
    columns=pc.shape[0]; wavec=pc.shape[1]; rows=columns+2*HALO
    nf=cols.shape[0]
    @pl.when(g==0)
    def _():
        for pad,src,i in ((cpad,pc,0),(wpad,pw,1)):
            z=jnp.zeros((rows,128),BF)
            pad[:,:128]=z
            pad[:,wavec+128:]=z
            pad[:columns,128:wavec+128]=src[...]
            pad[columns:,128:wavec+128]=halo[i]
        j=lax.broadcasted_iota(jnp.int32,(nf,rows),1)
        col=jnp.where(j<columns,j,jnp.where(j<columns+HALO,j-columns-HALO,j-HALO))
        pt=jnp.zeros((nf,rows),F32)
        for k in range(cols.shape[1]):
            pt=pt+jnp.where(cols[:,k:k+1]==col,cross[:,k:k+1].astype(F32),0.0)
        pt=pt.astype(BF).astype(F32)
        tot=jnp.sum(pt,axis=0,keepdims=True)
        for f in range(nf):
            q=pt*pt[f:f+1,:]
            hi=q.astype(BF)
            qt[f*nf:(f+1)*nf,:]=hi
            qt[(nf+f)*nf:(nf+f+1)*nf,:]=(q-hi.astype(F32)).astype(BF)
        n2=2*nf*nf
        qt[n2:n2+nf,:]=(pt*tot).astype(BF)
        qt[n2+nf:n2+2*nf,:]=pt.astype(BF)
    n1=nf*nf; n2=2*nf*nf
    z=jnp.zeros((nf,128),BF)
    def pairmm(a,b,m):
        a=a.astype(BF); b=b.astype(BF)
        l=jnp.concatenate([jnp.concatenate([a,z],axis=1),jnp.concatenate([z,b],axis=1)],axis=0)
        r=mm(l,m)
        return r[:nf],r[nf:]
    def two(ref,k):
        return ref[2*k:2*k+2].reshape(256,128) if isinstance(k,int) else ref[pl.ds(2*k,2)].reshape(256,128)
    def build(k,_):
        base=pl.multiple_of(g*(group*LW)+k*128,128)
        w3=wpad[:,pl.ds(base,384)].astype(F32)
        c3=cpad[:,pl.ds(base,384)].astype(F32)
        def win(v):
            return jnp.concatenate([v[:,96:224],v[:,160:288]],axis=1)
        w=win(w3)
        wc=w*win(c3)
        wb=w.astype(BF)
        hi=wc.astype(BF)
        lo=(wc-hi.astype(F32)).astype(BF)
        a=mm(qt[:n2+nf,:],wb)
        aa=a[:n1]+a[n1:n2]
        mixed=a[n2:].astype(BF).astype(F32)
        ptb=qt[n2+nf:,:]
        b=mm(ptb,hi)+mm(ptb,lo)
        mr=[]
        for h in range(2):
            p=2*k+h
            t=wave[p].T
            wt[p]=t
            rt=jnp.sum(t.astype(F32),axis=0,keepdims=True)
            mr.append(mixed[:,128*h:128*h+128]*rt)
            A[p]=aa[:,128*h:128*h+128]
            B0[p]=b[:,128*h:128*h+128]
        wv=two(wave,k)
        r=pairmm(*mr,wv)
        fl=pairmm(b[:,:128],b[:,128:],wv)
        for h in range(2):
            p=2*k+h
            rh=r[h]+RIDGE
            rw[p]=rh
            iv=1.0/rh
            inv[p]=iv
            flux[p]=fl[h]*iv
        return 0
    lax.fori_loop(0,group//2,build,0)
    def sweep(it,_):
        for k in range(group//2):
            fl=[flux[2*k],flux[2*k+1]]
            bl=pairmm(*fl,two(wt,k))
            fo=[]
            for h in range(2):
                p=2*k+h
                acc=B0[p]
                for f in range(nf):
                    acc=acc-A[p,f*nf:(f+1)*nf,:]*bl[h][f:f+1,:]
                fo.append(acc)
            gr=pairmm(*fo,two(wave,k))
            for h in range(2):
                p=2*k+h
                flux[p]=fl[h]+(gr[h]-RIDGE*fl[h])*inv[p]
        return 0
    lax.fori_loop(1,ITERS,sweep,0)
    m=LW//2
    s1=pick[:,0:1]; s2=pick[:,1:2]
    for k in range(group//2):
        fl=jnp.concatenate([flux[2*k,:,m:m+LW],flux[2*k+1,:,m:m+LW]],axis=1)
        rr=jnp.concatenate([rw[2*k,:,m:m+LW],rw[2*k+1,:,m:m+LW]],axis=1)
        sky=jnp.sum(s1*rr*fl,axis=0,keepdims=True)
        wt=jnp.sum(s2*rr,axis=0,keepdims=True)
        per=out.shape[2]//128
        at=slice(128*(k%per),128*(k%per)+128)
        out[k//per,:nf,at]=fl
        out[k//per,nf:,at]=jnp.concatenate([sky,wt,jnp.zeros((6,128),F32)],axis=0)

def extract(pc,pw,halo,wave,cols,cross,pick,parts):
    columns,wavec=pc.shape
    nf=cols.shape[0]; np_=wave.shape[0]; win=wave.shape[1]; group=np_
    rows=columns+2*HALO
    full=lambda shape: pl.BlockSpec(shape,lambda g:(0,)*len(shape))
    shape=(parts,nf+8,wavec//parts)
    return pl.pallas_call(
        functools.partial(kernel,group),
        grid=(1,),
        in_specs=[full(a.shape) for a in (pc,pw,halo,wave,cols,cross,pick)],
        out_specs=full(shape),
        out_shape=jax.ShapeDtypeStruct(shape,F32),
        scratch_shapes=[pltpu.VMEM((rows,wavec+256),BF),pltpu.VMEM((rows,wavec+256),BF),pltpu.VMEM((2*nf*nf+2*nf,rows),BF),
            pltpu.VMEM((group,nf*nf,win),F32)]+[pltpu.VMEM((group,nf,win),F32)]*4+[pltpu.VMEM((group,win,win),BF)],
        compiler_params=pltpu.CompilerParams(vmem_limit_bytes=48*2**20),
    )(pc,pw,halo,wave,cols,cross,pick)


def tree(terms):
    return terms[0] if len(terms)==1 else tree(terms[0::2])+tree(terms[1::2])


def per_device(pixel_counts,pixel_weights,wave_profile,cross_profile,trace_columns,throughput,sky_fibres,fibre_mask):
    columns=pixel_counts.shape[1]; wavec=pixel_counts.shape[2]; nf=trace_columns.shape[1]
    n=lax.axis_size("patch"); nc=lax.axis_size("ccd")
    me=lax.axis_index("patch")
    head=jnp.stack([pixel_counts[0,:HALO],pixel_weights[0,:HALO]])
    tail=jnp.stack([pixel_counts[0,columns-HALO:],pixel_weights[0,columns-HALO:]])
    lo=lax.ppermute(tail,"patch",[(i,i+1) for i in range(n-1)])
    hi=lax.ppermute(head,"patch",[(i+1,i) for i in range(n-1)])
    halo=jnp.concatenate([lo,hi],axis=1)
    gain=throughput[0]
    mask=fibre_mask[0].astype(F32)
    fibres=me*nf+jnp.arange(nf,dtype=jnp.int32)
    sky=jnp.any(sky_fibres[0][None,:]==fibres[:,None],axis=1)
    own=jnp.where(sky,lax.dynamic_slice(mask,(me*nf,),(nf,)),0.0)
    pick=jnp.stack([own*gain,own*(gain*gain)],axis=1)
    out=extract(pixel_counts[0],pixel_weights[0],halo,wave_profile[0,0],trace_columns[0]-me*columns,cross_profile[0],pick,n)
    got=lax.all_to_all(out,"patch",split_axis=0,concat_axis=0,tiled=True)
    part=jnp.sum(got[:,nf:nf+2],axis=0)
    total=tree([part]+[lax.ppermute(part,"ccd",[(i,(i+s)%nc) for i in range(nc)]) for s in range(1,nc)])
    model=total[0]/(PRIOR+total[1])
    flux=got[:,:nf].reshape(n*nf,wavec//n)
    calibrated=mask[:,None]*(flux-gain*model[None,:])
    return calibrated[None],model


def solution(mesh):
    return jax.shard_map(per_device,mesh=mesh,
        in_specs=(P("ccd","patch",None),P("ccd","patch",None),P("ccd","patch",None,None,None),P("ccd","patch",None),P("ccd","patch",None),P("ccd"),P("ccd",None),P("ccd",None)),
        out_specs=(P("ccd",None,"patch"),P("patch")),check_vma=False)
```

time: 155 us -> 62.5 us (0.40)
  matrix products: 72.9 us -> 0 us
  local copies, waits for them, and re-layouts: 30.8 us -> 4.65 us
  Pallas kernels: 0 us -> 24 us
  waiting for transfers between devices: 14.6 us -> 4.38 us
  starting transfers between devices: 13.9 us -> 9 us
  other arithmetic: 8.36 us -> 3.75 us
  blocking collectives: 12 us -> 15 us
    dot_general x29 -> x0, matrix products: 72.9 us -> none  [the longest x9 41.4 us: relax(): jnp.einsum('cf,cpr->fpr', profile, residual, preferred_element_type=jnp.f...]
    pallas_call x0 -> x1, Pallas kernels: none -> 24 us  [extract(): pl.pallas_call(functools.partial(kernel, group), grid=(1,), in_specs=[ful...]
    all_to_all x0 -> x1, blocking collectives: none -> 15 us  [per_device(): got = lax.all_to_all(out, 'patch', split_axis=0, concat_axis=0, tiled=True)]
    psum x1 -> x0, blocking collectives: 12 us -> none  [per_device(): sky_total, weight_total = lax.psum((sky_terms, weight_terms), 'ccd')]
    all_to_all x2 -> x0, waiting for transfers between devices: 11.5 us -> none  [the longest x1 6.02 us: per_device(): lax.all_to_all(extracted_weight, 'patch', split_axis=1, concat_axis=0, ti...]
    all_to_all x2 -> x0, starting transfers between devices: 10.2 us -> none  [the longest x1 6.81 us: per_device(): lax.all_to_all(extracted, 'patch', split_axis=1, concat_axis=0, tiled=True)]
    unnamed x25 -> x8, local copies, waits for them, and re-layouts: 12.6 us -> 3.5 us
    slice x7 -> x2, local copies, waits for them, and re-layouts: 8.3 us -> 1.06 us  [the longest x1 1.04 us: per_device(): pixel_counts[0, columns - HALO:]]
  transfers between devices with their start and end apart: 4 -> 5, of which waited for: 3 -> 2; matrix products, arithmetic and copies ran while one was open for 2% -> 4% of each run, Pallas kernels for 0% -> 0%
where the time goes in v1:
time: 62.5 us; the launch traced here: 62.1 us
  Pallas kernels  24 us (38%)
  blocking collectives  15 us (24%)
  starting transfers between devices  9 us (14%)
  local copies, waits for them, and re-layouts  4.65 us (7%)
  waiting for transfers between devices  4.38 us (7%)
  other arithmetic  3.75 us (6%)
  between operations  1.37 us (2%)
    pallas_call x1, Pallas kernels, extract(): pl.pallas_call(functools.partial(kernel, group), grid=(1,), in_specs=[ful...  24 us
    all_to_all x1, blocking collectives, per_device(): got = lax.all_to_all(out, 'patch', split_axis=0, concat_axis=0, tiled=True)  15 us
    ppermute x3, starting transfers between devices, per_device(): lax.ppermute(part, 'ccd', [(i, (i + s) % nc) for i in range(nc)])  4.67 us
    ppermute x3, waiting for transfers between devices, per_device(): lax.ppermute(part, 'ccd', [(i, (i + s) % nc) for i in range(nc)])  4.37 us
    unnamed x8, local copies, waits for them, and re-layouts  3.5 us
    ppermute x1, starting transfers between devices, per_device(): lo = lax.ppermute(tail, 'patch', [(i, i + 1) for i in range(n - 1)])  3.04 us
    mul x2, other arithmetic, per_device(): calibrated = mask[:, None] * (flux - gain * model[None, :])  1.38 us
    ppermute x1, starting transfers between devices, per_device(): hi = lax.ppermute(head, 'patch', [(i + 1, i) for i in range(n - 1)])  1.29 us
  transfers between devices with their start and end apart: 5, of which 2 were waited for; matrix products, arithmetic and copies ran while one was open for 4% of the time, Pallas kernels for 0%

profile of v1, /device:TPU:0, one launch (start us, length us, event | category | flops | bytes accessed | tf_op | source)
XLA Modules:
  0.0 62.1 jit_solution(6875892976401440060)
XLA Ops:
  0.6 1.0 %fusion.3 = (bf16[1,8,4096]{2,1,0:T(8,128)(2,1)S(1)}, bf16[1,8,4096]{2,1,0:T(8,128)(2,1)S(1)}, bf16[1,8,4096]{2,1,0:T(8,128)(2,1)S(1)}, bf16[1,8,4096]{2,1,0:T(8,128)(2,1)S(1)}) fusion(bf16[1,128,4096]{2,1,0:T(8,128)(2,1)} %param.8, bf16[1,128,4096]{2,1,0:T(8,128)(2,1)} %param.9), kind=kLoop, calls=%fused_computation.18 | loop fusion | bytes 524288 | tf_op jit(solution)/shard_map/slice | solution.py:144
  1.7 1.3 %collective-permute-start.1 = (bf16[2,8,4096]{2,1,0:T(8,128)(2,1)S(1)}, bf16[2,8,4096]{2,1,0:T(8,128)(2,1)S(1)}, u32[]{:S(2)}, u32[]{:S(2)}) collective-permute-start(bf16[2,8,4096]{2,1,0:T(8,128)(2,1)S(1)} %pad_maximum_fusion.2), channel_id=1, source_target_pairs={{1,0},{2,1},{3,2},{4,3},{5,4},{6,5},{7,6},{9,8},{10,9},{11,10},{12... | collective-permute-start | bytes 393224 | tf_op jit(solution)/shard_map/ppermute | solution.py:146
  3.0 3.0 %collective-permute-start = (bf16[2,8,4096]{2,1,0:T(8,128)(2,1)S(1)}, bf16[2,8,4096]{2,1,0:T(8,128)(2,1)S(1)}, u32[]{:S(2)}, u32[]{:S(2)}) collective-permute-start(bf16[2,8,4096]{2,1,0:T(8,128)(2,1)S(1)} %pad_maximum_fusion.1), channel_id=1, source_target_pairs={{0,1},{1,2},{2,3},{3,4},{4,5},{5,6},{6,7},{8,9},{9,10},{10,11},{11... | collective-permute-start | bytes 393224 | tf_op jit(solution)/shard_map/ppermute | solution.py:145
  6.7 0.7 %convert_bitcast_fusion = (f32[128]{0:T(128)S(1)}, f32[1,128]{1,0:T(1,128)S(1)}) fusion(s32[1,128]{1,0:T(1,128)} %param.15), kind=kLoop, calls=%fused_computation.17 | loop fusion | flops 128 | bytes 1536 | tf_op jit(solution)/shard_map/convert_element_type | solution.py:149
  7.4 0.8 %compare_reduce_fusion = pred[16]{0:T(512)(128)(4,1)S(1)} fusion(s32[16]{0:T(128)} %bitcast.38, s32[16]{0:T(128)S(1)} %iota_add_fusion), kind=kLoop, calls=%fused_computation.7 | loop fusion | flops 496 | bytes 144 | tf_op jit(solution)/shard_map/reduce_or | solution.py:151
  8.2 0.1 multiply_bitcast_fusion.1
  8.3 0.1 copy.13.pick
  8.4 0.7 %subtract_bitcast_fusion.cols = s32[16,16]{1,0:T(8,128)S(1)} fusion(s32[1,16,16]{2,1,0:T(8,128)} %param.12, s32[]{:T(128)S(6)} %mul.46), kind=kLoop, calls=%fused_computation.6 | loop fusion | flops 256 | bytes 2052 | tf_op jit(solution)/shard_map/sub | solution.py:154
  9.1 0.0 collective-permute-done.1
  9.1 0.0 collective-permute-done
  9.2 0.0 copy-start
  9.2 1.6 %copy-done = bf16[1,1,64,128,128]{4,3,2,1,0:T(8,128)(2,1)S(1)} copy-done((bf16[1,1,64,128,128]{4,3,2,1,0:T(8,128)(2,1)S(1)}, bf16[1,1,64,128,128]{4,3,2,1,0:T(8,128)(2,1)}, u32[]{:S(2)}) %copy-start) | copy-done | bytes 2097176
  10.8 1.2 %copy-done.2 = bf16[1,128,4096]{2,1,0:T(8,128)(2,1)S(1)} copy-done((bf16[1,128,4096]{2,1,0:T(8,128)(2,1)S(1)}, bf16[1,128,4096]{2,1,0:T(8,128)(2,1)}, u32[]{:S(2)}) %copy-start.2) | copy-done | bytes 1048600
  12.0 0.7 %copy-done.3 = bf16[1,16,16]{2,1,0:T(8,128)(2,1)S(1)} copy-done((bf16[1,16,16]{2,1,0:T(8,128)(2,1)S(1)}, bf16[1,16,16]{2,1,0:T(8,128)(2,1)}, u32[]{:S(2)}) %copy-start.3) | copy-done | bytes 536
  12.7 24.0 %shard_map.95 = f32[8,24,512]{2,1,0:T(8,128)S(1)} custom-call(bf16[128,4096]{1,0:T(8,128)(2,1)S(1)} %bitcast.32, bf16[128,4096]{1,0:T(8,128)(2,1)S(1)} %bitcast.33, bf16[2,16,4096]{2,1,0:T(8,128)(2,1)S(1)} %pad_maximum_fusion.halo, bf16[64,128,128]{2,1,0:T(8,128)(2,1)S(1)} %bitcast.31, s32[16,16]{1,0:T(8,128)S(1)} %subtract_bitcast_fusion.cols, ...), custom_call_target="tpu_custom_call" | custom-call | tf_op jit(solution)/shard_map/pallas_call | solution.py:123
  36.7 15.0 %all_to_all.5 = f32[8,24,512]{2,1,0:T(8,128)S(1)} all-to-all(f32[8,24,512]{2,1,0:T(8,128)S(1)} %shard_map.95), channel_id=1, replica_groups=mesh['ccd'=4,'patch'=8] {'patch'}, dimensions={0} | all-to-all | bytes 786432 | tf_op jit(solution)/shard_map/all_to_all | solution.py:155
  51.7 3.7 %collective-permute-start.4 = (f32[2,512]{1,0:T(2,128)S(1)}, f32[2,512]{1,0:T(2,128)S(1)}, u32[]{:S(2)}, u32[]{:S(2)}) collective-permute-start(f32[2,512]{1,0:T(2,128)S(1)} %slice_reduce_fusion), channel_id=1, source_target_pairs={{0,24},{8,0},{16,8},{24,16},{1,25},{9,1},{17,9},{25,17},{2,26},{10... | collective-permute-start | bytes 12296 | tf_op jit(solution)/shard_map/ppermute | solution.py:157
  55.3 0.0 collective-permute-start.3
  55.3 1.0 %collective-permute-start.2 = (f32[2,512]{1,0:T(2,128)S(1)}, f32[2,512]{1,0:T(2,128)S(1)}, u32[]{:S(2)}, u32[]{:S(2)}) collective-permute-start(f32[2,512]{1,0:T(2,128)S(1)} %slice_reduce_fusion), channel_id=1, source_target_pairs={{0,16},{8,24},{16,0},{24,8},{1,17},{9,25},{17,1},{25,9},{2,18},{10... | collective-permute-start | bytes 12296 | tf_op jit(solution)/shard_map/ppermute | solution.py:157
  56.3 0.3 collective-permute-done.4
  56.6 4.1 %collective-permute-done.3 = f32[2,512]{1,0:T(2,128)S(1)} collective-permute-done((f32[2,512]{1,0:T(2,128)S(1)}, f32[2,512]{1,0:T(2,128)S(1)}, u32[]{:S(2)}, u32[]{:S(2)}) %collective-permute-start.3) | collective-permute-done | bytes 4128 | tf_op jit(solution)/shard_map/ppermute | solution.py:157
  60.7 0.0 collective-permute-done.2
  60.7 0.6 broadcast_multiply_fusion
  61.3 0.8 %fusion = f32[1,128,512]{2,1,0:T(8,128)} fusion(f32[512]{0:T(512)S(1)} %bitcast.36, f32[128]{0:T(128)S(1)} %get-tuple-element.10, f32[1,128,512]{2,1,0:T(8,128)S(1)} %bitcast.35), kind=kLoop, calls=%fused_computation.2 | loop fusion | flops 131072 | bytes 526848 | tf_op jit(solution)/shard_map/mul | solution.py:160
  (12 shorter events, 0.1 us)
Async XLA Ops:
  0.6 8.5 %copy-start.1 = (bf16[1,128,4096]{2,1,0:T(8,128)(2,1)S(1)}, bf16[1,128,4096]{2,1,0:T(8,128)(2,1)}, u32[]{:S(2)}) copy-start(bf16[1,128,4096]{2,1,0:T(8,128)(2,1)} %param.8) | copy-start | bytes 3145732
  1.7 7.4 %collective-permute-start.1 = (bf16[2,8,4096]{2,1,0:T(8,128)(2,1)S(1)}, bf16[2,8,4096]{2,1,0:T(8,128)(2,1)S(1)}, u32[]{:S(2)}, u32[]{:S(2)}) collective-permute-start(bf16[2,8,4096]{2,1,0:T(8,128)(2,1)S(1)} %pad_maximum_fusion.2), channel_id=1, source_target_pairs={{1,0},{2,1},{3,2},{4,3},{5,4},{6,5},{7,6},{9,8},{10,9},{11,10},{12... | collective-permute-start | bytes 393224 | tf_op jit(solution)/shard_map/ppermute | solution.py:146
  3.0 6.1 %collective-permute-start = (bf16[2,8,4096]{2,1,0:T(8,128)(2,1)S(1)}, bf16[2,8,4096]{2,1,0:T(8,128)(2,1)S(1)}, u32[]{:S(2)}, u32[]{:S(2)}) collective-permute-start(bf16[2,8,4096]{2,1,0:T(8,128)(2,1)S(1)} %pad_maximum_fusion.1), channel_id=1, source_target_pairs={{0,1},{1,2},{2,3},{3,4},{4,5},{5,6},{6,7},{8,9},{9,10},{10,11},{11... | collective-permute-start | bytes 393224 | tf_op jit(solution)/shard_map/ppermute | solution.py:145
  9.2 1.6 %copy-start = (bf16[1,1,64,128,128]{4,3,2,1,0:T(8,128)(2,1)S(1)}, bf16[1,1,64,128,128]{4,3,2,1,0:T(8,128)(2,1)}, u32[]{:S(2)}) copy-start(bf16[1,1,64,128,128]{4,3,2,1,0:T(8,128)(2,1)} %param.10) | copy-start | bytes 6291460
  10.8 1.2 %copy-start.2 = (bf16[1,128,4096]{2,1,0:T(8,128)(2,1)S(1)}, bf16[1,128,4096]{2,1,0:T(8,128)(2,1)}, u32[]{:S(2)}) copy-start(bf16[1,128,4096]{2,1,0:T(8,128)(2,1)} %param.9) | copy-start | bytes 3145732
  12.0 0.7 %copy-start.3 = (bf16[1,16,16]{2,1,0:T(8,128)(2,1)S(1)}, bf16[1,16,16]{2,1,0:T(8,128)(2,1)}, u32[]{:S(2)}) copy-start(bf16[1,16,16]{2,1,0:T(8,128)(2,1)} %param.11) | copy-start | bytes 1540
  51.7 5.0 %collective-permute-start.4 = (f32[2,512]{1,0:T(2,128)S(1)}, f32[2,512]{1,0:T(2,128)S(1)}, u32[]{:S(2)}, u32[]{:S(2)}) collective-permute-start(f32[2,512]{1,0:T(2,128)S(1)} %slice_reduce_fusion), channel_id=1, source_target_pairs={{0,24},{8,0},{16,8},{24,16},{1,25},{9,1},{17,9},{25,17},{2,26},{10... | collective-permute-start | bytes 12296 | tf_op jit(solution)/shard_map/ppermute | solution.py:157
  55.3 5.4 %collective-permute-start.3 = (f32[2,512]{1,0:T(2,128)S(1)}, f32[2,512]{1,0:T(2,128)S(1)}, u32[]{:S(2)}, u32[]{:S(2)}) collective-permute-start(f32[2,512]{1,0:T(2,128)S(1)} %slice_reduce_fusion), channel_id=1, source_target_pairs={{0,8},{8,16},{16,24},{24,0},{1,9},{9,17},{17,25},{25,1},{2,10},{10... | collective-permute-start | bytes 12296 | tf_op jit(solution)/shard_map/ppermute | solution.py:157
  55.3 5.4 %collective-permute-start.2 = (f32[2,512]{1,0:T(2,128)S(1)}, f32[2,512]{1,0:T(2,128)S(1)}, u32[]{:S(2)}, u32[]{:S(2)}) collective-permute-start(f32[2,512]{1,0:T(2,128)S(1)} %slice_reduce_fusion), channel_id=1, source_target_pairs={{0,16},{8,24},{16,0},{24,8},{1,17},{9,25},{17,1},{25,9},{2,18},{10... | collective-permute-start | bytes 12296 | tf_op jit(solution)/shard_map/ppermute | solution.py:157

commit v2 on v0

v2 whole, which is shorter than its diff:
```python
import functools
import jax
import jax.numpy as jnp
from jax import lax
from jax.sharding import PartitionSpec as P
from jax.experimental import pallas as pl
from jax.experimental.pallas import tpu as pltpu

LW = 64
ITERS = 10
HALO = 8
RIDGE = 0.1
PRIOR = 1.0
LANES = 128
EXTRA = 8
CHUNKS = 4
F32 = jnp.float32
BF16 = jnp.bfloat16


def mm(a, b):
    return jnp.dot(a, b, preferred_element_type=F32)


def pair_mm(a, b, stacked):
    a = a.astype(BF16)
    b = b.astype(BF16)
    zero = jnp.zeros_like(a)
    left = jnp.concatenate(
        [jnp.concatenate([a, zero], axis=1), jnp.concatenate([zero, b], axis=1)], axis=0
    )
    both = mm(left, stacked)
    return both[: a.shape[0]], both[a.shape[0] :]


def profile_rows(cols, cross, columns):
    fibres = cols.shape[0]
    lane = lax.broadcasted_iota(jnp.int32, (fibres, columns + 2 * HALO), 1)
    column = jnp.where(
        lane < columns, lane, jnp.where(lane < columns + HALO, lane - columns - HALO, lane - HALO)
    )
    total = jnp.zeros(column.shape, F32)
    for k in range(cols.shape[1]):
        total = total + jnp.where(cols[:, k : k + 1] == column, cross[:, k : k + 1].astype(F32), 0.0)
    return total.astype(BF16).astype(F32)


def split(values):
    top = values.astype(BF16)
    return top, (values - top.astype(F32)).astype(BF16)


def prepare_kernel(
    gain, counts, weights, wave, traces, cross, sky, mask,
    terms, first, mixed, turned, row_total, wave_out, side, side_sum, pick, mask_out, gain_out,
    cpad, wpad, main, main_sum, gain_v, traces_v, cross_v, sky_v, mask_v, small, pixel_sem, wave_sem,
):
    me = lax.axis_index("patch")
    columns, wave_count = counts.shape
    fibres = traces.shape[0]
    patches = wave.shape[0]
    square = fibres * fibres

    copies = [
        pltpu.make_async_copy(a, b, small.at[i])
        for i, (a, b) in enumerate(
            ((gain, gain_v), (traces, traces_v), (cross, cross_v), (sky, sky_v), (mask, mask_v))
        )
    ]
    step = wave_count // CHUNKS
    pixel_copies = []
    for c in range(CHUNKS):
        source = pl.ds(c * step, step)
        target = pl.ds(LANES + c * step, step)
        pixel_copies.append(
            [
                pltpu.make_async_copy(counts.at[:, source], cpad.at[:, target], pixel_sem.at[0, c]),
                pltpu.make_async_copy(weights.at[:, source], wpad.at[:, target], pixel_sem.at[1, c]),
            ]
        )
    wave_copy = pltpu.make_async_copy(wave, wave_out, wave_sem)
    for copy in copies:
        copy.start()
    for pair in pixel_copies:
        for copy in pair:
            copy.start()
    wave_copy.start()
    zero = jnp.zeros((columns, LANES), BF16)
    for pad in (cpad, wpad):
        pad[:, :LANES] = zero
        pad[:, LANES + wave_count :] = zero
    for copy in copies:
        copy.wait()

    profile = profile_rows(traces_v[...] - me * columns, cross_v[...], columns)
    spread = (profile * jnp.sum(profile, axis=0, keepdims=True)).astype(BF16)
    for f in range(fibres):
        at = slice(f * fibres, (f + 1) * fibres)
        top, low = split(profile * profile[f : f + 1, :])
        main[at, :] = jnp.concatenate([top[:, :columns], low[:, :columns]], axis=1)
        side[at, :] = jnp.concatenate([top[:, columns:], low[:, columns:]], axis=1)
    half = profile.astype(BF16)
    main[square:, :] = jnp.concatenate([spread[:, :columns], jnp.zeros((fibres, columns), BF16)], axis=1)
    side[square:, :] = jnp.concatenate([spread[:, columns:], jnp.zeros((fibres, 2 * HALO), BF16)], axis=1)
    main_sum[...] = jnp.concatenate([half[:, :columns]] * 2, axis=1)
    side_sum[...] = jnp.concatenate([half[:, columns:]] * 2, axis=1)

    number = me * fibres + lax.broadcasted_iota(jnp.int32, (fibres, sky_v.shape[1]), 0)
    is_sky = jnp.max(jnp.where(number == sky_v[...], 1.0, 0.0), axis=1, keepdims=True)
    count = mask_v.shape[1]
    for b in range(count // fibres):
        row = b * fibres + lax.broadcasted_iota(jnp.int32, (fibres, count), 0)
        lane = lax.broadcasted_iota(jnp.int32, (fibres, count), 1)
        column = jnp.sum(jnp.where(row == lane, mask_v[...].astype(F32), 0.0), axis=1, keepdims=True)
        mask_out[b * fibres : (b + 1) * fibres, :] = jnp.broadcast_to(column, (fibres, LANES))
    scale = gain_v[...]
    own = mask_out[pl.ds(pl.multiple_of(me * fibres, fibres), fibres), :]
    chosen = is_sky * own * scale
    pick[0] = chosen
    pick[1] = chosen * scale
    gain_out[...] = jnp.broadcast_to(scale, gain_out.shape)

    ready = 0
    for k in range(patches // 2):
        need = min(CHUNKS, ((k + 1) * LANES + LW // 2 - 1) // step + 1)
        while ready < need:
            for copy in pixel_copies[ready]:
                copy.wait()
            ready += 1
        start = LANES - LW // 2 + k * LANES

        def window(pad):
            return jnp.concatenate(
                [pad[:, start : start + LANES], pad[:, start + LW : start + LW + LANES]], axis=1
            )

        weight = window(wpad)
        top, low = split(weight.astype(F32) * window(cpad).astype(F32))
        both = mm(main[...], jnp.concatenate([weight, weight], axis=0))
        sums = mm(main_sum[...], jnp.concatenate([top, low], axis=0))
        for h in range(2):
            at = slice(h * LANES, (h + 1) * LANES)
            terms[2 * k + h] = both[:square, at]
            mixed[2 * k + h] = both[square:, at]
            first[2 * k + h] = sums[:, at]

    wave_copy.wait()
    for p in range(patches):
        flipped = wave_out[p].T
        turned[p] = flipped
        total = jnp.sum(flipped.astype(F32), axis=0, keepdims=True)
        row_total[p] = jnp.broadcast_to(total, row_total.shape[1:])


def prepare(gain, counts, weights, wave, traces, cross, sky, mask):
    columns, wave_count = counts.shape
    fibres = traces.shape[0]
    patches, window, _ = wave.shape
    square = fibres * fibres
    far = pl.BlockSpec(memory_space=pltpu.HBM)
    near = pl.BlockSpec(memory_space=pltpu.VMEM)
    shape = jax.ShapeDtypeStruct
    return pl.pallas_call(
        prepare_kernel,
        in_specs=[far] * 8,
        out_specs=[near] * 11,
        out_shape=[
            shape((patches, square, window), F32),
            shape((patches, fibres, window), F32),
            shape((patches, fibres, window), F32),
            shape(wave.shape, BF16),
            shape((patches, 8, window), F32),
            shape(wave.shape, BF16),
            shape((square + fibres, 4 * HALO), BF16),
            shape((fibres, 4 * HALO), BF16),
            shape((2, fibres, LANES), F32),
            shape((mask.shape[1], LANES), F32),
            shape((8, LANES), F32),
        ],
        scratch_shapes=[
            pltpu.VMEM((columns, wave_count + 2 * LANES), BF16),
            pltpu.VMEM((columns, wave_count + 2 * LANES), BF16),
            pltpu.VMEM((square + fibres, 2 * columns), BF16),
            pltpu.VMEM((fibres, 2 * columns), BF16),
            pltpu.VMEM(gain.shape, F32),
            pltpu.VMEM(traces.shape, jnp.int32),
            pltpu.VMEM(cross.shape, BF16),
            pltpu.VMEM(sky.shape, jnp.int32),
            pltpu.VMEM(mask.shape, jnp.int32),
            pltpu.SemaphoreType.DMA((5,)),
            pltpu.SemaphoreType.DMA((2, CHUNKS)),
            pltpu.SemaphoreType.DMA,
        ],
        compiler_params=pltpu.CompilerParams(vmem_limit_bytes=24 * 2**20),
        name="prepare",
    )(gain, counts, weights, wave, traces, cross, sky, mask)


def relax_kernel(
    groups, low, high, terms_own, first_own, mixed_own, turned, row_total, wave, side, side_sum, pick, *rest
):
    outs = rest[: len(groups)]
    wpad, cpad, terms, first, inverse, flux, row_weight = rest[len(groups) :]
    me = lax.axis_index("patch")
    wave_count = low.shape[1]
    square, fibres = terms.shape[1], first.shape[1]
    width = outs[0].shape[-1]
    tiles = width // LANES
    per = width // LW
    flat = [(o, i, s) for o, group in enumerate(groups) for i, s in enumerate(group)]
    owner = [me ^ s for _, _, s in flat]
    pairs = [(g, j) for g in range(len(flat)) for j in range(per // 2)]

    last = wave_count // LANES - 1
    for g in range(len(flat)):
        for t in range(tiles + 2):
            tile = owner[g] * tiles + (t - 1)
            lanes = pl.ds(pl.multiple_of(jnp.clip(tile, 0, last) * LANES, LANES), LANES)
            below = low[:, lanes].astype(F32)
            above = high[:, lanes].astype(F32)
            for i, pad in ((0, cpad), (1, wpad)):
                at = slice(i * HALO, (i + 1) * HALO)
                both = jnp.concatenate([below[at], above[at]], axis=0).astype(BF16)
                if t == 0 or t == tiles + 1:
                    inside = jnp.logical_and(tile >= 0, tile <= last)
                    both = jnp.where(inside, both, jnp.zeros_like(both))
                pad[g, :, t * LANES : (t + 1) * LANES] = both

    for q, (g, j) in enumerate(pairs):
        start = LANES - LW // 2 + j * LANES

        def window(pad):
            return jnp.concatenate(
                [pad[g, :, start : start + LANES], pad[g, :, start + LW : start + LW + LANES]], axis=1
            )

        weight = window(wpad)
        top, bottom = split(weight.astype(F32) * window(cpad).astype(F32))
        both = mm(side[...], jnp.concatenate([weight, weight], axis=0))
        sums = mm(side_sum[...], jnp.concatenate([top, bottom], axis=0))
        for h in range(2):
            p = owner[g] * per + 2 * j + h
            at = slice(h * LANES, (h + 1) * LANES)
            terms[2 * q + h] = terms_own[p] + both[:square, at]
            first[2 * q + h] = first_own[p] + sums[:, at]
            whole_sum = (mixed_own[p] + both[square:, at]).astype(BF16).astype(F32)
            flux[2 * q + h] = whole_sum * row_total[p, 0:1, :]

    def stacked(ref, g, j):
        return ref[pl.ds(owner[g] * per + 2 * j, 2)].reshape(2 * LANES, LANES)

    for q, (g, j) in enumerate(pairs):
        grid = stacked(wave, g, j)
        weight_pair = pair_mm(flux[2 * q], flux[2 * q + 1], grid)
        step_pair = pair_mm(first[2 * q], first[2 * q + 1], grid)
        for h in range(2):
            total = weight_pair[h] + RIDGE
            row_weight[2 * q + h] = total
            reciprocal = 1.0 / total
            inverse[2 * q + h] = reciprocal
            flux[2 * q + h] = step_pair[h] * reciprocal

    def sweep(_, carry):
        for q, (g, j) in enumerate(pairs):
            now = [flux[2 * q], flux[2 * q + 1]]
            blurred = pair_mm(*now, stacked(turned, g, j))
            folded = []
            for h in range(2):
                total = first[2 * q + h]
                for f in range(fibres):
                    term = terms[2 * q + h, f * fibres : (f + 1) * fibres, :]
                    total = total - term * blurred[h][f : f + 1, :]
                folded.append(total)
            gradient = pair_mm(*folded, stacked(wave, g, j))
            for h in range(2):
                flux[2 * q + h] = now[h] + (gradient[h] - RIDGE * now[h]) * inverse[2 * q + h]
        return carry

    lax.fori_loop(1, ITERS, sweep, 0)

    margin = LW // 2
    for q, (g, j) in enumerate(pairs):
        half = slice(j * LANES, (j + 1) * LANES)

        def kept(values):
            return jnp.concatenate(
                [values[2 * q, :, margin : margin + LW], values[2 * q + 1, :, margin : margin + LW]],
                axis=1,
            )

        spectrum = kept(flux)
        strength = kept(row_weight)
        o, i, _ = flat[g]
        outs[o][i, :fibres, half] = spectrum
        outs[o][i, fibres:, half] = jnp.concatenate(
            [
                jnp.sum(pick[0] * strength * spectrum, axis=0, keepdims=True),
                jnp.sum(pick[1] * strength, axis=0, keepdims=True),
                jnp.zeros((EXTRA - 2, LANES), F32),
            ],
            axis=0,
        )


def relax(groups, width, low, high, terms, first, *rest):
    square, window = terms.shape[1:]
    fibres = first.shape[1]
    number = sum(len(group) for group in groups)
    count = number * width // LW
    near = pl.BlockSpec(memory_space=pltpu.VMEM)
    return pl.pallas_call(
        functools.partial(relax_kernel, groups),
        in_specs=[near] * (4 + len(rest)),
        out_specs=[near] * len(groups),
        out_shape=[jax.ShapeDtypeStruct((len(group), fibres + EXTRA, width), F32) for group in groups],
        scratch_shapes=[pltpu.VMEM((number, 2 * HALO, width + 2 * LANES), BF16)] * 2
        + [pltpu.VMEM((count, square, window), F32)]
        + [pltpu.VMEM((count, fibres, window), F32)] * 4,
        compiler_params=pltpu.CompilerParams(vmem_limit_bytes=24 * 2**20),
        name="relax",
    )(low, high, terms, first, *rest)


def finish_kernel(fibres, gain, mask, own, swapped, totals, *rest):
    *across, calibrated, model = rest
    me = lax.axis_index("patch")
    width = model.shape[1]
    sky = totals[0:1, :] / (PRIOR + totals[1:2, :])
    model[...] = sky
    blocks = {0: own[0, :fibres, :], 1: swapped[0, :fibres, :]}
    for t, block in enumerate(across):
        blocks[2 * t + 2] = block[0, :fibres, :]
        blocks[2 * t + 3] = swapped[t + 1, :fibres, :]
    for s, block in blocks.items():
        at = pl.ds(pl.multiple_of((me ^ s) * fibres, fibres), fibres)
        calibrated[at, :] = mask[at, 0:1] * (block - gain[0:1, 0:1] * sky)


def finish(fibres, gain, mask, own, swapped, totals, across):
    width = totals.shape[1]
    near = pl.BlockSpec(memory_space=pltpu.VMEM)
    return pl.pallas_call(
        functools.partial(finish_kernel, fibres),
        in_specs=[near] * (5 + len(across)),
        out_specs=[near] * 2,
        out_shape=[
            jax.ShapeDtypeStruct((mask.shape[0], width), F32),
            jax.ShapeDtypeStruct((1, width), F32),
        ],
        name="finish",
    )(gain, mask, own, swapped, totals, *across)


def tree(terms):
    return terms[0] if len(terms) == 1 else tree(terms[0::2]) + tree(terms[1::2])


def swap(values, axis, shift):
    return lax.ppermute(values, axis, [(i, i ^ shift) for i in range(lax.axis_size(axis))])


def edges(counts, weights):
    columns = counts.shape[0]
    parts = lax.axis_size("patch")
    me = lax.axis_index("patch")
    odd = me % 2 == 1
    first = jnp.concatenate([counts[:HALO], weights[:HALO]], axis=0)
    final = jnp.concatenate([counts[columns - HALO :], weights[columns - HALO :]], axis=0)
    far = [(i, i + 1) for i in range(1, parts - 1, 2)]
    outer = lax.ppermute(jnp.where(odd, final, first), "patch", far + [(b, a) for a, b in far])
    inner = swap(jnp.where(odd, first, final), "patch", 1)
    return jnp.where(odd, inner, outer), jnp.where(odd, outer, inner)


def per_device(
    pixel_counts,
    pixel_weights,
    wave_profile,
    cross_profile,
    trace_columns,
    throughput,
    sky_fibres,
    fibre_mask,
):
    fibres = trace_columns.shape[1]
    parts = lax.axis_size("patch")
    cameras = lax.axis_size("ccd")
    width = pixel_counts.shape[2] // parts
    low, high = edges(pixel_counts[0], pixel_weights[0])
    *state, mask, gain = prepare(
        throughput[None, :],
        pixel_counts[0],
        pixel_weights[0],
        wave_profile[0, 0],
        trace_columns[0],
        cross_profile[0],
        sky_fibres,
        fibre_mask,
    )
    away = relax([(s, s + 1) for s in range(2, parts, 2)], width, low, high, *state)
    across = [swap(block, "patch", 2 * t + 2) for t, block in enumerate(away)]
    state[0], *away = lax.optimization_barrier((state[0], *away))
    own, mate = relax([(0,), (1,)], width, low, high, *state)
    swapped = swap(jnp.concatenate([mate] + [block[1:] for block in across], axis=0), "patch", 1)
    sky = slice(fibres, fibres + 2)
    part = own[0, sky] + jnp.sum(swapped[:, sky], axis=0)
    for block in across:
        part = part + block[0, sky]
    totals = tree([part] + [swap(part, "ccd", s) for s in range(1, cameras)])
    calibrated, model = finish(fibres, gain, mask, own, swapped, totals, across)
    return calibrated[None], model[0]


def solution(mesh):
    return jax.shard_map(
        per_device,
        mesh=mesh,
        in_specs=(
            P("ccd", "patch", None),
            P("ccd", "patch", None),
            P("ccd", "patch", None, None, None),
            P("ccd", "patch", None),
            P("ccd", "patch", None),
            P("ccd"),
            P("ccd", None),
            P("ccd", None),
        ),
        out_specs=(P("ccd", None, "patch"), P("patch")),
        check_vma=False,
    )
```

time: 155 us -> 50.3 us (0.32)
  matrix products: 72.9 us -> 0 us
  local copies, waits for them, and re-layouts: 30.8 us -> 7.73 us
  Pallas kernels: 0 us -> 21.7 us
  blocking collectives: 12 us -> 0 us
  waiting for transfers between devices: 14.6 us -> 5.17 us
  other arithmetic: 8.36 us -> 0.71 us
    dot_general x29 -> x0, matrix products: 72.9 us -> none  [the longest x9 41.4 us: relax(): jnp.einsum('cf,cpr->fpr', profile, residual, preferred_element_type=jnp.f...]
    pallas_call x0 -> x4, Pallas kernels: none -> 21.7 us  [the longest x2 15.1 us: relax(): pl.pallas_call(functools.partial(relax_kernel, groups), in_specs=[near] *...]
    psum x1 -> x0, blocking collectives: 12 us -> none  [per_device(): sky_total, weight_total = lax.psum((sky_terms, weight_terms), 'ccd')]
    all_to_all x2 -> x0, waiting for transfers between devices: 11.5 us -> none  [the longest x1 6.02 us: per_device(): lax.all_to_all(extracted_weight, 'patch', split_axis=1, concat_axis=0, ti...]
    all_to_all x2 -> x0, starting transfers between devices: 10.2 us -> none  [the longest x1 6.81 us: per_device(): lax.all_to_all(extracted, 'patch', split_axis=1, concat_axis=0, tiled=True)]
    ppermute x2 -> x9, starting transfers between devices: 3.66 us -> 13.1 us  [the longest x8 12.4 us: swap(): lax.ppermute(values, axis, [(i, i ^ shift) for i in range(lax.axis_size(a...]
    slice x7 -> x4, local copies, waits for them, and re-layouts: 8.3 us -> 0.97 us  [the longest x1 0.96 us: edges(): first = jnp.concatenate([counts[:HALO], weights[:HALO]], axis=0)]
    concatenate x2 -> x1, other arithmetic: 5.91 us -> 0.02 us  [per_device(): jnp.concatenate([mate] + [block[1:] for block in across], axis=0)]
  transfers between devices with their start and end apart: 4 -> 9, of which waited for: 3 -> 4; matrix products, arithmetic and copies ran while one was open for 2% -> 0% of each run, Pallas kernels for 0% -> 19%
where the time goes in v2:
time: 50.3 us; the launch traced here: 49.9 us
  Pallas kernels  21.7 us (43%)
  starting transfers between devices  13.1 us (26%)
  local copies, waits for them, and re-layouts  7.73 us (15%)
  waiting for transfers between devices  5.17 us (10%)
  between operations  1.52 us (3%)
  other arithmetic  0.71 us (1%)
    pallas_call x2, Pallas kernels, relax(): pl.pallas_call(functools.partial(relax_kernel, groups), in_specs=[near] *...  15.1 us
    ppermute x8, starting transfers between devices, swap(): lax.ppermute(values, axis, [(i, i ^ shift) for i in range(lax.axis_size(a...  12.4 us
    unnamed x28, local copies, waits for them, and re-layouts  6.76 us
    ppermute x8, waiting for transfers between devices, swap(): lax.ppermute(values, axis, [(i, i ^ shift) for i in range(lax.axis_size(a...  5.16 us
    pallas_call x1, Pallas kernels, prepare(): pl.pallas_call(prepare_kernel, in_specs=[far] * 8, out_specs=[near] * 11,...  4.59 us
    pallas_call x1, Pallas kernels, finish(): pl.pallas_call(functools.partial(finish_kernel, fibres), in_specs=[near]...  1.96 us
  transfers between devices with their start and end apart: 9, of which 4 were waited for; matrix products, arithmetic and copies ran while one was open for 0% of the time, Pallas kernels for 19%

profile of v2, /device:TPU:0, one launch (start us, length us, event | category | flops | bytes accessed | tf_op | source)
XLA Modules:
  0.0 49.9 jit_solution(12717462129799523796)
XLA Ops:
  0.6 1.0 %slice_bitcast_fusion.2 = (bf16[8,4096]{1,0:T(8,128)(2,1)S(1)}, bf16[8,4096]{1,0:T(8,128)(2,1)S(1)}, bf16[8,4096]{1,0:T(8,128)(2,1)S(1)}, bf16[8,4096]{1,0:T(8,128)(2,1)S(1)}) fusion(bf16[1,128,4096]{2,1,0:T(8,128)(2,1)} %param.9, bf16[1,128,4096]{2,1,0:T(8,128)(2,1)} %param.8), kind=kLoop, calls=%fused_computation.9 | loop fusion | bytes 524288 | tf_op jit(solution)/shard_map/slice | solution.py:367
  1.7 0.7 %collective-permute-start.1 = (bf16[16,4096]{1,0:T(8,128)(2,1)S(1)}, bf16[16,4096]{1,0:T(8,128)(2,1)S(1)}, u32[]{:S(2)}, u32[]{:S(2)}) collective-permute-start(bf16[16,4096]{1,0:T(8,128)(2,1)S(1)} %get-tuple-element.46), channel_id=1, source_target_pairs={{1,2},{3,4},{5,6},{2,1},{4,3},{6,5},{9,10},{11,12},{13,14},{10,9},... | collective-permute-start | bytes 393224 | tf_op jit(solution)/shard_map/ppermute | solution.py:370
  2.3 4.4 %collective-permute-start = (bf16[16,4096]{1,0:T(8,128)(2,1)S(1)}, bf16[16,4096]{1,0:T(8,128)(2,1)S(1)}, u32[]{:S(2)}, u32[]{:S(2)}) collective-permute-start(bf16[16,4096]{1,0:T(8,128)(2,1)S(1)} %get-tuple-element.47), channel_id=1, source_target_pairs={{0,1},{1,0},{2,3},{3,2},{4,5},{5,4},{6,7},{7,6},{8,9},{9,8},{10,11... | collective-permute-start | bytes 393224 | tf_op jit(solution)/shard_map/ppermute | solution.py:359
  7.4 1.6 %copy-done = bf16[1,1,64,128,128]{4,3,2,1,0:T(8,128)(2,1)S(1)} copy-done((bf16[1,1,64,128,128]{4,3,2,1,0:T(8,128)(2,1)S(1)}, bf16[1,1,64,128,128]{4,3,2,1,0:T(8,128)(2,1)}, u32[]{:S(2)}) %copy-start) | copy-done | bytes 2097176
  8.9 1.2 %copy-done.1 = bf16[1,128,4096]{2,1,0:T(8,128)(2,1)S(1)} copy-done((bf16[1,128,4096]{2,1,0:T(8,128)(2,1)S(1)}, bf16[1,128,4096]{2,1,0:T(8,128)(2,1)}, u32[]{:S(2)}) %copy-start.1) | copy-done | bytes 1048600
  10.2 1.2 %copy-done.2 = bf16[1,128,4096]{2,1,0:T(8,128)(2,1)S(1)} copy-done((bf16[1,128,4096]{2,1,0:T(8,128)(2,1)S(1)}, bf16[1,128,4096]{2,1,0:T(8,128)(2,1)}, u32[]{:S(2)}) %copy-start.2) | copy-done | bytes 1048600
  11.4 0.7 %copy-done.5 = s32[1,16,16]{2,1,0:T(8,128)S(1)} copy-done((s32[1,16,16]{2,1,0:T(8,128)S(1)}, s32[1,16,16]{2,1,0:T(8,128)}, u32[]{:S(2)}) %copy-start.5) | copy-done | bytes 1048
  12.1 0.7 %copy-done.7 = bf16[1,16,16]{2,1,0:T(8,128)(2,1)S(1)} copy-done((bf16[1,16,16]{2,1,0:T(8,128)(2,1)S(1)}, bf16[1,16,16]{2,1,0:T(8,128)(2,1)}, u32[]{:S(2)}) %copy-start.7) | copy-done | bytes 536
  12.8 0.7 %copy-done.8 = s32[1,16]{1,0:T(1,128)S(1)} copy-done((s32[1,16]{1,0:T(1,128)S(1)}, s32[1,16]{1,0:T(1,128)}, u32[]{:S(2)}) %copy-start.8) | copy-done | bytes 88
  13.4 0.7 %copy-done.9 = s32[1,128]{1,0:T(1,128)S(1)} copy-done((s32[1,128]{1,0:T(1,128)S(1)}, s32[1,128]{1,0:T(1,128)}, u32[]{:S(2)}) %copy-start.9) | copy-done | bytes 536
  14.1 4.6 %prepare.1 = (f32[64,256,128]{2,1,0:T(8,128)S(1)}, f32[64,16,128]{2,1,0:T(8,128)S(1)}, f32[64,16,128]{2,1,0:T(8,128)S(1)}, bf16[64,128,128]{2,1,0:T(8,128)(2,1)S...) custom-call(f32[1,1]{1,0:T(1,128)} %bitcast.36.gain, ...), custom_call_target="tpu_custom_call" | custom-call | tf_op jit(solution)/shard_map/prepare/pallas_call | solution.py:163
  18.8 10.3 %relax.2 = (f32[2,24,512]{2,1,0:T(8,128)S(1)}, f32[2,24,512]{2,1,0:T(8,128)S(1)}, f32[2,24,512]{2,1,0:T(8,128)S(1)}) custom-call(bf16[16,4096]{1,0:T(8,128)(2,1)S(1)} %get-tuple-element.45.low, bf16[16,4096]{1,0:T(8,128)(2,1)S(1)} %get-tuple-element.44.high, f32[64,256,128]{2,1,0:T(8,128)S(1)} %get-tuple-element.35.terms_own, ...), custom_call_target="tpu_custom_call" | custom-call | tf_op jit(solution)/shard_map/relax/pallas_call | solution.py:311
  29.1 1.6 %collective-permute-start.2 = (f32[2,24,512]{2,1,0:T(8,128)S(1)}, f32[2,24,512]{2,1,0:T(8,128)S(1)}, u32[]{:S(2)}, u32[]{:S(2)}) collective-permute-start(f32[2,24,512]{2,1,0:T(8,128)S(1)} %get-tuple-element.32), channel_id=1, source_target_pairs={{0,2},{1,3},{2,0},{3,1},{4,6},{5,7},{6,4},{7,5},{8,10},{9,11},{10,... | collective-permute-start | bytes 294920 | tf_op jit(solution)/shard_map/ppermute | solution.py:359
  30.7 0.1 collective-permute-start.3
  30.8 1.9 %collective-permute-start.4 = (f32[2,24,512]{2,1,0:T(8,128)S(1)}, f32[2,24,512]{2,1,0:T(8,128)S(1)}, u32[]{:S(2)}, u32[]{:S(2)}) collective-permute-start(f32[2,24,512]{2,1,0:T(8,128)S(1)} %get-tuple-element.34), channel_id=1, source_target_pairs={{0,6},{1,7},{2,4},{3,5},{4,2},{5,3},{6,0},{7,1},{8,14},{9,15},{10,... | collective-permute-start | bytes 294920 | tf_op jit(solution)/shard_map/ppermute | solution.py:359
  32.7 4.8 %relax.3 = (f32[1,24,512]{2,1,0:T(8,128)S(1)}, f32[1,24,512]{2,1,0:T(8,128)S(1)}) custom-call(bf16[16,4096]{1,0:T(8,128)(2,1)S(1)} %get-tuple-element.45.low, bf16[16,4096]{1,0:T(8,128)(2,1)S(1)} %get-tuple-element.44.high, f32[64,256,128]{2,1,0:T(8,128)S(1)} %get-tuple-element.35.terms_own, f32[64,16,128]{2,1,0:T(8,128)S(1)} %get-tuple-element.24.first_own, ...), custom_call_target="tpu_custom_call" | custom-call | tf_op jit(solution)/shard_map/relax/pallas_call | solution.py:311
  37.7 1.4 %collective-permute-done.5.swapped = f32[4,24,512]{2,1,0:T(8,128)S(1)} collective-permute-done((f32[4,24,512]{2,1,0:T(8,128)S(1)}, f32[4,24,512]{2,1,0:T(8,128)S(1)}, u32[]{:S(2)}, u32[]{:S(2)}) %collective-permute-start.5) | collective-permute-done | bytes 196640 | tf_op jit(solution)/shard_map/ppermute | solution.py:359
  39.2 3.7 %collective-permute-start.8 = (f32[2,512]{1,0:T(2,128)S(1)}, f32[2,512]{1,0:T(2,128)S(1)}, u32[]{:S(2)}, u32[]{:S(2)}) collective-permute-start(f32[2,512]{1,0:T(2,128)S(1)} %fusion), channel_id=1, source_target_pairs={{0,24},{8,16},{16,8},{24,0},{1,25},{9,17},{17,9},{25,1},{2,26},{10... | collective-permute-start | bytes 12296 | tf_op jit(solution)/shard_map/ppermute | solution.py:359
  42.8 0.8 %collective-permute-start.6 = (f32[2,512]{1,0:T(2,128)S(1)}, f32[2,512]{1,0:T(2,128)S(1)}, u32[]{:S(2)}, u32[]{:S(2)}) collective-permute-start(f32[2,512]{1,0:T(2,128)S(1)} %fusion), channel_id=1, source_target_pairs={{0,16},{8,24},{16,0},{24,8},{1,17},{9,25},{17,1},{25,9},{2,18},{10... | collective-permute-start | bytes 12296 | tf_op jit(solution)/shard_map/ppermute | solution.py:359
  43.6 1.0 %collective-permute-done.8 = f32[2,512]{1,0:T(2,128)S(1)} collective-permute-done((f32[2,512]{1,0:T(2,128)S(1)}, f32[2,512]{1,0:T(2,128)S(1)}, u32[]{:S(2)}, u32[]{:S(2)}) %collective-permute-start.8) | collective-permute-done | bytes 4128 | tf_op jit(solution)/shard_map/ppermute | solution.py:359
  44.6 1.8 %collective-permute-done.7 = f32[2,512]{1,0:T(2,128)S(1)} collective-permute-done((f32[2,512]{1,0:T(2,128)S(1)}, f32[2,512]{1,0:T(2,128)S(1)}, u32[]{:S(2)}, u32[]{:S(2)}) %collective-permute-start.7) | collective-permute-done | bytes 4128 | tf_op jit(solution)/shard_map/ppermute | solution.py:359
  46.4 0.9 %collective-permute-done.6 = f32[2,512]{1,0:T(2,128)S(1)} collective-permute-done((f32[2,512]{1,0:T(2,128)S(1)}, f32[2,512]{1,0:T(2,128)S(1)}, u32[]{:S(2)}, u32[]{:S(2)}) %collective-permute-start.6) | collective-permute-done | bytes 4128 | tf_op jit(solution)/shard_map/ppermute | solution.py:359
  47.3 0.6 %add_add_fusion.totals = f32[2,512]{1,0:T(2,128)} fusion(f32[2,512]{1,0:T(2,128)S(1)} %collective-permute-done.7, f32[2,512]{1,0:T(2,128)S(1)} %collective-permute-done.8, f32[2,512]{1,0:T(2,128)S(1)} %fusion, f32[2,512]{1,0:T(2,128)S(1)} %collective-permute-done.6), kind=kLoop, calls=%fused_computation.19 | loop fusion | flops 3072 | bytes 20480 | tf_op jit(solution)/shard_map/add | solution.py:355
  48.0 2.0 %finish.1 = (f32[128,512]{1,0:T(8,128)}, f32[1,512]{1,0:T(1,128)}) custom-call(f32[8,128]{1,0:T(8,128)} %copy-done.6, f32[128,128]{1,0:T(8,128)} %copy-done.3, f32[1,24,512]{2,1,0:T(8,128)} %copy-done.4, f32[4,24,512]{2,1,0:T(8,128)} %copy-done.13, f32[2,512]{1,0:T(2,128)} %add_add_fusion.totals, f32[2,24,512]{2,1,0:T(8,128)} %copy-done.10, ...), custom_call_target="tpu_custom_call" | custom-call | tf_op jit(solution)/shard_map/finish/pallas_call | solution.py:342
  (36 shorter events, 0.3 us)
Async XLA Ops:
  1.7 17.0 %collective-permute-start.1 = (bf16[16,4096]{1,0:T(8,128)(2,1)S(1)}, bf16[16,4096]{1,0:T(8,128)(2,1)S(1)}, u32[]{:S(2)}, u32[]{:S(2)}) collective-permute-start(bf16[16,4096]{1,0:T(8,128)(2,1)S(1)} %get-tuple-element.46), channel_id=1, source_target_pairs={{1,2},{3,4},{5,6},{2,1},{4,3},{6,5},{9,10},{11,12},{13,14},{10,9},... | collective-permute-start | bytes 393224 | tf_op jit(solution)/shard_map/ppermute | solution.py:370
  2.3 16.4 %collective-permute-start = (bf16[16,4096]{1,0:T(8,128)(2,1)S(1)}, bf16[16,4096]{1,0:T(8,128)(2,1)S(1)}, u32[]{:S(2)}, u32[]{:S(2)}) collective-permute-start(bf16[16,4096]{1,0:T(8,128)(2,1)S(1)} %get-tuple-element.47), channel_id=1, source_target_pairs={{0,1},{1,0},{2,3},{3,2},{4,5},{5,4},{6,7},{7,6},{8,9},{9,8},{10,11... | collective-permute-start | bytes 393224 | tf_op jit(solution)/shard_map/ppermute | solution.py:359
  7.3 1.6 %copy-start = (bf16[1,1,64,128,128]{4,3,2,1,0:T(8,128)(2,1)S(1)}, bf16[1,1,64,128,128]{4,3,2,1,0:T(8,128)(2,1)}, u32[]{:S(2)}) copy-start(bf16[1,1,64,128,128]{4,3,2,1,0:T(8,128)(2,1)} %param.10) | copy-start | bytes 6291460
  8.9 1.2 %copy-start.1 = (bf16[1,128,4096]{2,1,0:T(8,128)(2,1)S(1)}, bf16[1,128,4096]{2,1,0:T(8,128)(2,1)}, u32[]{:S(2)}) copy-start(bf16[1,128,4096]{2,1,0:T(8,128)(2,1)} %param.8) | copy-start | bytes 3145732
  10.2 1.2 %copy-start.2 = (bf16[1,128,4096]{2,1,0:T(8,128)(2,1)S(1)}, bf16[1,128,4096]{2,1,0:T(8,128)(2,1)}, u32[]{:S(2)}) copy-start(bf16[1,128,4096]{2,1,0:T(8,128)(2,1)} %param.9) | copy-start | bytes 3145732
  11.4 0.7 %copy-start.5 = (s32[1,16,16]{2,1,0:T(8,128)S(1)}, s32[1,16,16]{2,1,0:T(8,128)}, u32[]{:S(2)}) copy-start(s32[1,16,16]{2,1,0:T(8,128)} %param.12) | copy-start | bytes 3076
  12.1 0.7 %copy-start.7 = (bf16[1,16,16]{2,1,0:T(8,128)(2,1)S(1)}, bf16[1,16,16]{2,1,0:T(8,128)(2,1)}, u32[]{:S(2)}) copy-start(bf16[1,16,16]{2,1,0:T(8,128)(2,1)} %param.11) | copy-start | bytes 1540
  12.8 0.7 %copy-start.8 = (s32[1,16]{1,0:T(1,128)S(1)}, s32[1,16]{1,0:T(1,128)}, u32[]{:S(2)}) copy-start(s32[1,16]{1,0:T(1,128)} %sky.1) | copy-start | bytes 196
  13.4 0.7 %copy-start.9 = (s32[1,128]{1,0:T(1,128)S(1)}, s32[1,128]{1,0:T(1,128)}, u32[]{:S(2)}) copy-start(s32[1,128]{1,0:T(1,128)} %mask.1) | copy-start | bytes 1540
  18.7 10.4 %copy-start.3 = (f32[128,128]{1,0:T(8,128)}, f32[128,128]{1,0:T(8,128)S(1)}, u32[]{:S(2)}) copy-start(f32[128,128]{1,0:T(8,128)S(1)} %get-tuple-element.22.mask) | copy-start | bytes 196612
  18.7 10.4 %copy-start.6 = (f32[8,128]{1,0:T(8,128)}, f32[8,128]{1,0:T(8,128)S(1)}, u32[]{:S(2)}) copy-start(f32[8,128]{1,0:T(8,128)S(1)} %get-tuple-element.21.gain) | copy-start | bytes 12292
  29.1 8.4 %collective-permute-start.2 = (f32[2,24,512]{2,1,0:T(8,128)S(1)}, f32[2,24,512]{2,1,0:T(8,128)S(1)}, u32[]{:S(2)}, u32[]{:S(2)}) collective-permute-start(f32[2,24,512]{2,1,0:T(8,128)S(1)} %get-tuple-element.32), channel_id=1, source_target_pairs={{0,2},{1,3},{2,0},{3,1},{4,6},{5,7},{6,4},{7,5},{8,10},{9,11},{10,... | collective-permute-start | bytes 294920 | tf_op jit(solution)/shard_map/ppermute | solution.py:359
  30.7 6.8 %collective-permute-start.3 = (f32[2,24,512]{2,1,0:T(8,128)S(1)}, f32[2,24,512]{2,1,0:T(8,128)S(1)}, u32[]{:S(2)}, u32[]{:S(2)}) collective-permute-start(f32[2,24,512]{2,1,0:T(8,128)S(1)} %get-tuple-element.33), channel_id=1, source_target_pairs={{0,4},{1,5},{2,6},{3,7},{4,0},{5,1},{6,2},{7,3},{8,12},{9,13},{10,... | collective-permute-start | bytes 294920 | tf_op jit(solution)/shard_map/ppermute | solution.py:359
  30.8 6.8 %collective-permute-start.4 = (f32[2,24,512]{2,1,0:T(8,128)S(1)}, f32[2,24,512]{2,1,0:T(8,128)S(1)}, u32[]{:S(2)}, u32[]{:S(2)}) collective-permute-start(f32[2,24,512]{2,1,0:T(8,128)S(1)} %get-tuple-element.34), channel_id=1, source_target_pairs={{0,6},{1,7},{2,4},{3,5},{4,2},{5,3},{6,0},{7,1},{8,14},{9,15},{10,... | collective-permute-start | bytes 294920 | tf_op jit(solution)/shard_map/ppermute | solution.py:359
  37.5 10.5 %copy-start.4 = (f32[1,24,512]{2,1,0:T(8,128)}, f32[1,24,512]{2,1,0:T(8,128)S(1)}, u32[]{:S(2)}) copy-start(f32[1,24,512]{2,1,0:T(8,128)S(1)} %get-tuple-element.36.own) | copy-start | bytes 147460
  37.5 10.4 %copy-start.10 = (f32[2,24,512]{2,1,0:T(8,128)}, f32[2,24,512]{2,1,0:T(8,128)S(1)}, u32[]{:S(2)}) copy-start(f32[2,24,512]{2,1,0:T(8,128)S(1)} %collective-permute-done.2.rest_0_) | copy-start | bytes 294916
  37.5 10.4 %copy-start.11 = (f32[2,24,512]{2,1,0:T(8,128)}, f32[2,24,512]{2,1,0:T(8,128)S(1)}, u32[]{:S(2)}) copy-start(f32[2,24,512]{2,1,0:T(8,128)S(1)} %collective-permute-done.3.rest_1_) | copy-start | bytes 294916
  37.6 10.4 %copy-start.12 = (f32[2,24,512]{2,1,0:T(8,128)}, f32[2,24,512]{2,1,0:T(8,128)S(1)}, u32[]{:S(2)}) copy-start(f32[2,24,512]{2,1,0:T(8,128)S(1)} %collective-permute-done.4.rest_2_) | copy-start | bytes 294916
  37.6 1.5 %collective-permute-start.5 = (f32[4,24,512]{2,1,0:T(8,128)S(1)}, f32[4,24,512]{2,1,0:T(8,128)S(1)}, u32[]{:S(2)}, u32[]{:S(2)}) collective-permute-start(f32[4,24,512]{2,1,0:T(8,128)S(1)} %pad_maximum_fusion), channel_id=1, source_target_pairs={{0,1},{1,0},{2,3},{3,2},{4,5},{5,4},{6,7},{7,6},{8,9},{9,8},{10,11... | collective-permute-start | bytes 589832 | tf_op jit(solution)/shard_map/ppermute | solution.py:359
  39.1 8.8 %copy-start.13 = (f32[4,24,512]{2,1,0:T(8,128)}, f32[4,24,512]{2,1,0:T(8,128)S(1)}, u32[]{:S(2)}) copy-start(f32[4,24,512]{2,1,0:T(8,128)S(1)} %collective-permute-done.5.swapped) | copy-start | bytes 589828
  39.2 5.5 %collective-permute-start.8 = (f32[2,512]{1,0:T(2,128)S(1)}, f32[2,512]{1,0:T(2,128)S(1)}, u32[]{:S(2)}, u32[]{:S(2)}) collective-permute-start(f32[2,512]{1,0:T(2,128)S(1)} %fusion), channel_id=1, source_target_pairs={{0,24},{8,16},{16,8},{24,0},{1,25},{9,17},{17,9},{25,1},{2,26},{10... | collective-permute-start | bytes 12296 | tf_op jit(solution)/shard_map/ppermute | solution.py:359
  42.8 3.6 %collective-permute-start.7 = (f32[2,512]{1,0:T(2,128)S(1)}, f32[2,512]{1,0:T(2,128)S(1)}, u32[]{:S(2)}, u32[]{:S(2)}) collective-permute-start(f32[2,512]{1,0:T(2,128)S(1)} %fusion), channel_id=1, source_target_pairs={{0,8},{8,0},{16,24},{24,16},{1,9},{9,1},{17,25},{25,17},{2,10},{10... | collective-permute-start | bytes 12296 | tf_op jit(solution)/shard_map/ppermute | solution.py:359
  42.8 4.5 %collective-permute-start.6 = (f32[2,512]{1,0:T(2,128)S(1)}, f32[2,512]{1,0:T(2,128)S(1)}, u32[]{:S(2)}, u32[]{:S(2)}) collective-permute-start(f32[2,512]{1,0:T(2,128)S(1)} %fusion), channel_id=1, source_target_pairs={{0,16},{8,24},{16,0},{24,8},{1,17},{9,25},{17,1},{25,9},{2,18},{10... | collective-permute-start | bytes 12296 | tf_op jit(solution)/shard_map/ppermute | solution.py:359

commit v3 on v2

v3 whole, which is shorter than its diff:
```python
import functools
import jax
import jax.numpy as jnp
from jax import lax
from jax.sharding import PartitionSpec as P
from jax.experimental import pallas as pl
from jax.experimental.pallas import tpu as pltpu

LW = 64
ITERS = 10
HALO = 8
RIDGE = 0.1
PRIOR = 1.0
LANES = 128
EXTRA = 8
F32 = jnp.float32
BF16 = jnp.bfloat16


def mm(a, b):
    return jnp.dot(a, b, preferred_element_type=F32)


def pair_mm(a, b, stacked):
    a = a.astype(BF16)
    b = b.astype(BF16)
    zero = jnp.zeros_like(a)
    left = jnp.concatenate(
        [jnp.concatenate([a, zero], axis=1), jnp.concatenate([zero, b], axis=1)], axis=0
    )
    both = mm(left, stacked)
    return both[: a.shape[0]], both[a.shape[0] :]


def profile_rows(cols, cross, columns):
    fibres = cols.shape[0]
    lane = lax.broadcasted_iota(jnp.int32, (fibres, columns + 2 * HALO), 1)
    column = jnp.where(
        lane < columns, lane, jnp.where(lane < columns + HALO, lane - columns - HALO, lane - HALO)
    ).astype(F32)
    total = jnp.zeros(column.shape, F32)
    for k in range(cols.shape[1]):
        total = total + jnp.where(cols[:, k : k + 1] == column, cross[:, k : k + 1], 0.0)
    return total.astype(BF16).astype(F32)


def split(values):
    top = values.astype(BF16)
    return top, (values - top.astype(F32)).astype(BF16)


def prepare_kernel(
    small, pixels, wave,
    terms, first, mixed, turned, row_total, side, side_sum, main, main_sum,
):
    columns = pixels.shape[0] // 2
    fibres = first.shape[1]
    patches = wave.shape[0]
    square = fibres * fibres
    taps = 2 * HALO

    profile = profile_rows(small[:fibres, :taps], small[:fibres, taps : 2 * taps], columns)
    spread = (profile * jnp.sum(profile, axis=0, keepdims=True)).astype(BF16)
    for f in range(fibres):
        at = slice(f * fibres, (f + 1) * fibres)
        top, low = split(profile * profile[f : f + 1, :])
        main[at, :] = jnp.concatenate([top[:, :columns], low[:, :columns]], axis=1)
        side[at, :] = jnp.concatenate([top[:, columns:], low[:, columns:]], axis=1)
    half = profile.astype(BF16)
    main[square:, :] = jnp.concatenate([spread[:, :columns], jnp.zeros((fibres, columns), BF16)], axis=1)
    side[square:, :] = jnp.concatenate([spread[:, columns:], jnp.zeros((fibres, 2 * HALO), BF16)], axis=1)
    main_sum[...] = jnp.concatenate([half[:, :columns]] * 2, axis=1)
    side_sum[...] = jnp.concatenate([half[:, columns:]] * 2, axis=1)

    for k in range(patches // 2):
        start = LANES - LW // 2 + k * LANES

        def window(rows):
            return jnp.concatenate(
                [pixels[rows, start : start + LANES], pixels[rows, start + LW : start + LW + LANES]], axis=1
            )

        weight = window(slice(columns, 2 * columns))
        top, low = split(weight.astype(F32) * window(slice(columns)).astype(F32))
        both = mm(main[...], jnp.concatenate([weight, weight], axis=0))
        sums = mm(main_sum[...], jnp.concatenate([top, low], axis=0))
        for h in range(2):
            at = slice(h * LANES, (h + 1) * LANES)
            terms[2 * k + h] = both[:square, at]
            mixed[2 * k + h] = both[square:, at]
            first[2 * k + h] = sums[:, at]

    for p in range(patches):
        flipped = wave[p].T
        turned[p] = flipped
        total = jnp.sum(flipped.astype(F32), axis=0, keepdims=True)
        row_total[p] = jnp.broadcast_to(total, row_total.shape[1:])


def prepare(small, pixels, wave, fibres):
    columns = pixels.shape[0] // 2
    patches, window, _ = wave.shape
    square = fibres * fibres
    near = pl.BlockSpec(memory_space=pltpu.VMEM)
    shape = jax.ShapeDtypeStruct
    return pl.pallas_call(
        prepare_kernel,
        in_specs=[near] * 3,
        out_specs=[near] * 7,
        out_shape=[
            shape((patches, square, window), F32),
            shape((patches, fibres, window), F32),
            shape((patches, fibres, window), F32),
            shape(wave.shape, BF16),
            shape((patches, 8, window), F32),
            shape((square + fibres, 4 * HALO), BF16),
            shape((fibres, 4 * HALO), BF16),
        ],
        scratch_shapes=[
            pltpu.VMEM((square + fibres, 2 * columns), BF16),
            pltpu.VMEM((fibres, 2 * columns), BF16),
        ],
        compiler_params=pltpu.CompilerParams(vmem_limit_bytes=8 * 2**20),
        name="prepare",
    )(small, pixels, wave)


def relax_kernel(
    groups, outer, inner, terms_own, first_own, mixed_own, turned, row_total, side, side_sum, small, wave, *rest
):
    outs = rest[: len(groups)]
    mask_out, gain_out, wpad, cpad, terms, first, inverse, flux, row_weight = rest[len(groups) :]
    me = lax.axis_index("patch")
    odd = me % 2 == 1
    square, fibres = terms.shape[1], first.shape[1]
    width = outs[0].shape[-1]
    tiles = width // LANES
    per = width // LW
    flat = [(o, i, s) for o, group in enumerate(groups) for i, s in enumerate(group)]
    owner = [me ^ s for _, _, s in flat]
    pairs = [(g, j) for g in range(len(flat)) for j in range(per // 2)]

    for g in range(len(flat)):
        for t in range(tiles + 2):
            lanes = pl.ds(pl.multiple_of((owner[g] * tiles + t) * LANES, LANES), LANES)
            near = inner[:, lanes].astype(F32)
            far = outer[:, lanes].astype(F32)
            below = jnp.where(odd, near, far)
            above = jnp.where(odd, far, near)
            for i, pad in ((0, cpad), (1, wpad)):
                at = slice(i * HALO, (i + 1) * HALO)
                both = jnp.concatenate([below[at], above[at]], axis=0).astype(BF16)
                pad[g, :, t * LANES : (t + 1) * LANES] = both

    for q, (g, j) in enumerate(pairs):
        start = LANES - LW // 2 + j * LANES

        def window(pad):
            return jnp.concatenate(
                [pad[g, :, start : start + LANES], pad[g, :, start + LW : start + LW + LANES]], axis=1
            )

        weight = window(wpad)
        top, bottom = split(weight.astype(F32) * window(cpad).astype(F32))
        both = mm(side[...], jnp.concatenate([weight, weight], axis=0))
        sums = mm(side_sum[...], jnp.concatenate([top, bottom], axis=0))
        for h in range(2):
            p = owner[g] * per + 2 * j + h
            at = slice(h * LANES, (h + 1) * LANES)
            terms[2 * q + h] = terms_own[p] + both[:square, at]
            first[2 * q + h] = first_own[p] + sums[:, at]
            whole_sum = (mixed_own[p] + both[square:, at]).astype(BF16).astype(F32)
            flux[2 * q + h] = whole_sum * row_total[p, 0:1, :]

    def stacked(ref, g, j):
        return ref[pl.ds(owner[g] * per + 2 * j, 2)].reshape(2 * LANES, LANES)

    for q, (g, j) in enumerate(pairs):
        grid = stacked(wave, g, j)
        weight_pair = pair_mm(flux[2 * q], flux[2 * q + 1], grid)
        step_pair = pair_mm(first[2 * q], first[2 * q + 1], grid)
        for h in range(2):
            total = weight_pair[h] + RIDGE
            row_weight[2 * q + h] = total
            reciprocal = 1.0 / total
            inverse[2 * q + h] = reciprocal
            flux[2 * q + h] = step_pair[h] * reciprocal

    def sweep(_, carry):
        for q, (g, j) in enumerate(pairs):
            now = [flux[2 * q], flux[2 * q + 1]]
            blurred = pair_mm(*now, stacked(turned, g, j))
            folded = []
            for h in range(2):
                total = first[2 * q + h]
                for f in range(fibres):
                    term = terms[2 * q + h, f * fibres : (f + 1) * fibres, :]
                    total = total - term * blurred[h][f : f + 1, :]
                folded.append(total)
            gradient = pair_mm(*folded, stacked(wave, g, j))
            for h in range(2):
                flux[2 * q + h] = now[h] + (gradient[h] - RIDGE * now[h]) * inverse[2 * q + h]
        return carry

    lax.fori_loop(1, ITERS, sweep, 0)

    mask_row = small[fibres : fibres + 1, :]
    sky_row = small[fibres + 1 : fibres + 2, :]
    scale = small[fibres + 2 : fibres + 3, 0:1]
    number = me * fibres + lax.broadcasted_iota(jnp.int32, (fibres, small.shape[1]), 0)
    is_sky = jnp.max(jnp.where(number.astype(F32) == sky_row, 1.0, 0.0), axis=1, keepdims=True)
    count = mask_out.shape[0]
    for b in range(count // fibres):
        row = b * fibres + lax.broadcasted_iota(jnp.int32, (fibres, small.shape[1]), 0)
        lane = lax.broadcasted_iota(jnp.int32, (fibres, small.shape[1]), 1)
        column = jnp.sum(jnp.where(row == lane, mask_row, 0.0), axis=1, keepdims=True)
        mask_out[b * fibres : (b + 1) * fibres, :] = jnp.broadcast_to(column, (fibres, LANES))
    own = mask_out[pl.ds(pl.multiple_of(me * fibres, fibres), fibres), :]
    chosen = is_sky * own * scale
    pick = (chosen, chosen * scale)
    gain_out[...] = jnp.broadcast_to(scale, gain_out.shape)

    margin = LW // 2
    for q, (g, j) in enumerate(pairs):
        half = slice(j * LANES, (j + 1) * LANES)

        def kept(values):
            return jnp.concatenate(
                [values[2 * q, :, margin : margin + LW], values[2 * q + 1, :, margin : margin + LW]],
                axis=1,
            )

        spectrum = kept(flux)
        strength = kept(row_weight)
        o, i, _ = flat[g]
        outs[o][i, :fibres, half] = spectrum
        outs[o][i, fibres:, half] = jnp.concatenate(
            [
                jnp.sum(pick[0] * strength * spectrum, axis=0, keepdims=True),
                jnp.sum(pick[1] * strength, axis=0, keepdims=True),
                jnp.zeros((EXTRA - 2, LANES), F32),
            ],
            axis=0,
        )


def relax(groups, width, outer, inner, terms, first, *rest):
    square, window = terms.shape[1:]
    fibres = first.shape[1]
    number = sum(len(group) for group in groups)
    count = number * width // LW
    count_all = terms.shape[0] * LW // width * fibres
    near = pl.BlockSpec(memory_space=pltpu.VMEM)
    return pl.pallas_call(
        functools.partial(relax_kernel, groups),
        in_specs=[near] * (4 + len(rest)),
        out_specs=[near] * (len(groups) + 2),
        out_shape=[jax.ShapeDtypeStruct((len(group), fibres + EXTRA, width), F32) for group in groups]
        + [jax.ShapeDtypeStruct((count_all, LANES), F32), jax.ShapeDtypeStruct((8, LANES), F32)],
        scratch_shapes=[pltpu.VMEM((number, 2 * HALO, width + 2 * LANES), BF16)] * 2
        + [pltpu.VMEM((count, square, window), F32)]
        + [pltpu.VMEM((count, fibres, window), F32)] * 4,
        compiler_params=pltpu.CompilerParams(vmem_limit_bytes=16 * 2**20),
        name="relax",
    )(outer, inner, terms, first, *rest)


def finish_kernel(fibres, cameras, gain, mask, own, swapped, *rest):
    *blocks_in, calibrated, model = rest
    totals = tree([part[...] for part in blocks_in[:cameras]])
    across = blocks_in[cameras:]
    me = lax.axis_index("patch")
    sky = totals[0:1, :] / (PRIOR + totals[1:2, :])
    model[...] = sky
    blocks = {0: own[0, :fibres, :], 1: swapped[0, :fibres, :]}
    for t, block in enumerate(across):
        blocks[2 * t + 2] = block[0, :fibres, :]
        blocks[2 * t + 3] = swapped[t + 1, :fibres, :]
    for s, block in blocks.items():
        at = pl.ds(pl.multiple_of((me ^ s) * fibres, fibres), fibres)
        calibrated[at, :] = mask[at, 0:1] * (block - gain[0:1, 0:1] * sky)


def finish(fibres, gain, mask, own, swapped, parts, across):
    width = own.shape[-1]
    near = pl.BlockSpec(memory_space=pltpu.VMEM)
    return pl.pallas_call(
        functools.partial(finish_kernel, fibres, len(parts)),
        in_specs=[near] * (4 + len(parts) + len(across)),
        out_specs=[near] * 2,
        out_shape=[
            jax.ShapeDtypeStruct((mask.shape[0], width), F32),
            jax.ShapeDtypeStruct((1, width), F32),
        ],
        name="finish",
    )(gain, mask, own, swapped, *parts, *across)


def tree(terms):
    return terms[0] if len(terms) == 1 else tree(terms[0::2]) + tree(terms[1::2])


def swap(values, axis, shift):
    return lax.ppermute(values, axis, [(i, i ^ shift) for i in range(lax.axis_size(axis))])


def packed(traces, cross, mask, sky, gain):
    width = max(LANES, mask.shape[1])

    def wide(values, fill=0.0):
        values = values.astype(F32)
        return jnp.pad(values, ((0, 0), (0, width - values.shape[1])), constant_values=fill)

    rows = [
        wide(jnp.concatenate([traces.astype(F32), cross.astype(F32)], axis=1)),
        wide(mask),
        wide(sky, -1.0),
        jnp.broadcast_to(gain[:, None], (1, width)),
        jnp.zeros((5, width), F32),
    ]
    return jnp.concatenate(rows, axis=0)


def per_device(
    pixel_counts,
    pixel_weights,
    wave_profile,
    cross_profile,
    trace_columns,
    throughput,
    sky_fibres,
    fibre_mask,
):
    fibres = trace_columns.shape[1]
    parts = lax.axis_size("patch")
    cameras = lax.axis_size("ccd")
    width = pixel_counts.shape[2] // parts
    me = lax.axis_index("patch")
    columns = pixel_counts.shape[1]
    wave = wave_profile[0, 0]
    pixels = jnp.pad(
        jnp.concatenate([pixel_counts[0], pixel_weights[0]], axis=0), ((0, 0), (LANES, LANES))
    )
    first = jnp.concatenate([pixels[:HALO], pixels[columns : columns + HALO]], axis=0)
    final = jnp.concatenate([pixels[columns - HALO : columns], pixels[2 * columns - HALO :]], axis=0)
    odd = me % 2 == 1
    outer = jnp.where(odd, final, first)
    inner = jnp.where(odd, first, final)
    small = packed(
        trace_columns[0] - me * columns, cross_profile[0], fibre_mask, sky_fibres, throughput
    )
    far = [(i, i + 1) for i in range(1, parts - 1, 2)]
    outer = lax.ppermute(outer, "patch", far + [(b, a) for a, b in far])
    inner = swap(inner, "patch", 1)
    state = [*prepare(small, pixels, wave, fibres), small, wave]
    *away, _, _ = relax([(s, s + 1) for s in range(2, parts, 2)], width, outer, inner, *state)
    across = [swap(block, "patch", 2 * t + 2) for t, block in enumerate(away)]
    state[0], *away = lax.optimization_barrier((state[0], *away))
    own, mate, mask, gain = relax([(0,), (1,)], width, outer, inner, *state)
    swapped = swap(jnp.concatenate([mate] + [block[1:] for block in across], axis=0), "patch", 1)
    sky = slice(fibres, fibres + 2)
    part = own[0, sky] + jnp.sum(swapped[:, sky], axis=0)
    for block in across:
        part = part + block[0, sky]
    sums = [part] + [swap(part, "ccd", s) for s in range(1, cameras)]
    calibrated, model = finish(fibres, gain, mask, own, swapped, sums, across)
    return calibrated[None], model[0]


def solution(mesh):
    return jax.shard_map(
        per_device,
        mesh=mesh,
        in_specs=(
            P("ccd", "patch", None),
            P("ccd", "patch", None),
            P("ccd", "patch", None, None, None),
            P("ccd", "patch", None),
            P("ccd", "patch", None),
            P("ccd"),
            P("ccd", None),
            P("ccd", None),
        ),
        out_specs=(P("ccd", None, "patch"), P("patch")),
        check_vma=False,
    )
```

time: 50.3 us -> 46.9 us (0.932)
  local copies, waits for them, and re-layouts: 7.73 us -> 4.77 us
  other arithmetic: 0.71 us -> 2.02 us
  Pallas kernels: 21.7 us -> 20.7 us
  starting transfers between devices: 13.1 us -> 12.4 us
    unnamed x28 -> x36, local copies, waits for them, and re-layouts: 6.76 us -> 4.7 us
    concatenate x0 -> x2, other arithmetic: none -> 1.92 us  [the longest x1 1.84 us: per_device(): jnp.concatenate([pixel_counts[0], pixel_weights[0]], axis=0)]
    pallas_call x2, Pallas kernels: 6.55 us -> 5.02 us  [the longest x1 3.05 us: prepare(): pl.pallas_call(prepare_kernel, in_specs=[near] * 3, out_specs=[near] * 7,...]
    slice x1, local copies, waits for them, and re-layouts: 0.96 us -> 0.02 us  [per_device(): pixels[columns - HALO:columns]]
    ppermute x8, starting transfers between devices: 12.4 us -> 11.7 us  [swap(): lax.ppermute(values, axis, [(i, i ^ shift) for i in range(lax.axis_size(a...]
    add x1 -> x0, other arithmetic: 0.59 us -> none  [tree(): tree(terms[0::2]) + tree(terms[1::2])]
    pallas_call x2, Pallas kernels: 15.1 us -> 15.7 us  [relax(): pl.pallas_call(functools.partial(relax_kernel, groups), in_specs=[near] *...]
  transfers between devices with their start and end apart: 9 -> 9, of which waited for: 4 -> 3; matrix products, arithmetic and copies ran while one was open for 0% -> 0% of each run, Pallas kernels for 19% -> 17%
where the time goes in v3:
time: 46.9 us; the launch traced here: 46.7 us
  Pallas kernels  20.7 us (44%)
  starting transfers between devices  12.4 us (26%)
  waiting for transfers between devices  5.17 us (11%)
  local copies, waits for them, and re-layouts  4.77 us (10%)
  other arithmetic  2.02 us (4%)
  between operations  1.62 us (3%)
    pallas_call x2, Pallas kernels, relax(): pl.pallas_call(functools.partial(relax_kernel, groups), in_specs=[near] *...  15.7 us
    ppermute x8, starting transfers between devices, swap(): lax.ppermute(values, axis, [(i, i ^ shift) for i in range(lax.axis_size(a...  11.7 us
    ppermute x8, waiting for transfers between devices, swap(): lax.ppermute(values, axis, [(i, i ^ shift) for i in range(lax.axis_size(a...  5.17 us
    unnamed x36, local copies, waits for them, and re-layouts  4.7 us
    pallas_call x1, Pallas kernels, prepare(): pl.pallas_call(prepare_kernel, in_specs=[near] * 3, out_specs=[near] * 7,...  3.05 us
    pallas_call x1, Pallas kernels, finish(): pl.pallas_call(functools.partial(finish_kernel, fibres, len(parts)), in_s...  1.97 us
    concatenate x1, other arithmetic, per_device(): jnp.concatenate([pixel_counts[0], pixel_weights[0]], axis=0)  1.84 us
  transfers between devices with their start and end apart: 9, of which 3 were waited for; matrix products, arithmetic and copies ran while one was open for 0% of the time, Pallas kernels for 17%

profile of v3, /device:TPU:0, one launch (start us, length us, event | category | flops | bytes accessed | tf_op | source)
XLA Modules:
  0.0 46.7 jit_solution(17585290839734168108)
XLA Ops:
  0.7 1.8 %fusion.3.pixels = bf16[256,4352]{1,0:T(8,128)(2,1)S(1)} fusion(bf16[128,4096]{1,0:T(8,128)(2,1)} %bitcast.35, bf16[128,4096]{1,0:T(8,128)(2,1)} %bitcast.36), kind=kLoop, calls=%fused_computation.5 | loop fusion | flops 10027008 | bytes 4325376 | tf_op jit(solution)/shard_map/concatenate | solution.py:342
  2.6 1.4 %copy-done.1 = bf16[256,4352]{1,0:T(8,128)(2,1)} copy-done((bf16[256,4352]{1,0:T(8,128)(2,1)}, bf16[256,4352]{1,0:T(8,128)(2,1)S(1)}, u32[]{:S(2)}) %copy-start.1) | copy-done | bytes 2228248
  4.0 0.5 %collective-permute-start.1 = (bf16[16,4352]{1,0:T(8,128)(2,1)S(1)}, bf16[16,4352]{1,0:T(8,128)(2,1)S(1)}, u32[]{:S(2)}, u32[]{:S(2)}) collective-permute-start(bf16[16,4352]{1,0:T(8,128)(2,1)S(1)} %get-tuple-element.40), channel_id=1, source_target_pairs={{0,1},{1,0},{2,3},{3,2},{4,5},{5,4},{6,7},{7,6},{8,9},{9,8},{10,11... | collective-permute-start | bytes 417800 | tf_op jit(solution)/shard_map/ppermute | solution.py:304
  4.5 0.7 %collective-permute-start = (bf16[16,4352]{1,0:T(8,128)(2,1)S(1)}, bf16[16,4352]{1,0:T(8,128)(2,1)S(1)}, u32[]{:S(2)}, u32[]{:S(2)}) collective-permute-start(bf16[16,4352]{1,0:T(8,128)(2,1)S(1)} %get-tuple-element.41), channel_id=1, source_target_pairs={{1,2},{3,4},{5,6},{2,1},{4,3},{6,5},{9,10},{11,12},{13,14},{10,9},... | collective-permute-start | bytes 417800 | tf_op jit(solution)/shard_map/ppermute | solution.py:353
  6.0 0.1 select_maximum_fusion
  6.1 1.6 %copy-done.2 = bf16[256,4352]{1,0:T(8,128)(2,1)S(1)} copy-done((bf16[256,4352]{1,0:T(8,128)(2,1)S(1)}, bf16[256,4352]{1,0:T(8,128)(2,1)}, u32[]{:S(2)}) %copy-start.2) | copy-done | bytes 2228248
  7.7 3.1 %prepare.1 = (f32[64,256,128]{2,1,0:T(8,128)S(1)}, f32[64,16,128]{2,1,0:T(8,128)S(1)}, f32[64,16,128]{2,1,0:T(8,128)S(1)}, bf16[64,128,128]{2,1,0:T(8,128)(2,1)S...) custom-call(f32[24,128]{1,0:T(8,128)S(1)} %concatenate.22.small, ...), custom_call_target="tpu_custom_call" | custom-call | tf_op jit(solution)/shard_map/prepare/pallas_call | solution.py:106
  10.8 0.0 collective-permute-done.1.inner
  10.8 10.9 %relax.2 = (f32[2,24,512]{2,1,0:T(8,128)S(1)}, f32[2,24,512]{2,1,0:T(8,128)S(1)}, f32[2,24,512]{2,1,0:T(8,128)S(1)}, f32[128,128]{1,0:T(8,128)}, f32[8,128]{1,0:T(8,128)}) custom-call(bf16[16,4352]{1,0:T(8,128)(2,1)S(1)} %collective-permute-done.outer, bf16[16,4352]{1,0:T(8,128)(2,1)S(1)} %collective-permute-done.1.inner, ...), custom_call_target="tpu_custom_call" | custom-call | tf_op jit(solution)/shard_map/relax/pallas_call | solution.py:254
  21.6 3.8 %collective-permute-start.2 = (f32[2,24,512]{2,1,0:T(8,128)S(1)}, f32[2,24,512]{2,1,0:T(8,128)S(1)}, u32[]{:S(2)}, u32[]{:S(2)}) collective-permute-start(f32[2,24,512]{2,1,0:T(8,128)S(1)} %get-tuple-element.26), channel_id=1, source_target_pairs={{0,2},{1,3},{2,0},{3,1},{4,6},{5,7},{6,4},{7,5},{8,10},{9,11},{10,... | collective-permute-start | bytes 294920 | tf_op jit(solution)/shard_map/ppermute | solution.py:304
  25.4 2.1 %collective-permute-start.3 = (f32[2,24,512]{2,1,0:T(8,128)S(1)}, f32[2,24,512]{2,1,0:T(8,128)S(1)}, u32[]{:S(2)}, u32[]{:S(2)}) collective-permute-start(f32[2,24,512]{2,1,0:T(8,128)S(1)} %get-tuple-element.27), channel_id=1, source_target_pairs={{0,4},{1,5},{2,6},{3,7},{4,0},{5,1},{6,2},{7,3},{8,12},{9,13},{10,... | collective-permute-start | bytes 294920 | tf_op jit(solution)/shard_map/ppermute | solution.py:304
  27.5 0.9 %collective-permute-start.4 = (f32[2,24,512]{2,1,0:T(8,128)S(1)}, f32[2,24,512]{2,1,0:T(8,128)S(1)}, u32[]{:S(2)}, u32[]{:S(2)}) collective-permute-start(f32[2,24,512]{2,1,0:T(8,128)S(1)} %get-tuple-element.28), channel_id=1, source_target_pairs={{0,6},{1,7},{2,4},{3,5},{4,2},{5,3},{6,0},{7,1},{8,14},{9,15},{10,... | collective-permute-start | bytes 294920 | tf_op jit(solution)/shard_map/ppermute | solution.py:304
  28.4 4.8 %relax.3 = (f32[1,24,512]{2,1,0:T(8,128)S(1)}, f32[1,24,512]{2,1,0:T(8,128)S(1)}, f32[128,128]{1,0:T(8,128)S(1)}, f32[8,128]{1,0:T(8,128)S(1)}) custom-call(bf16[16,4352]{1,0:T(8,128)(2,1)S(1)} %collective-permute-done.outer, bf16[16,4352]{1,0:T(8,128)(2,1)S(1)} %collective-permute-done.1.inner, f32[64,256,128]{2,1,0:T(8,128)S(1)} %get-tuple-element.29.terms_own, ...), custom_call_target="tpu_custom_call" | custom-call | tf_op jit(solution)/shard_map/relax/pallas_call | solution.py:254
  33.2 0.6 %copy-done.3 = f32[128,128]{1,0:T(8,128)} copy-done((f32[128,128]{1,0:T(8,128)}, f32[128,128]{1,0:T(8,128)S(1)}, u32[]{:S(2)}) %copy-start.3) | copy-done | bytes 65560
  33.9 0.0 collective-permute-done.4.rest_6_
  34.0 0.5 %copy-done.5 = f32[8,128]{1,0:T(8,128)} copy-done((f32[8,128]{1,0:T(8,128)}, f32[8,128]{1,0:T(8,128)S(1)}, u32[]{:S(2)}) %copy-start.5) | copy-done | bytes 4120
  34.5 0.0 collective-permute-start.5
  34.5 1.4 %collective-permute-done.5.swapped = f32[4,24,512]{2,1,0:T(8,128)S(1)} collective-permute-done((f32[4,24,512]{2,1,0:T(8,128)S(1)}, f32[4,24,512]{2,1,0:T(8,128)S(1)}, u32[]{:S(2)}, u32[]{:S(2)}) %collective-permute-start.5) | collective-permute-done | bytes 196640 | tf_op jit(solution)/shard_map/ppermute | solution.py:304
  35.9 3.7 %collective-permute-start.8 = (f32[2,512]{1,0:T(2,128)S(1)}, f32[2,512]{1,0:T(2,128)S(1)}, u32[]{:S(2)}, u32[]{:S(2)}) collective-permute-start(f32[2,512]{1,0:T(2,128)S(1)} %fusion.4.rest_0_), channel_id=1, source_target_pairs={{0,24},{8,16},{16,8},{24,0},{1,25},{9,17},{17,9},{25,1},{2,26},{10... | collective-permute-start | bytes 12296 | tf_op jit(solution)/shard_map/ppermute | solution.py:304
  39.6 0.8 %collective-permute-start.6 = (f32[2,512]{1,0:T(2,128)S(1)}, f32[2,512]{1,0:T(2,128)S(1)}, u32[]{:S(2)}, u32[]{:S(2)}) collective-permute-start(f32[2,512]{1,0:T(2,128)S(1)} %fusion.4.rest_0_), channel_id=1, source_target_pairs={{0,8},{8,0},{16,24},{24,16},{1,9},{9,1},{17,25},{25,17},{2,10},{10... | collective-permute-start | bytes 12296 | tf_op jit(solution)/shard_map/ppermute | solution.py:304
  40.4 1.0 %collective-permute-done.8.rest_3_ = f32[2,512]{1,0:T(2,128)S(1)} collective-permute-done((f32[2,512]{1,0:T(2,128)S(1)}, f32[2,512]{1,0:T(2,128)S(1)}, u32[]{:S(2)}, u32[]{:S(2)}) %collective-permute-start.8) | collective-permute-done | bytes 4128 | tf_op jit(solution)/shard_map/ppermute | solution.py:304
  41.4 2.7 %collective-permute-done.7.rest_2_ = f32[2,512]{1,0:T(2,128)S(1)} collective-permute-done((f32[2,512]{1,0:T(2,128)S(1)}, f32[2,512]{1,0:T(2,128)S(1)}, u32[]{:S(2)}, u32[]{:S(2)}) %collective-permute-start.7) | collective-permute-done | bytes 4128 | tf_op jit(solution)/shard_map/ppermute | solution.py:304
  44.2 0.5 %copy-done.13 = f32[2,512]{1,0:T(2,128)} copy-done((f32[2,512]{1,0:T(2,128)}, f32[2,512]{1,0:T(2,128)S(1)}, u32[]{:S(2)}) %copy-start.13) | copy-done | bytes 4120
  44.7 2.0 %finish.1 = (f32[128,512]{1,0:T(8,128)}, f32[1,512]{1,0:T(1,128)}) custom-call(f32[8,128]{1,0:T(8,128)} %copy-done.5, f32[128,128]{1,0:T(8,128)} %copy-done.3, f32[1,24,512]{2,1,0:T(8,128)} %copy-done.4, f32[4,24,512]{2,1,0:T(8,128)} %copy-done.9, f32[2,512]{1,0:T(2,128)} %copy-done.10, f32[2,512]{1,0:T(2,128)} %copy-done.14, f32[2,512]{1,0:T(2,128)} %copy-done.13, ...), custom_call_target="tpu_custom_call" | custom-call | tf_op jit(solution)/shard_map/finish/pallas_call | solution.py:287
  (52 shorter events, 0.2 us)
Async XLA Ops:
  0.6 4.6 %copy-start.11 = (s32[1,16,16]{2,1,0:T(8,128)S(1)}, s32[1,16,16]{2,1,0:T(8,128)}, u32[]{:S(2)}) copy-start(s32[1,16,16]{2,1,0:T(8,128)} %param.12) | copy-start | bytes 3076
  0.7 4.6 %copy-start.15 = (bf16[1,16,16]{2,1,0:T(8,128)(2,1)S(1)}, bf16[1,16,16]{2,1,0:T(8,128)(2,1)}, u32[]{:S(2)}) copy-start(bf16[1,16,16]{2,1,0:T(8,128)(2,1)} %param.11) | copy-start | bytes 1540
  0.7 5.2 %copy-start.16 = (s32[1,16]{1,0:T(1,128)S(1)}, s32[1,16]{1,0:T(1,128)}, u32[]{:S(2)}) copy-start(s32[1,16]{1,0:T(1,128)} %param.14) | copy-start | bytes 196
  0.7 5.3 %copy-start.17 = (s32[1,128]{1,0:T(1,128)S(1)}, s32[1,128]{1,0:T(1,128)}, u32[]{:S(2)}) copy-start(s32[1,128]{1,0:T(1,128)} %param.15) | copy-start | bytes 1540
  0.7 5.4 %copy-start = (bf16[1,1,64,128,128]{4,3,2,1,0:T(8,128)(2,1)S(1)}, bf16[1,1,64,128,128]{4,3,2,1,0:T(8,128)(2,1)}, u32[]{:S(2)}) copy-start(bf16[1,1,64,128,128]{4,3,2,1,0:T(8,128)(2,1)} %param.10) | copy-start | bytes 6291460
  2.6 1.4 %copy-start.1 = (bf16[256,4352]{1,0:T(8,128)(2,1)}, bf16[256,4352]{1,0:T(8,128)(2,1)S(1)}, u32[]{:S(2)}) copy-start(bf16[256,4352]{1,0:T(8,128)(2,1)S(1)} %fusion.3.pixels) | copy-start | bytes 6684676
  4.0 6.7 %collective-permute-start.1 = (bf16[16,4352]{1,0:T(8,128)(2,1)S(1)}, bf16[16,4352]{1,0:T(8,128)(2,1)S(1)}, u32[]{:S(2)}, u32[]{:S(2)}) collective-permute-start(bf16[16,4352]{1,0:T(8,128)(2,1)S(1)} %get-tuple-element.40), channel_id=1, source_target_pairs={{0,1},{1,0},{2,3},{3,2},{4,5},{5,4},{6,7},{7,6},{8,9},{9,8},{10,11... | collective-permute-start | bytes 417800 | tf_op jit(solution)/shard_map/ppermute | solution.py:304
  4.5 6.2 %collective-permute-start = (bf16[16,4352]{1,0:T(8,128)(2,1)S(1)}, bf16[16,4352]{1,0:T(8,128)(2,1)S(1)}, u32[]{:S(2)}, u32[]{:S(2)}) collective-permute-start(bf16[16,4352]{1,0:T(8,128)(2,1)S(1)} %get-tuple-element.41), channel_id=1, source_target_pairs={{1,2},{3,4},{5,6},{2,1},{4,3},{6,5},{9,10},{11,12},{13,14},{10,9},... | collective-permute-start | bytes 417800 | tf_op jit(solution)/shard_map/ppermute | solution.py:353
  6.1 1.6 %copy-start.2 = (bf16[256,4352]{1,0:T(8,128)(2,1)S(1)}, bf16[256,4352]{1,0:T(8,128)(2,1)}, u32[]{:S(2)}) copy-start(bf16[256,4352]{1,0:T(8,128)(2,1)} %copy-done.1) | copy-start | bytes 6684676
  21.6 12.2 %collective-permute-start.2 = (f32[2,24,512]{2,1,0:T(8,128)S(1)}, f32[2,24,512]{2,1,0:T(8,128)S(1)}, u32[]{:S(2)}, u32[]{:S(2)}) collective-permute-start(f32[2,24,512]{2,1,0:T(8,128)S(1)} %get-tuple-element.26), channel_id=1, source_target_pairs={{0,2},{1,3},{2,0},{3,1},{4,6},{5,7},{6,4},{7,5},{8,10},{9,11},{10,... | collective-permute-start | bytes 294920 | tf_op jit(solution)/shard_map/ppermute | solution.py:304
  25.4 8.5 %collective-permute-start.3 = (f32[2,24,512]{2,1,0:T(8,128)S(1)}, f32[2,24,512]{2,1,0:T(8,128)S(1)}, u32[]{:S(2)}, u32[]{:S(2)}) collective-permute-start(f32[2,24,512]{2,1,0:T(8,128)S(1)} %get-tuple-element.27), channel_id=1, source_target_pairs={{0,4},{1,5},{2,6},{3,7},{4,0},{5,1},{6,2},{7,3},{8,12},{9,13},{10,... | collective-permute-start | bytes 294920 | tf_op jit(solution)/shard_map/ppermute | solution.py:304
  27.5 6.4 %collective-permute-start.4 = (f32[2,24,512]{2,1,0:T(8,128)S(1)}, f32[2,24,512]{2,1,0:T(8,128)S(1)}, u32[]{:S(2)}, u32[]{:S(2)}) collective-permute-start(f32[2,24,512]{2,1,0:T(8,128)S(1)} %get-tuple-element.28), channel_id=1, source_target_pairs={{0,6},{1,7},{2,4},{3,5},{4,2},{5,3},{6,0},{7,1},{8,14},{9,15},{10,... | collective-permute-start | bytes 294920 | tf_op jit(solution)/shard_map/ppermute | solution.py:304
  33.2 0.6 %copy-start.3 = (f32[128,128]{1,0:T(8,128)}, f32[128,128]{1,0:T(8,128)S(1)}, u32[]{:S(2)}) copy-start(f32[128,128]{1,0:T(8,128)S(1)} %get-tuple-element.31.mask) | copy-start | bytes 196612
  33.9 10.3 %copy-start.4 = (f32[1,24,512]{2,1,0:T(8,128)}, f32[1,24,512]{2,1,0:T(8,128)S(1)}, u32[]{:S(2)}) copy-start(f32[1,24,512]{2,1,0:T(8,128)S(1)} %get-tuple-element.32.own) | copy-start | bytes 147460
  33.9 10.3 %copy-start.6 = (f32[2,24,512]{2,1,0:T(8,128)}, f32[2,24,512]{2,1,0:T(8,128)S(1)}, u32[]{:S(2)}) copy-start(f32[2,24,512]{2,1,0:T(8,128)S(1)} %collective-permute-done.2.rest_4_) | copy-start | bytes 294916
  33.9 10.2 %copy-start.7 = (f32[2,24,512]{2,1,0:T(8,128)}, f32[2,24,512]{2,1,0:T(8,128)S(1)}, u32[]{:S(2)}) copy-start(f32[2,24,512]{2,1,0:T(8,128)S(1)} %collective-permute-done.3.rest_5_) | copy-start | bytes 294916
  33.9 10.2 %copy-start.8 = (f32[2,24,512]{2,1,0:T(8,128)}, f32[2,24,512]{2,1,0:T(8,128)S(1)}, u32[]{:S(2)}) copy-start(f32[2,24,512]{2,1,0:T(8,128)S(1)} %collective-permute-done.4.rest_6_) | copy-start | bytes 294916
  34.5 1.4 %collective-permute-start.5 = (f32[4,24,512]{2,1,0:T(8,128)S(1)}, f32[4,24,512]{2,1,0:T(8,128)S(1)}, u32[]{:S(2)}, u32[]{:S(2)}) collective-permute-start(f32[4,24,512]{2,1,0:T(8,128)S(1)} %pad_maximum_fusion), channel_id=1, source_target_pairs={{0,1},{1,0},{2,3},{3,2},{4,5},{5,4},{6,7},{7,6},{8,9},{9,8},{10,11... | collective-permute-start | bytes 589832 | tf_op jit(solution)/shard_map/ppermute | solution.py:304
  35.9 8.3 %copy-start.9 = (f32[4,24,512]{2,1,0:T(8,128)}, f32[4,24,512]{2,1,0:T(8,128)S(1)}, u32[]{:S(2)}) copy-start(f32[4,24,512]{2,1,0:T(8,128)S(1)} %collective-permute-done.5.swapped) | copy-start | bytes 589828
  35.9 8.2 %copy-start.10 = (f32[2,512]{1,0:T(2,128)}, f32[2,512]{1,0:T(2,128)S(1)}, u32[]{:S(2)}) copy-start(f32[2,512]{1,0:T(2,128)S(1)} %fusion.4.rest_0_) | copy-start | bytes 12292
  35.9 5.5 %collective-permute-start.8 = (f32[2,512]{1,0:T(2,128)S(1)}, f32[2,512]{1,0:T(2,128)S(1)}, u32[]{:S(2)}, u32[]{:S(2)}) collective-permute-start(f32[2,512]{1,0:T(2,128)S(1)} %fusion.4.rest_0_), channel_id=1, source_target_pairs={{0,24},{8,16},{16,8},{24,0},{1,25},{9,17},{17,9},{25,1},{2,26},{10... | collective-permute-start | bytes 12296 | tf_op jit(solution)/shard_map/ppermute | solution.py:304
  39.6 4.5 %collective-permute-start.7 = (f32[2,512]{1,0:T(2,128)S(1)}, f32[2,512]{1,0:T(2,128)S(1)}, u32[]{:S(2)}, u32[]{:S(2)}) collective-permute-start(f32[2,512]{1,0:T(2,128)S(1)} %fusion.4.rest_0_), channel_id=1, source_target_pairs={{0,16},{8,24},{16,0},{24,8},{1,17},{9,25},{17,1},{25,9},{2,18},{10... | collective-permute-start | bytes 12296 | tf_op jit(solution)/shard_map/ppermute | solution.py:304
  39.6 4.5 %collective-permute-start.6 = (f32[2,512]{1,0:T(2,128)S(1)}, f32[2,512]{1,0:T(2,128)S(1)}, u32[]{:S(2)}, u32[]{:S(2)}) collective-permute-start(f32[2,512]{1,0:T(2,128)S(1)} %fusion.4.rest_0_), channel_id=1, source_target_pairs={{0,8},{8,0},{16,24},{24,16},{1,9},{9,1},{17,25},{25,17},{2,10},{10... | collective-permute-start | bytes 12296 | tf_op jit(solution)/shard_map/ppermute | solution.py:304
  41.4 2.8 %copy-start.12 = (f32[2,512]{1,0:T(2,128)}, f32[2,512]{1,0:T(2,128)S(1)}, u32[]{:S(2)}) copy-start(f32[2,512]{1,0:T(2,128)S(1)} %collective-permute-done.8.rest_3_) | copy-start | bytes 12292
  (3 other events, 1.8 us)

commit v4 on v3

--- a/solution.py
+++ b/solution.py
@@ -37,7 +37,7 @@
     lane = lax.broadcasted_iota(jnp.int32, (fibres, columns + 2 * HALO), 1)
     column = jnp.where(
         lane < columns, lane, jnp.where(lane < columns + HALO, lane - columns - HALO, lane - HALO)
-    ).astype(F32)
+    )
     total = jnp.zeros(column.shape, F32)
     for k in range(cols.shape[1]):
         total = total + jnp.where(cols[:, k : k + 1] == column, cross[:, k : k + 1], 0.0)
@@ -50,16 +50,16 @@
 
 
 def prepare_kernel(
-    small, pixels, wave,
+    traces, cross, pixels, wave,
     terms, first, mixed, turned, row_total, side, side_sum, main, main_sum,
 ):
     columns = pixels.shape[0] // 2
     fibres = first.shape[1]
     patches = wave.shape[0]
     square = fibres * fibres
-    taps = 2 * HALO
-
-    profile = profile_rows(small[:fibres, :taps], small[:fibres, taps : 2 * taps], columns)
+
+    first_column = lax.axis_index("patch") * columns
+    profile = profile_rows(traces[...] - first_column, cross[...].astype(F32), columns)
     spread = (profile * jnp.sum(profile, axis=0, keepdims=True)).astype(BF16)
     for f in range(fibres):
         at = slice(f * fibres, (f + 1) * fibres)
@@ -97,15 +97,16 @@
         row_total[p] = jnp.broadcast_to(total, row_total.shape[1:])
 
 
-def prepare(small, pixels, wave, fibres):
+def prepare(traces, cross, pixels, wave):
     columns = pixels.shape[0] // 2
+    fibres = traces.shape[0]
     patches, window, _ = wave.shape
     square = fibres * fibres
     near = pl.BlockSpec(memory_space=pltpu.VMEM)
     shape = jax.ShapeDtypeStruct
     return pl.pallas_call(
         prepare_kernel,
-        in_specs=[near] * 3,
+        in_specs=[near] * 4,
         out_specs=[near] * 7,
         out_shape=[
             shape((patches, square, window), F32),
@@ -122,14 +123,14 @@
         ],
         compiler_params=pltpu.CompilerParams(vmem_limit_bytes=8 * 2**20),
         name="prepare",
-    )(small, pixels, wave)
+    )(traces, cross, pixels, wave)
 
 
 def relax_kernel(
-    groups, outer, inner, terms_own, first_own, mixed_own, turned, row_total, side, side_sum, small, wave, *rest
+    groups, outer, inner, terms_own, first_own, mixed_own, turned, row_total, side, side_sum, wave, sky, mask, gain, *rest
 ):
     outs = rest[: len(groups)]
-    mask_out, gain_out, wpad, cpad, terms, first, inverse, flux, row_weight = rest[len(groups) :]
+    *columns_out, wpad, cpad, terms, first, inverse, flux, row_weight = rest[len(groups) :]
     me = lax.axis_index("patch")
     odd = me % 2 == 1
     square, fibres = terms.shape[1], first.shape[1]
@@ -202,23 +203,24 @@
                 flux[2 * q + h] = now[h] + (gradient[h] - RIDGE * now[h]) * inverse[2 * q + h]
         return carry
 
-    lax.fori_loop(1, ITERS, sweep, 0)
-
-    mask_row = small[fibres : fibres + 1, :]
-    sky_row = small[fibres + 1 : fibres + 2, :]
-    scale = small[fibres + 2 : fibres + 3, 0:1]
-    number = me * fibres + lax.broadcasted_iota(jnp.int32, (fibres, small.shape[1]), 0)
-    is_sky = jnp.max(jnp.where(number.astype(F32) == sky_row, 1.0, 0.0), axis=1, keepdims=True)
-    count = mask_out.shape[0]
-    for b in range(count // fibres):
-        row = b * fibres + lax.broadcasted_iota(jnp.int32, (fibres, small.shape[1]), 0)
-        lane = lax.broadcasted_iota(jnp.int32, (fibres, small.shape[1]), 1)
-        column = jnp.sum(jnp.where(row == lane, mask_row, 0.0), axis=1, keepdims=True)
-        mask_out[b * fibres : (b + 1) * fibres, :] = jnp.broadcast_to(column, (fibres, LANES))
-    own = mask_out[pl.ds(pl.multiple_of(me * fibres, fibres), fibres), :]
+    lax.fori_loop(1, ITERS, sweep, 0, unroll=9)
+
+    number = me * fibres + lax.broadcasted_iota(jnp.int32, (fibres, sky.shape[1]), 0)
+    is_sky = jnp.max(jnp.where(number == sky[...], 1.0, 0.0), axis=1, keepdims=True)
+    row = lax.broadcasted_iota(jnp.int32, (fibres, mask.shape[1]), 0)
+    lane = lax.broadcasted_iota(jnp.int32, (fibres, mask.shape[1]), 1)
+    working = mask[...].astype(F32)
+
+    def mask_column(first_row):
+        return jnp.sum(jnp.where(lane == row + first_row, working, 0.0), axis=1, keepdims=True)
+
+    for out in columns_out:
+        for b in range(out.shape[0] // fibres):
+            out[b * fibres : (b + 1) * fibres, :] = jnp.broadcast_to(mask_column(b * fibres), (fibres, LANES))
+    own = mask_column(me * fibres)
+    scale = gain[0]
     chosen = is_sky * own * scale
     pick = (chosen, chosen * scale)
-    gain_out[...] = jnp.broadcast_to(scale, gain_out.shape)
 
     margin = LW // 2
     for q, (g, j) in enumerate(pairs):
@@ -244,22 +246,21 @@
         )
 
 
-def relax(groups, width, outer, inner, terms, first, *rest):
+def relax(groups, width, columns, outer, inner, terms, first, *rest):
     square, window = terms.shape[1:]
     fibres = first.shape[1]
     number = sum(len(group) for group in groups)
-    count = number * width // LW
-    count_all = terms.shape[0] * LW // width * fibres
+    patches = number * width // LW
     near = pl.BlockSpec(memory_space=pltpu.VMEM)
     return pl.pallas_call(
         functools.partial(relax_kernel, groups),
-        in_specs=[near] * (4 + len(rest)),
-        out_specs=[near] * (len(groups) + 2),
+        in_specs=[near] * (3 + len(rest)) + [pl.BlockSpec(memory_space=pltpu.SMEM)],
+        out_specs=[near] * (len(groups) + len(columns)),
         out_shape=[jax.ShapeDtypeStruct((len(group), fibres + EXTRA, width), F32) for group in groups]
-        + [jax.ShapeDtypeStruct((count_all, LANES), F32), jax.ShapeDtypeStruct((8, LANES), F32)],
+        + [jax.ShapeDtypeStruct((count, LANES), F32) for count in columns],
         scratch_shapes=[pltpu.VMEM((number, 2 * HALO, width + 2 * LANES), BF16)] * 2
-        + [pltpu.VMEM((count, square, window), F32)]
-        + [pltpu.VMEM((count, fibres, window), F32)] * 4,
+        + [pltpu.VMEM((patches, square, window), F32)]
+        + [pltpu.VMEM((patches, fibres, window), F32)] * 4,
         compiler_params=pltpu.CompilerParams(vmem_limit_bytes=16 * 2**20),
         name="relax",
     )(outer, inner, terms, first, *rest)
@@ -278,7 +279,7 @@
         blocks[2 * t + 3] = swapped[t + 1, :fibres, :]
     for s, block in blocks.items():
         at = pl.ds(pl.multiple_of((me ^ s) * fibres, fibres), fibres)
-        calibrated[at, :] = mask[at, 0:1] * (block - gain[0:1, 0:1] * sky)
+        calibrated[at, :] = mask[at, 0:1] * (block - gain[0] * sky)
 
 
 def finish(fibres, gain, mask, own, swapped, parts, across):
@@ -286,12 +287,13 @@
     near = pl.BlockSpec(memory_space=pltpu.VMEM)
     return pl.pallas_call(
         functools.partial(finish_kernel, fibres, len(parts)),
-        in_specs=[near] * (4 + len(parts) + len(across)),
+        in_specs=[pl.BlockSpec(memory_space=pltpu.SMEM)] + [near] * (3 + len(parts) + len(across)),
         out_specs=[near] * 2,
         out_shape=[
             jax.ShapeDtypeStruct((mask.shape[0], width), F32),
             jax.ShapeDtypeStruct((1, width), F32),
         ],
+        compiler_params=pltpu.CompilerParams(vmem_limit_bytes=8 * 2**20),
         name="finish",
     )(gain, mask, own, swapped, *parts, *across)
 
@@ -302,23 +304,6 @@
 
 def swap(values, axis, shift):
     return lax.ppermute(values, axis, [(i, i ^ shift) for i in range(lax.axis_size(axis))])
-
-
-def packed(traces, cross, mask, sky, gain):
-    width = max(LANES, mask.shape[1])
-
-    def wide(values, fill=0.0):
-        values = values.astype(F32)
-        return jnp.pad(values, ((0, 0), (0, width - values.shape[1])), constant_values=fill)
-
-    rows = [
-        wide(jnp.concatenate([traces.astype(F32), cross.astype(F32)], axis=1)),
-        wide(mask),
-        wide(sky, -1.0),
-        jnp.broadcast_to(gain[:, None], (1, width)),
-        jnp.zeros((5, width), F32),
-    ]
-    return jnp.concatenate(rows, axis=0)
 
 
 def per_device(
@@ -346,24 +331,22 @@
     odd = me % 2 == 1
     outer = jnp.where(odd, final, first)
     inner = jnp.where(odd, first, final)
-    small = packed(
-        trace_columns[0] - me * columns, cross_profile[0], fibre_mask, sky_fibres, throughput
-    )
     far = [(i, i + 1) for i in range(1, parts - 1, 2)]
     outer = lax.ppermute(outer, "patch", far + [(b, a) for a, b in far])
     inner = swap(inner, "patch", 1)
-    state = [*prepare(small, pixels, wave, fibres), small, wave]
-    *away, _, _ = relax([(s, s + 1) for s in range(2, parts, 2)], width, outer, inner, *state)
+    state = prepare(trace_columns[0], cross_profile[0], pixels, wave)
+    state = [*state, wave, sky_fibres, fibre_mask, throughput]
+    away = relax([(s, s + 1) for s in range(2, parts, 2)], width, (), outer, inner, *state)
     across = [swap(block, "patch", 2 * t + 2) for t, block in enumerate(away)]
     state[0], *away = lax.optimization_barrier((state[0], *away))
-    own, mate, mask, gain = relax([(0,), (1,)], width, outer, inner, *state)
+    own, mate, mask = relax([(0,), (1,)], width, (fibre_mask.shape[1],), outer, inner, *state)
     swapped = swap(jnp.concatenate([mate] + [block[1:] for block in across], axis=0), "patch", 1)
     sky = slice(fibres, fibres + 2)
     part = own[0, sky] + jnp.sum(swapped[:, sky], axis=0)
     for block in across:
         part = part + block[0, sky]
     sums = [part] + [swap(part, "ccd", s) for s in range(1, cameras)]
-    calibrated, model = finish(fibres, gain, mask, own, swapped, sums, across)
+    calibrated, model = finish(fibres, throughput, mask, own, swapped, sums, across)
     return calibrated[None], model[0]
 
 

time: 46.9 us -> 42.1 us (0.90)
  local copies, waits for them, and re-layouts: 4.77 us -> 0.06 us
  Pallas kernels: 20.7 us -> 16.8 us
  waiting for transfers between devices: 5.17 us -> 8.42 us
  starting transfers between devices: 12.4 us -> 13.2 us
    unnamed x36 -> x10, local copies, waits for them, and re-layouts: 4.7 us -> 0.03 us
    ppermute x8, waiting for transfers between devices: 5.17 us -> 8.42 us  [swap(): lax.ppermute(values, axis, [(i, i ^ shift) for i in range(lax.axis_size(a...]
    pallas_call x2, Pallas kernels: 15.7 us -> 13 us  [relax(): pl.pallas_call(functools.partial(relax_kernel, groups), in_specs=[near] *...]
    pallas_call x1, Pallas kernels: 1.97 us -> 0.8 us  [finish(): pl.pallas_call(functools.partial(finish_kernel, fibres, len(parts)), in_s...]
    ppermute x8, starting transfers between devices: 11.7 us -> 12.6 us  [swap(): lax.ppermute(values, axis, [(i, i ^ shift) for i in range(lax.axis_size(a...]
  transfers between devices with their start and end apart: 9 -> 9, of which waited for: 3 -> 4; matrix products, arithmetic and copies ran while one was open for 0% -> 0% of each run, Pallas kernels for 17% -> 16%
where the time goes in v4:
time: 42.1 us; the launch traced here: 41.9 us
  Pallas kernels  16.8 us (40%)
  starting transfers between devices  13.2 us (31%)
  waiting for transfers between devices  8.42 us (20%)
  other arithmetic  1.92 us (5%)
  between operations  1.48 us (4%)
    pallas_call x2, Pallas kernels, relax(): pl.pallas_call(functools.partial(relax_kernel, groups), in_specs=[near] *...  13 us
    ppermute x8, starting transfers between devices, swap(): lax.ppermute(values, axis, [(i, i ^ shift) for i in range(lax.axis_size(a...  12.6 us
    ppermute x8, waiting for transfers between devices, swap(): lax.ppermute(values, axis, [(i, i ^ shift) for i in range(lax.axis_size(a...  8.42 us
    pallas_call x1, Pallas kernels, prepare(): pl.pallas_call(prepare_kernel, in_specs=[near] * 4, out_specs=[near] * 7,...  3.01 us
    concatenate x1, other arithmetic, per_device(): jnp.concatenate([pixel_counts[0], pixel_weights[0]], axis=0)  1.83 us
  transfers between devices with their start and end apart: 9, of which 4 were waited for; matrix products, arithmetic and copies ran while one was open for 0% of the time, Pallas kernels for 16%

profile of v4, /device:TPU:0, one launch (start us, length us, event | category | flops | bytes accessed | tf_op | source)
XLA Modules:
  0.0 41.9 jit_solution(643244017472783038)
XLA Ops:
  0.7 1.8 %fusion.3.pixels = bf16[256,4352]{1,0:T(8,128)(2,1)S(1)} fusion(bf16[128,4096]{1,0:T(8,128)(2,1)} %bitcast.32, bf16[128,4096]{1,0:T(8,128)(2,1)} %bitcast.33), kind=kLoop, calls=%fused_computation.5 | loop fusion | flops 10027008 | bytes 4325376 | tf_op jit(solution)/shard_map/concatenate | solution.py:327
  2.5 0.1 broadcast_select_fusion
  2.6 0.0 copy-start.3
  2.6 0.0 copy-start.4
  2.6 0.7 %collective-permute-start = (bf16[16,4352]{1,0:T(8,128)(2,1)S(1)}, bf16[16,4352]{1,0:T(8,128)(2,1)S(1)}, u32[]{:S(2)}, u32[]{:S(2)}) collective-permute-start(bf16[16,4352]{1,0:T(8,128)(2,1)S(1)} %get-tuple-element.39), channel_id=1, source_target_pairs={{1,2},{3,4},{5,6},{2,1},{4,3},{6,5},{9,10},{11,12},{13,14},{10,9},... | collective-permute-start | bytes 417800 | tf_op jit(solution)/shard_map/ppermute | solution.py:335
  3.3 4.4 %collective-permute-start.1 = (bf16[16,4352]{1,0:T(8,128)(2,1)S(1)}, bf16[16,4352]{1,0:T(8,128)(2,1)S(1)}, u32[]{:S(2)}, u32[]{:S(2)}) collective-permute-start(bf16[16,4352]{1,0:T(8,128)(2,1)S(1)} %get-tuple-element.38), channel_id=1, source_target_pairs={{0,1},{1,0},{2,3},{3,2},{4,5},{5,4},{6,7},{7,6},{8,9},{9,8},{10,11... | collective-permute-start | bytes 417800 | tf_op jit(solution)/shard_map/ppermute | solution.py:306
  8.3 3.0 %prepare.1 = (f32[64,256,128]{2,1,0:T(8,128)S(1)}, f32[64,16,128]{2,1,0:T(8,128)S(1)}, f32[64,16,128]{2,1,0:T(8,128)S(1)}, bf16[64,128,128]{2,1,0:T(8,128)(2,1)S...) custom-call(s32[16,16]{1,0:T(8,128)S(1)} %bitcast.30, ...), custom_call_target="tpu_custom_call" | custom-call | tf_op jit(solution)/shard_map/prepare/pallas_call | solution.py:107
  11.4 0.0 collective-permute-done.outer
  11.4 0.0 collective-permute-done.1.inner
  11.4 9.2 %relax.2 = (f32[2,24,512]{2,1,0:T(8,128)S(1)}, f32[2,24,512]{2,1,0:T(8,128)S(1)}, f32[2,24,512]{2,1,0:T(8,128)S(1)}) custom-call(bf16[16,4352]{1,0:T(8,128)(2,1)S(1)} %collective-permute-done.outer, bf16[16,4352]{1,0:T(8,128)(2,1)S(1)} %collective-permute-done.1.inner, f32[64,256,128]{2,1,0:T(8,128)S(1)} %get-tuple-element.28.terms_own, ...), custom_call_target="tpu_custom_call" | custom-call | tf_op jit(solution)/shard_map/relax/pallas_call | solution.py:255
  20.5 1.6 %collective-permute-start.2 = (f32[2,24,512]{2,1,0:T(8,128)S(1)}, f32[2,24,512]{2,1,0:T(8,128)S(1)}, u32[]{:S(2)}, u32[]{:S(2)}) collective-permute-start(f32[2,24,512]{2,1,0:T(8,128)S(1)} %get-tuple-element.25), channel_id=1, source_target_pairs={{0,2},{1,3},{2,0},{3,1},{4,6},{5,7},{6,4},{7,5},{8,10},{9,11},{10,... | collective-permute-start | bytes 294920 | tf_op jit(solution)/shard_map/ppermute | solution.py:306
  22.1 2.0 %collective-permute-start.3 = (f32[2,24,512]{2,1,0:T(8,128)S(1)}, f32[2,24,512]{2,1,0:T(8,128)S(1)}, u32[]{:S(2)}, u32[]{:S(2)}) collective-permute-start(f32[2,24,512]{2,1,0:T(8,128)S(1)} %get-tuple-element.26), channel_id=1, source_target_pairs={{0,4},{1,5},{2,6},{3,7},{4,0},{5,1},{6,2},{7,3},{8,12},{9,13},{10,... | collective-permute-start | bytes 294920 | tf_op jit(solution)/shard_map/ppermute | solution.py:306
  24.1 0.0 collective-permute-start.4
  24.1 3.8 %relax.3 = (f32[1,24,512]{2,1,0:T(8,128)S(1)}, f32[1,24,512]{2,1,0:T(8,128)S(1)}, f32[128,128]{1,0:T(8,128)S(1)}) custom-call(bf16[16,4352]{1,0:T(8,128)(2,1)S(1)} %collective-permute-done.outer, bf16[16,4352]{1,0:T(8,128)(2,1)S(1)} %collective-permute-done.1.inner, f32[64,256,128]{2,1,0:T(8,128)S(1)} %get-tuple-element.28.terms_own, ...), custom_call_target="tpu_custom_call" | custom-call | tf_op jit(solution)/shard_map/relax/pallas_call | solution.py:255
  28.0 1.9 %collective-permute-done.3.rest_5_ = f32[2,24,512]{2,1,0:T(8,128)S(1)} collective-permute-done((f32[2,24,512]{2,1,0:T(8,128)S(1)}, f32[2,24,512]{2,1,0:T(8,128)S(1)}, u32[]{:S(2)}, u32[]{:S(2)}) %collective-permute-start.3) | collective-permute-done | bytes 98336 | tf_op jit(solution)/shard_map/ppermute | solution.py:306
  29.9 0.2 collective-permute-start.5
  30.1 1.3 %collective-permute-done.5.swapped = f32[4,24,512]{2,1,0:T(8,128)S(1)} collective-permute-done((f32[4,24,512]{2,1,0:T(8,128)S(1)}, f32[4,24,512]{2,1,0:T(8,128)S(1)}, u32[]{:S(2)}, u32[]{:S(2)}) %collective-permute-start.5) | collective-permute-done | bytes 196640 | tf_op jit(solution)/shard_map/ppermute | solution.py:306
  31.5 1.6 %collective-permute-start.6 = (f32[2,512]{1,0:T(2,128)S(1)}, f32[2,512]{1,0:T(2,128)S(1)}, u32[]{:S(2)}, u32[]{:S(2)}) collective-permute-start(f32[2,512]{1,0:T(2,128)S(1)} %fusion.4.rest_0_), channel_id=1, source_target_pairs={{0,8},{8,0},{16,24},{24,16},{1,9},{9,1},{17,25},{25,17},{2,10},{10... | collective-permute-start | bytes 12296 | tf_op jit(solution)/shard_map/ppermute | solution.py:306
  33.1 2.6 %collective-permute-start.7 = (f32[2,512]{1,0:T(2,128)S(1)}, f32[2,512]{1,0:T(2,128)S(1)}, u32[]{:S(2)}, u32[]{:S(2)}) collective-permute-start(f32[2,512]{1,0:T(2,128)S(1)} %fusion.4.rest_0_), channel_id=1, source_target_pairs={{0,16},{8,24},{16,0},{24,8},{1,17},{9,25},{17,1},{25,9},{2,18},{10... | collective-permute-start | bytes 12296 | tf_op jit(solution)/shard_map/ppermute | solution.py:306
  35.7 0.2 collective-permute-start.8
  35.9 0.0 collective-permute-done.6.rest_1_
  35.9 1.7 %collective-permute-done.7.rest_2_ = f32[2,512]{1,0:T(2,128)S(1)} collective-permute-done((f32[2,512]{1,0:T(2,128)S(1)}, f32[2,512]{1,0:T(2,128)S(1)}, u32[]{:S(2)}, u32[]{:S(2)}) %collective-permute-start.7) | collective-permute-done | bytes 4128 | tf_op jit(solution)/shard_map/ppermute | solution.py:306
  37.6 3.5 %collective-permute-done.8.rest_3_ = f32[2,512]{1,0:T(2,128)S(1)} collective-permute-done((f32[2,512]{1,0:T(2,128)S(1)}, f32[2,512]{1,0:T(2,128)S(1)}, u32[]{:S(2)}, u32[]{:S(2)}) %collective-permute-start.8) | collective-permute-done | bytes 4128 | tf_op jit(solution)/shard_map/ppermute | solution.py:306
  41.1 0.8 %finish.1 = (f32[128,512]{1,0:T(8,128)}, f32[1,512]{1,0:T(1,128)}) custom-call(f32[1]{0:T(128)S(6)} %copy.10.gain, f32[128,128]{1,0:T(8,128)S(1)} %get-tuple-element.29.mask, f32[1,24,512]{2,1,0:T(8,128)S(1)} %get-tuple-element.30.own, f32[4,24,512]{2,1,0:T(8,128)S(1)} %collective-permute-done.5.swapped, f32[2,512]{1,0:T(2,128)S(1)} %fusion.4.rest_0_, ...), custom_call_target="tpu_custom_call" | custom-call | tf_op jit(solution)/shard_map/finish/pallas_call | solution.py:288
  (17 shorter events, 0.1 us)
Async XLA Ops:
  0.6 7.7 %copy-start = (bf16[1,1,64,128,128]{4,3,2,1,0:T(8,128)(2,1)S(1)}, bf16[1,1,64,128,128]{4,3,2,1,0:T(8,128)(2,1)}, u32[]{:S(2)}) copy-start(bf16[1,1,64,128,128]{4,3,2,1,0:T(8,128)(2,1)} %param.10) | copy-start | bytes 6291460
  0.7 7.7 %copy-start.1 = (s32[1,16,16]{2,1,0:T(8,128)S(1)}, s32[1,16,16]{2,1,0:T(8,128)}, u32[]{:S(2)}) copy-start(s32[1,16,16]{2,1,0:T(8,128)} %param.12) | copy-start | bytes 3076
  0.7 7.7 %copy-start.2 = (bf16[1,16,16]{2,1,0:T(8,128)(2,1)S(1)}, bf16[1,16,16]{2,1,0:T(8,128)(2,1)}, u32[]{:S(2)}) copy-start(bf16[1,16,16]{2,1,0:T(8,128)(2,1)} %param.11) | copy-start | bytes 1540
  2.6 8.8 %copy-start.3 = (s32[1,16]{1,0:T(1,128)S(1)}, s32[1,16]{1,0:T(1,128)}, u32[]{:S(2)}) copy-start(s32[1,16]{1,0:T(1,128)} %sky.3) | copy-start | bytes 196
  2.6 8.8 %copy-start.4 = (s32[1,128]{1,0:T(1,128)S(1)}, s32[1,128]{1,0:T(1,128)}, u32[]{:S(2)}) copy-start(s32[1,128]{1,0:T(1,128)} %mask.3) | copy-start | bytes 1540
  2.6 8.7 %collective-permute-start = (bf16[16,4352]{1,0:T(8,128)(2,1)S(1)}, bf16[16,4352]{1,0:T(8,128)(2,1)S(1)}, u32[]{:S(2)}, u32[]{:S(2)}) collective-permute-start(bf16[16,4352]{1,0:T(8,128)(2,1)S(1)} %get-tuple-element.39), channel_id=1, source_target_pairs={{1,2},{3,4},{5,6},{2,1},{4,3},{6,5},{9,10},{11,12},{13,14},{10,9},... | collective-permute-start | bytes 417800 | tf_op jit(solution)/shard_map/ppermute | solution.py:335
  3.3 8.1 %collective-permute-start.1 = (bf16[16,4352]{1,0:T(8,128)(2,1)S(1)}, bf16[16,4352]{1,0:T(8,128)(2,1)S(1)}, u32[]{:S(2)}, u32[]{:S(2)}) collective-permute-start(bf16[16,4352]{1,0:T(8,128)(2,1)S(1)} %get-tuple-element.38), channel_id=1, source_target_pairs={{0,1},{1,0},{2,3},{3,2},{4,5},{5,4},{6,7},{7,6},{8,9},{9,8},{10,11... | collective-permute-start | bytes 417800 | tf_op jit(solution)/shard_map/ppermute | solution.py:306
  20.5 7.4 %collective-permute-start.2 = (f32[2,24,512]{2,1,0:T(8,128)S(1)}, f32[2,24,512]{2,1,0:T(8,128)S(1)}, u32[]{:S(2)}, u32[]{:S(2)}) collective-permute-start(f32[2,24,512]{2,1,0:T(8,128)S(1)} %get-tuple-element.25), channel_id=1, source_target_pairs={{0,2},{1,3},{2,0},{3,1},{4,6},{5,7},{6,4},{7,5},{8,10},{9,11},{10,... | collective-permute-start | bytes 294920 | tf_op jit(solution)/shard_map/ppermute | solution.py:306
  22.1 7.8 %collective-permute-start.3 = (f32[2,24,512]{2,1,0:T(8,128)S(1)}, f32[2,24,512]{2,1,0:T(8,128)S(1)}, u32[]{:S(2)}, u32[]{:S(2)}) collective-permute-start(f32[2,24,512]{2,1,0:T(8,128)S(1)} %get-tuple-element.26), channel_id=1, source_target_pairs={{0,4},{1,5},{2,6},{3,7},{4,0},{5,1},{6,2},{7,3},{8,12},{9,13},{10,... | collective-permute-start | bytes 294920 | tf_op jit(solution)/shard_map/ppermute | solution.py:306
  24.1 5.7 %collective-permute-start.4 = (f32[2,24,512]{2,1,0:T(8,128)S(1)}, f32[2,24,512]{2,1,0:T(8,128)S(1)}, u32[]{:S(2)}, u32[]{:S(2)}) collective-permute-start(f32[2,24,512]{2,1,0:T(8,128)S(1)} %get-tuple-element.27), channel_id=1, source_target_pairs={{0,6},{1,7},{2,4},{3,5},{4,2},{5,3},{6,0},{7,1},{8,14},{9,15},{10,... | collective-permute-start | bytes 294920 | tf_op jit(solution)/shard_map/ppermute | solution.py:306
  29.9 1.5 %collective-permute-start.5 = (f32[4,24,512]{2,1,0:T(8,128)S(1)}, f32[4,24,512]{2,1,0:T(8,128)S(1)}, u32[]{:S(2)}, u32[]{:S(2)}) collective-permute-start(f32[4,24,512]{2,1,0:T(8,128)S(1)} %pad_maximum_fusion), channel_id=1, source_target_pairs={{0,1},{1,0},{2,3},{3,2},{4,5},{5,4},{6,7},{7,6},{8,9},{9,8},{10,11... | collective-permute-start | bytes 589832 | tf_op jit(solution)/shard_map/ppermute | solution.py:306
  31.5 4.5 %collective-permute-start.6 = (f32[2,512]{1,0:T(2,128)S(1)}, f32[2,512]{1,0:T(2,128)S(1)}, u32[]{:S(2)}, u32[]{:S(2)}) collective-permute-start(f32[2,512]{1,0:T(2,128)S(1)} %fusion.4.rest_0_), channel_id=1, source_target_pairs={{0,8},{8,0},{16,24},{24,16},{1,9},{9,1},{17,25},{25,17},{2,10},{10... | collective-permute-start | bytes 12296 | tf_op jit(solution)/shard_map/ppermute | solution.py:306
  33.1 4.5 %collective-permute-start.7 = (f32[2,512]{1,0:T(2,128)S(1)}, f32[2,512]{1,0:T(2,128)S(1)}, u32[]{:S(2)}, u32[]{:S(2)}) collective-permute-start(f32[2,512]{1,0:T(2,128)S(1)} %fusion.4.rest_0_), channel_id=1, source_target_pairs={{0,16},{8,24},{16,0},{24,8},{1,17},{9,25},{17,1},{25,9},{2,18},{10... | collective-permute-start | bytes 12296 | tf_op jit(solution)/shard_map/ppermute | solution.py:306
  35.7 5.4 %collective-permute-start.8 = (f32[2,512]{1,0:T(2,128)S(1)}, f32[2,512]{1,0:T(2,128)S(1)}, u32[]{:S(2)}, u32[]{:S(2)}) collective-permute-start(f32[2,512]{1,0:T(2,128)S(1)} %fusion.4.rest_0_), channel_id=1, source_target_pairs={{0,24},{8,16},{16,8},{24,0},{1,25},{9,17},{17,9},{25,1},{2,26},{10... | collective-permute-start | bytes 12296 | tf_op jit(solution)/shard_map/ppermute | solution.py:306

commit v5 on v4

--- a/solution.py
+++ b/solution.py
@@ -127,7 +127,7 @@
 
 
 def relax_kernel(
-    groups, outer, inner, terms_own, first_own, mixed_own, turned, row_total, side, side_sum, wave, sky, mask, gain, *rest
+    groups, outer, inner, terms_own, first_own, mixed_own, turned, row_total, side, side_sum, wave, sky, mask, *rest
 ):
     outs = rest[: len(groups)]
     *columns_out, wpad, cpad, terms, first, inverse, flux, row_weight = rest[len(groups) :]
@@ -141,11 +141,17 @@
     owner = [me ^ s for _, _, s in flat]
     pairs = [(g, j) for g in range(len(flat)) for j in range(per // 2)]
 
+    last = outer.shape[1] // LANES - 1
     for g in range(len(flat)):
         for t in range(tiles + 2):
-            lanes = pl.ds(pl.multiple_of((owner[g] * tiles + t) * LANES, LANES), LANES)
+            tile = owner[g] * tiles + t - 1
+            lanes = pl.ds(pl.multiple_of(jnp.clip(tile, 0, last) * LANES, LANES), LANES)
             near = inner[:, lanes].astype(F32)
             far = outer[:, lanes].astype(F32)
+            if t == 0 or t == tiles + 1:
+                inside = jnp.logical_and(tile >= 0, tile <= last)
+                near = jnp.where(inside, near, 0.0)
+                far = jnp.where(inside, far, 0.0)
             below = jnp.where(odd, near, far)
             above = jnp.where(odd, far, near)
             for i, pad in ((0, cpad), (1, wpad)):
@@ -217,10 +223,7 @@
     for out in columns_out:
         for b in range(out.shape[0] // fibres):
             out[b * fibres : (b + 1) * fibres, :] = jnp.broadcast_to(mask_column(b * fibres), (fibres, LANES))
-    own = mask_column(me * fibres)
-    scale = gain[0]
-    chosen = is_sky * own * scale
-    pick = (chosen, chosen * scale)
+    chosen = is_sky * mask_column(me * fibres)
 
     margin = LW // 2
     for q, (g, j) in enumerate(pairs):
@@ -238,8 +241,8 @@
         outs[o][i, :fibres, half] = spectrum
         outs[o][i, fibres:, half] = jnp.concatenate(
             [
-                jnp.sum(pick[0] * strength * spectrum, axis=0, keepdims=True),
-                jnp.sum(pick[1] * strength, axis=0, keepdims=True),
+                jnp.sum(chosen * strength * spectrum, axis=0, keepdims=True),
+                jnp.sum(chosen * strength, axis=0, keepdims=True),
                 jnp.zeros((EXTRA - 2, LANES), F32),
             ],
             axis=0,
@@ -254,7 +257,7 @@
     near = pl.BlockSpec(memory_space=pltpu.VMEM)
     return pl.pallas_call(
         functools.partial(relax_kernel, groups),
-        in_specs=[near] * (3 + len(rest)) + [pl.BlockSpec(memory_space=pltpu.SMEM)],
+        in_specs=[near] * (4 + len(rest)),
         out_specs=[near] * (len(groups) + len(columns)),
         out_shape=[jax.ShapeDtypeStruct((len(group), fibres + EXTRA, width), F32) for group in groups]
         + [jax.ShapeDtypeStruct((count, LANES), F32) for count in columns],
@@ -268,7 +271,7 @@
 
 def finish_kernel(fibres, cameras, gain, mask, own, swapped, *rest):
     *blocks_in, calibrated, model = rest
-    totals = tree([part[...] for part in blocks_in[:cameras]])
+    totals = tree([part[...] for part in blocks_in[:cameras][::-1]])
     across = blocks_in[cameras:]
     me = lax.axis_index("patch")
     sky = totals[0:1, :] / (PRIOR + totals[1:2, :])
@@ -323,30 +326,34 @@
     me = lax.axis_index("patch")
     columns = pixel_counts.shape[1]
     wave = wave_profile[0, 0]
-    pixels = jnp.pad(
-        jnp.concatenate([pixel_counts[0], pixel_weights[0]], axis=0), ((0, 0), (LANES, LANES))
-    )
-    first = jnp.concatenate([pixels[:HALO], pixels[columns : columns + HALO]], axis=0)
-    final = jnp.concatenate([pixels[columns - HALO : columns], pixels[2 * columns - HALO :]], axis=0)
+    counts, weights = pixel_counts[0], pixel_weights[0]
+    first = jnp.concatenate([counts[:HALO], weights[:HALO]], axis=0)
+    final = jnp.concatenate([counts[columns - HALO :], weights[columns - HALO :]], axis=0)
     odd = me % 2 == 1
     outer = jnp.where(odd, final, first)
     inner = jnp.where(odd, first, final)
     far = [(i, i + 1) for i in range(1, parts - 1, 2)]
     outer = lax.ppermute(outer, "patch", far + [(b, a) for a, b in far])
     inner = swap(inner, "patch", 1)
+    pixels = jnp.pad(
+        jnp.concatenate([pixel_counts[0], pixel_weights[0]], axis=0), ((0, 0), (LANES, LANES))
+    )
     state = prepare(trace_columns[0], cross_profile[0], pixels, wave)
-    state = [*state, wave, sky_fibres, fibre_mask, throughput]
+    state = [*state, wave, sky_fibres, fibre_mask]
     away = relax([(s, s + 1) for s in range(2, parts, 2)], width, (), outer, inner, *state)
     across = [swap(block, "patch", 2 * t + 2) for t, block in enumerate(away)]
     state[0], *away = lax.optimization_barrier((state[0], *away))
     own, mate, mask = relax([(0,), (1,)], width, (fibre_mask.shape[1],), outer, inner, *state)
+    sky = slice(fibres, fibres + 2)
+    part, other = own[0, sky], mate[0, sky]
+    for block in across:
+        part, other = part + block[0, sky], other + block[1, sky]
+    other = swap(other, "patch", 1)
     swapped = swap(jnp.concatenate([mate] + [block[1:] for block in across], axis=0), "patch", 1)
-    sky = slice(fibres, fibres + 2)
-    part = own[0, sky] + jnp.sum(swapped[:, sky], axis=0)
-    for block in across:
-        part = part + block[0, sky]
+    part = part + other
+    part = part * jnp.stack([throughput, throughput * throughput])
     sums = [part] + [swap(part, "ccd", s) for s in range(1, cameras)]
-    calibrated, model = finish(fibres, throughput, mask, own, swapped, sums, across)
+    calibrated, model = finish(fibres, throughput, mask, own, swapped, sums[::-1], across)
     return calibrated[None], model[0]
 
 

time: 42.1 us -> 40.2 us (0.955)
  waiting for transfers between devices: 8.42 us -> 4.96 us
  local copies, waits for them, and re-layouts: 0.06 us -> 1 us
  starting transfers between devices: 13.2 us -> 13.7 us
    ppermute x8 -> x9, waiting for transfers between devices: 8.42 us -> 4.96 us  [swap(): lax.ppermute(values, axis, [(i, i ^ shift) for i in range(lax.axis_size(a...]
    slice x1, local copies, waits for them, and re-layouts: 0.02 us -> 0.96 us  [per_device(): weights[columns - HALO:]]
    ppermute x8 -> x9, starting transfers between devices: 12.6 us -> 12.9 us  [swap(): lax.ppermute(values, axis, [(i, i ^ shift) for i in range(lax.axis_size(a...]
  transfers between devices with their start and end apart: 9 -> 10, of which waited for: 4 -> 4; matrix products, arithmetic and copies ran while one was open for 0% -> 5% of each run, Pallas kernels for 16% -> 17%
where the time goes in v5:
time: 40.2 us; the launch traced here: 40 us
  Pallas kernels  16.9 us (42%)
  starting transfers between devices  13.7 us (34%)
  waiting for transfers between devices  4.96 us (12%)
  other arithmetic  1.9 us (5%)
  between operations  1.49 us (4%)
  local copies, waits for them, and re-layouts  1 us (2%)
    pallas_call x2, Pallas kernels, relax(): pl.pallas_call(functools.partial(relax_kernel, groups), in_specs=[near] *...  13.1 us
    ppermute x9, starting transfers between devices, swap(): lax.ppermute(values, axis, [(i, i ^ shift) for i in range(lax.axis_size(a...  12.9 us
    ppermute x9, waiting for transfers between devices, swap(): lax.ppermute(values, axis, [(i, i ^ shift) for i in range(lax.axis_size(a...  4.96 us
    pallas_call x1, Pallas kernels, prepare(): pl.pallas_call(prepare_kernel, in_specs=[near] * 4, out_specs=[near] * 7,...  3.01 us
    concatenate x1, other arithmetic, per_device(): jnp.concatenate([pixel_counts[0], pixel_weights[0]], axis=0)  1.69 us
    slice x1, local copies, waits for them, and re-layouts, per_device(): weights[columns - HALO:]  0.96 us
  transfers between devices with their start and end apart: 10, of which 4 were waited for; matrix products, arithmetic and copies ran while one was open for 5% of the time, Pallas kernels for 17%

profile of v5, /device:TPU:0, one launch (start us, length us, event | category | flops | bytes accessed | tf_op | source)
XLA Modules:
  0.0 40.0 jit_solution(8804343161330930520)
XLA Ops:
  0.6 1.0 %slice_bitcast_fusion.2 = (bf16[8,4096]{1,0:T(8,128)(2,1)S(1)}, bf16[8,4096]{1,0:T(8,128)(2,1)S(1)}, bf16[8,4096]{1,0:T(8,128)(2,1)S(1)}, bf16[8,4096]{1,0:T(8,128)(2,1)S(1)}) fusion(bf16[1,128,4096]{2,1,0:T(8,128)(2,1)} %param.9, bf16[1,128,4096]{2,1,0:T(8,128)(2,1)} %param.8), kind=kLoop, calls=%fused_computation.13 | loop fusion | bytes 524288 | tf_op jit(solution)/shard_map/slice | solution.py:331
  1.7 0.0 copy-start.1
  1.7 0.0 copy-start.2
  1.7 0.8 %collective-permute-start = (bf16[16,4096]{1,0:T(8,128)(2,1)S(1)}, bf16[16,4096]{1,0:T(8,128)(2,1)S(1)}, u32[]{:S(2)}, u32[]{:S(2)}) collective-permute-start(bf16[16,4096]{1,0:T(8,128)(2,1)S(1)} %get-tuple-element.39), channel_id=1, source_target_pairs={{1,2},{3,4},{5,6},{2,1},{4,3},{6,5},{9,10},{11,12},{13,14},{10,9},... | collective-permute-start | bytes 393224 | tf_op jit(solution)/shard_map/ppermute | solution.py:336
  2.5 4.4 %collective-permute-start.1 = (bf16[16,4096]{1,0:T(8,128)(2,1)S(1)}, bf16[16,4096]{1,0:T(8,128)(2,1)S(1)}, u32[]{:S(2)}, u32[]{:S(2)}) collective-permute-start(bf16[16,4096]{1,0:T(8,128)(2,1)S(1)} %get-tuple-element.38), channel_id=1, source_target_pairs={{0,1},{1,0},{2,3},{3,2},{4,5},{5,4},{6,7},{7,6},{8,9},{9,8},{10,11... | collective-permute-start | bytes 393224 | tf_op jit(solution)/shard_map/ppermute | solution.py:309
  6.9 1.7 %fusion.3.pixels = bf16[256,4352]{1,0:T(8,128)(2,1)S(1)} fusion(bf16[128,4096]{1,0:T(8,128)(2,1)} %bitcast.33, bf16[128,4096]{1,0:T(8,128)(2,1)} %bitcast.34), kind=kLoop, calls=%fused_computation.5 | loop fusion | flops 10027008 | bytes 4325376 | tf_op jit(solution)/shard_map/concatenate | solution.py:339
  8.6 0.0 copy-start.3
  9.3 3.0 %prepare.1 = (f32[64,256,128]{2,1,0:T(8,128)S(1)}, f32[64,16,128]{2,1,0:T(8,128)S(1)}, f32[64,16,128]{2,1,0:T(8,128)S(1)}, bf16[64,128,128]{2,1,0:T(8,128)(2,1)S...) custom-call(s32[16,16]{1,0:T(8,128)S(1)} %bitcast.31, ...), custom_call_target="tpu_custom_call" | custom-call | tf_op jit(solution)/shard_map/prepare/pallas_call | solution.py:107
  12.3 9.2 %relax.2 = (f32[2,24,512]{2,1,0:T(8,128)S(1)}, f32[2,24,512]{2,1,0:T(8,128)S(1)}, f32[2,24,512]{2,1,0:T(8,128)S(1)}) custom-call(bf16[16,4096]{1,0:T(8,128)(2,1)S(1)} %collective-permute-done.outer, bf16[16,4096]{1,0:T(8,128)(2,1)S(1)} %collective-permute-done.1.inner, f32[64,256,128]{2,1,0:T(8,128)S(1)} %get-tuple-element.28.terms_own, ...), custom_call_target="tpu_custom_call" | custom-call | tf_op jit(solution)/shard_map/relax/pallas_call | solution.py:258
  21.5 1.6 %collective-permute-start.2 = (f32[2,24,512]{2,1,0:T(8,128)S(1)}, f32[2,24,512]{2,1,0:T(8,128)S(1)}, u32[]{:S(2)}, u32[]{:S(2)}) collective-permute-start(f32[2,24,512]{2,1,0:T(8,128)S(1)} %get-tuple-element.25), channel_id=1, source_target_pairs={{0,2},{1,3},{2,0},{3,1},{4,6},{5,7},{6,4},{7,5},{8,10},{9,11},{10,... | collective-permute-start | bytes 294920 | tf_op jit(solution)/shard_map/ppermute | solution.py:309
  23.1 0.1 collective-permute-start.3
  23.2 1.9 %collective-permute-start.4 = (f32[2,24,512]{2,1,0:T(8,128)S(1)}, f32[2,24,512]{2,1,0:T(8,128)S(1)}, u32[]{:S(2)}, u32[]{:S(2)}) collective-permute-start(f32[2,24,512]{2,1,0:T(8,128)S(1)} %get-tuple-element.27), channel_id=1, source_target_pairs={{0,6},{1,7},{2,4},{3,5},{4,2},{5,3},{6,0},{7,1},{8,14},{9,15},{10,... | collective-permute-start | bytes 294920 | tf_op jit(solution)/shard_map/ppermute | solution.py:309
  25.1 0.1 maximum_bitcast_fusion
  25.2 3.9 %relax.3 = (f32[1,24,512]{2,1,0:T(8,128)S(1)}, f32[1,24,512]{2,1,0:T(8,128)S(1)}, f32[128,128]{1,0:T(8,128)S(1)}) custom-call(bf16[16,4096]{1,0:T(8,128)(2,1)S(1)} %collective-permute-done.outer, bf16[16,4096]{1,0:T(8,128)(2,1)S(1)} %collective-permute-done.1.inner, f32[64,256,128]{2,1,0:T(8,128)S(1)} %get-tuple-element.28.terms_own, ...), custom_call_target="tpu_custom_call" | custom-call | tf_op jit(solution)/shard_map/relax/pallas_call | solution.py:258
  29.0 0.7 %collective-permute-done.3.rest_5_ = f32[2,24,512]{2,1,0:T(8,128)S(1)} collective-permute-done((f32[2,24,512]{2,1,0:T(8,128)S(1)}, f32[2,24,512]{2,1,0:T(8,128)S(1)}, u32[]{:S(2)}, u32[]{:S(2)}) %collective-permute-start.3) | collective-permute-done | bytes 98336 | tf_op jit(solution)/shard_map/ppermute | solution.py:309
  29.7 0.1 collective-permute-start.6
  29.9 0.5 %collective-permute-start.5 = (f32[4,24,512]{2,1,0:T(8,128)S(1)}, f32[4,24,512]{2,1,0:T(8,128)S(1)}, u32[]{:S(2)}, u32[]{:S(2)}) collective-permute-start(f32[4,24,512]{2,1,0:T(8,128)S(1)} %pad_maximum_fusion), channel_id=1, source_target_pairs={{0,1},{1,0},{2,3},{3,2},{4,5},{5,4},{6,7},{7,6},{8,9},{9,8},{10,11... | collective-permute-start | bytes 589832 | tf_op jit(solution)/shard_map/ppermute | solution.py:309
  30.4 0.5 %collective-permute-done.6 = f32[2,512]{1,0:T(2,128)S(1)} collective-permute-done((f32[2,512]{1,0:T(2,128)S(1)}, f32[2,512]{1,0:T(2,128)S(1)}, u32[]{:S(2)}, u32[]{:S(2)}) %collective-permute-start.6) | collective-permute-done | bytes 4128 | tf_op jit(solution)/shard_map/ppermute | solution.py:309
  31.0 0.1 fusion.7.rest_3_
  31.0 3.6 %collective-permute-start.7 = (f32[2,512]{1,0:T(2,128)S(1)}, f32[2,512]{1,0:T(2,128)S(1)}, u32[]{:S(2)}, u32[]{:S(2)}) collective-permute-start(f32[2,512]{1,0:T(2,128)S(1)} %fusion.7.rest_3_), channel_id=1, source_target_pairs={{0,24},{8,16},{16,8},{24,0},{1,25},{9,17},{17,9},{25,1},{2,26},{10... | collective-permute-start | bytes 12296 | tf_op jit(solution)/shard_map/ppermute | solution.py:309
  34.7 0.8 %collective-permute-start.9 = (f32[2,512]{1,0:T(2,128)S(1)}, f32[2,512]{1,0:T(2,128)S(1)}, u32[]{:S(2)}, u32[]{:S(2)}) collective-permute-start(f32[2,512]{1,0:T(2,128)S(1)} %fusion.7.rest_3_), channel_id=1, source_target_pairs={{0,8},{8,0},{16,24},{24,16},{1,9},{9,1},{17,25},{25,17},{2,10},{10... | collective-permute-start | bytes 12296 | tf_op jit(solution)/shard_map/ppermute | solution.py:309
  35.4 1.0 %collective-permute-done.7.rest_0_ = f32[2,512]{1,0:T(2,128)S(1)} collective-permute-done((f32[2,512]{1,0:T(2,128)S(1)}, f32[2,512]{1,0:T(2,128)S(1)}, u32[]{:S(2)}, u32[]{:S(2)}) %collective-permute-start.7) | collective-permute-done | bytes 4128 | tf_op jit(solution)/shard_map/ppermute | solution.py:309
  36.5 2.7 %collective-permute-done.8.rest_1_ = f32[2,512]{1,0:T(2,128)S(1)} collective-permute-done((f32[2,512]{1,0:T(2,128)S(1)}, f32[2,512]{1,0:T(2,128)S(1)}, u32[]{:S(2)}, u32[]{:S(2)}) %collective-permute-start.8) | collective-permute-done | bytes 4128 | tf_op jit(solution)/shard_map/ppermute | solution.py:309
  39.2 0.8 %finish.1 = (f32[128,512]{1,0:T(8,128)}, f32[1,512]{1,0:T(1,128)}) custom-call(f32[1]{0:T(128)} %copy.10.gain, f32[128,128]{1,0:T(8,128)S(1)} %get-tuple-element.29.mask, f32[1,24,512]{2,1,0:T(8,128)S(1)} %get-tuple-element.30.own, f32[4,24,512]{2,1,0:T(8,128)S(1)} %collective-permute-done.5.swapped, f32[2,512]{1,0:T(2,128)S(1)} %collective-permute-done.7.rest_0_, ...), custom_call_target="tpu_custom_call" | custom-call | tf_op jit(solution)/shard_map/finish/pallas_call | solution.py:291
  (20 shorter events, 0.1 us)
Async XLA Ops:
  1.7 7.6 %copy-start = (bf16[1,1,64,128,128]{4,3,2,1,0:T(8,128)(2,1)S(1)}, bf16[1,1,64,128,128]{4,3,2,1,0:T(8,128)(2,1)}, u32[]{:S(2)}) copy-start(bf16[1,1,64,128,128]{4,3,2,1,0:T(8,128)(2,1)} %param.10) | copy-start | bytes 6291460
  1.7 7.6 %copy-start.1 = (s32[1,16,16]{2,1,0:T(8,128)S(1)}, s32[1,16,16]{2,1,0:T(8,128)}, u32[]{:S(2)}) copy-start(s32[1,16,16]{2,1,0:T(8,128)} %param.12) | copy-start | bytes 3076
  1.7 7.6 %copy-start.2 = (bf16[1,16,16]{2,1,0:T(8,128)(2,1)S(1)}, bf16[1,16,16]{2,1,0:T(8,128)(2,1)}, u32[]{:S(2)}) copy-start(bf16[1,16,16]{2,1,0:T(8,128)(2,1)} %param.11) | copy-start | bytes 1540
  1.7 10.6 %collective-permute-start = (bf16[16,4096]{1,0:T(8,128)(2,1)S(1)}, bf16[16,4096]{1,0:T(8,128)(2,1)S(1)}, u32[]{:S(2)}, u32[]{:S(2)}) collective-permute-start(bf16[16,4096]{1,0:T(8,128)(2,1)S(1)} %get-tuple-element.39), channel_id=1, source_target_pairs={{1,2},{3,4},{5,6},{2,1},{4,3},{6,5},{9,10},{11,12},{13,14},{10,9},... | collective-permute-start | bytes 393224 | tf_op jit(solution)/shard_map/ppermute | solution.py:336
  2.5 9.8 %collective-permute-start.1 = (bf16[16,4096]{1,0:T(8,128)(2,1)S(1)}, bf16[16,4096]{1,0:T(8,128)(2,1)S(1)}, u32[]{:S(2)}, u32[]{:S(2)}) collective-permute-start(bf16[16,4096]{1,0:T(8,128)(2,1)S(1)} %get-tuple-element.38), channel_id=1, source_target_pairs={{0,1},{1,0},{2,3},{3,2},{4,5},{5,4},{6,7},{7,6},{8,9},{9,8},{10,11... | collective-permute-start | bytes 393224 | tf_op jit(solution)/shard_map/ppermute | solution.py:309
  8.6 3.8 %copy-start.3 = (s32[1,16]{1,0:T(1,128)S(1)}, s32[1,16]{1,0:T(1,128)}, u32[]{:S(2)}) copy-start(s32[1,16]{1,0:T(1,128)} %sky.3) | copy-start | bytes 196
  8.6 3.8 %copy-start.4 = (s32[1,128]{1,0:T(1,128)S(1)}, s32[1,128]{1,0:T(1,128)}, u32[]{:S(2)}) copy-start(s32[1,128]{1,0:T(1,128)} %mask.3) | copy-start | bytes 1540
  21.5 7.5 %collective-permute-start.2 = (f32[2,24,512]{2,1,0:T(8,128)S(1)}, f32[2,24,512]{2,1,0:T(8,128)S(1)}, u32[]{:S(2)}, u32[]{:S(2)}) collective-permute-start(f32[2,24,512]{2,1,0:T(8,128)S(1)} %get-tuple-element.25), channel_id=1, source_target_pairs={{0,2},{1,3},{2,0},{3,1},{4,6},{5,7},{6,4},{7,5},{8,10},{9,11},{10,... | collective-permute-start | bytes 294920 | tf_op jit(solution)/shard_map/ppermute | solution.py:309
  23.1 6.6 %collective-permute-start.3 = (f32[2,24,512]{2,1,0:T(8,128)S(1)}, f32[2,24,512]{2,1,0:T(8,128)S(1)}, u32[]{:S(2)}, u32[]{:S(2)}) collective-permute-start(f32[2,24,512]{2,1,0:T(8,128)S(1)} %get-tuple-element.26), channel_id=1, source_target_pairs={{0,4},{1,5},{2,6},{3,7},{4,0},{5,1},{6,2},{7,3},{8,12},{9,13},{10,... | collective-permute-start | bytes 294920 | tf_op jit(solution)/shard_map/ppermute | solution.py:309
  23.2 6.5 %collective-permute-start.4 = (f32[2,24,512]{2,1,0:T(8,128)S(1)}, f32[2,24,512]{2,1,0:T(8,128)S(1)}, u32[]{:S(2)}, u32[]{:S(2)}) collective-permute-start(f32[2,24,512]{2,1,0:T(8,128)S(1)} %get-tuple-element.27), channel_id=1, source_target_pairs={{0,6},{1,7},{2,4},{3,5},{4,2},{5,3},{6,0},{7,1},{8,14},{9,15},{10,... | collective-permute-start | bytes 294920 | tf_op jit(solution)/shard_map/ppermute | solution.py:309
  29.7 1.2 %collective-permute-start.6 = (f32[2,512]{1,0:T(2,128)S(1)}, f32[2,512]{1,0:T(2,128)S(1)}, u32[]{:S(2)}, u32[]{:S(2)}) collective-permute-start(f32[2,512]{1,0:T(2,128)S(1)} %fusion.4), channel_id=1, source_target_pairs={{0,1},{1,0},{2,3},{3,2},{4,5},{5,4},{6,7},{7,6},{8,9},{9,8},{10,11... | collective-permute-start | bytes 12296 | tf_op jit(solution)/shard_map/ppermute | solution.py:309
  29.9 9.3 %collective-permute-start.5 = (f32[4,24,512]{2,1,0:T(8,128)S(1)}, f32[4,24,512]{2,1,0:T(8,128)S(1)}, u32[]{:S(2)}, u32[]{:S(2)}) collective-permute-start(f32[4,24,512]{2,1,0:T(8,128)S(1)} %pad_maximum_fusion), channel_id=1, source_target_pairs={{0,1},{1,0},{2,3},{3,2},{4,5},{5,4},{6,7},{7,6},{8,9},{9,8},{10,11... | collective-permute-start | bytes 589832 | tf_op jit(solution)/shard_map/ppermute | solution.py:309
  31.0 5.4 %collective-permute-start.7 = (f32[2,512]{1,0:T(2,128)S(1)}, f32[2,512]{1,0:T(2,128)S(1)}, u32[]{:S(2)}, u32[]{:S(2)}) collective-permute-start(f32[2,512]{1,0:T(2,128)S(1)} %fusion.7.rest_3_), channel_id=1, source_target_pairs={{0,24},{8,16},{16,8},{24,0},{1,25},{9,17},{17,9},{25,1},{2,26},{10... | collective-permute-start | bytes 12296 | tf_op jit(solution)/shard_map/ppermute | solution.py:309
  34.7 4.5 %collective-permute-start.8 = (f32[2,512]{1,0:T(2,128)S(1)}, f32[2,512]{1,0:T(2,128)S(1)}, u32[]{:S(2)}, u32[]{:S(2)}) collective-permute-start(f32[2,512]{1,0:T(2,128)S(1)} %fusion.7.rest_3_), channel_id=1, source_target_pairs={{0,16},{8,24},{16,0},{24,8},{1,17},{9,25},{17,1},{25,9},{2,18},{10... | collective-permute-start | bytes 12296 | tf_op jit(solution)/shard_map/ppermute | solution.py:309
  34.7 4.5 %collective-permute-start.9 = (f32[2,512]{1,0:T(2,128)S(1)}, f32[2,512]{1,0:T(2,128)S(1)}, u32[]{:S(2)}, u32[]{:S(2)}) collective-permute-start(f32[2,512]{1,0:T(2,128)S(1)} %fusion.7.rest_3_), channel_id=1, source_target_pairs={{0,8},{8,0},{16,24},{24,16},{1,9},{9,1},{17,25},{25,17},{2,10},{10... | collective-permute-start | bytes 12296 | tf_op jit(solution)/shard_map/ppermute | solution.py:309

commit v6 on v5

--- a/solution.py
+++ b/solution.py
@@ -272,14 +272,15 @@
 def finish_kernel(fibres, cameras, gain, mask, own, swapped, *rest):
     *blocks_in, calibrated, model = rest
     totals = tree([part[...] for part in blocks_in[:cameras][::-1]])
-    across = blocks_in[cameras:]
+    across = blocks_in[cameras:][::-1]
     me = lax.axis_index("patch")
     sky = totals[0:1, :] / (PRIOR + totals[1:2, :])
     model[...] = sky
-    blocks = {0: own[0, :fibres, :], 1: swapped[0, :fibres, :]}
+    last = len(across)
+    blocks = {0: own[0, :fibres, :], 1: swapped[last, :fibres, :]}
     for t, block in enumerate(across):
         blocks[2 * t + 2] = block[0, :fibres, :]
-        blocks[2 * t + 3] = swapped[t + 1, :fibres, :]
+        blocks[2 * t + 3] = swapped[last - 1 - t, :fibres, :]
     for s, block in blocks.items():
         at = pl.ds(pl.multiple_of((me ^ s) * fibres, fibres), fibres)
         calibrated[at, :] = mask[at, 0:1] * (block - gain[0] * sky)
@@ -346,14 +347,14 @@
     own, mate, mask = relax([(0,), (1,)], width, (fibre_mask.shape[1],), outer, inner, *state)
     sky = slice(fibres, fibres + 2)
     part, other = own[0, sky], mate[0, sky]
-    for block in across:
+    for block in across[::-1]:
         part, other = part + block[0, sky], other + block[1, sky]
     other = swap(other, "patch", 1)
-    swapped = swap(jnp.concatenate([mate] + [block[1:] for block in across], axis=0), "patch", 1)
+    swapped = swap(jnp.concatenate([block[1:] for block in across[::-1]] + [mate], axis=0), "patch", 1)
     part = part + other
     part = part * jnp.stack([throughput, throughput * throughput])
     sums = [part] + [swap(part, "ccd", s) for s in range(1, cameras)]
-    calibrated, model = finish(fibres, throughput, mask, own, swapped, sums[::-1], across)
+    calibrated, model = finish(fibres, throughput, mask, own, swapped, sums[::-1], across[::-1])
     return calibrated[None], model[0]
 
 

time: 40.2 us -> 39.8 us (0.990)
  transfers between devices with their start and end apart: 10 -> 10, of which waited for: 4 -> 5; matrix products, arithmetic and copies ran while one was open for 5% -> 5% of each run, Pallas kernels for 17% -> 17%
where the time goes in v6:
time: 39.8 us; the launch traced here: 39.6 us
  Pallas kernels  16.9 us (42%)
  starting transfers between devices  13.7 us (34%)
  waiting for transfers between devices  4.62 us (12%)
  other arithmetic  1.9 us (5%)
  between operations  1.49 us (4%)
  local copies, waits for them, and re-layouts  1 us (3%)
    pallas_call x2, Pallas kernels, relax(): pl.pallas_call(functools.partial(relax_kernel, groups), in_specs=[near] *...  13.1 us
    ppermute x9, starting transfers between devices, swap(): lax.ppermute(values, axis, [(i, i ^ shift) for i in range(lax.axis_size(a...  12.9 us
    ppermute x9, waiting for transfers between devices, swap(): lax.ppermute(values, axis, [(i, i ^ shift) for i in range(lax.axis_size(a...  4.62 us
    pallas_call x1, Pallas kernels, prepare(): pl.pallas_call(prepare_kernel, in_specs=[near] * 4, out_specs=[near] * 7,...  3.01 us
    concatenate x1, other arithmetic, per_device(): jnp.concatenate([pixel_counts[0], pixel_weights[0]], axis=0)  1.69 us
    slice x1, local copies, waits for them, and re-layouts, per_device(): weights[columns - HALO:]  0.96 us
    pallas_call x1, Pallas kernels, finish(): pl.pallas_call(functools.partial(finish_kernel, fibres, len(parts)), in_s...  0.8 us
    ppermute x1, starting transfers between devices, per_device(): outer = lax.ppermute(outer, 'patch', far + [(b, a) for a, b in far])  0.8 us
  transfers between devices with their start and end apart: 10, of which 5 were waited for; matrix products, arithmetic and copies ran while one was open for 5% of the time, Pallas kernels for 17%

profile of v6, /device:TPU:0, one launch (start us, length us, event | category | flops | bytes accessed | tf_op | source)
XLA Modules:
  0.0 39.6 jit_solution(8080227993196843683)
XLA Ops:
  0.6 1.0 %slice_bitcast_fusion.2 = (bf16[8,4096]{1,0:T(8,128)(2,1)S(1)}, bf16[8,4096]{1,0:T(8,128)(2,1)S(1)}, bf16[8,4096]{1,0:T(8,128)(2,1)S(1)}, bf16[8,4096]{1,0:T(8,128)(2,1)S(1)}) fusion(bf16[1,128,4096]{2,1,0:T(8,128)(2,1)} %param.9, bf16[1,128,4096]{2,1,0:T(8,128)(2,1)} %param.8), kind=kLoop, calls=%fused_computation.13 | loop fusion | bytes 524288 | tf_op jit(solution)/shard_map/slice | solution.py:332
  1.7 0.0 copy-start.1
  1.7 0.0 copy-start.2
  1.7 0.8 %collective-permute-start = (bf16[16,4096]{1,0:T(8,128)(2,1)S(1)}, bf16[16,4096]{1,0:T(8,128)(2,1)S(1)}, u32[]{:S(2)}, u32[]{:S(2)}) collective-permute-start(bf16[16,4096]{1,0:T(8,128)(2,1)S(1)} %get-tuple-element.39), channel_id=1, source_target_pairs={{1,2},{3,4},{5,6},{2,1},{4,3},{6,5},{9,10},{11,12},{13,14},{10,9},... | collective-permute-start | bytes 393224 | tf_op jit(solution)/shard_map/ppermute | solution.py:337
  2.5 4.4 %collective-permute-start.1 = (bf16[16,4096]{1,0:T(8,128)(2,1)S(1)}, bf16[16,4096]{1,0:T(8,128)(2,1)S(1)}, u32[]{:S(2)}, u32[]{:S(2)}) collective-permute-start(bf16[16,4096]{1,0:T(8,128)(2,1)S(1)} %get-tuple-element.38), channel_id=1, source_target_pairs={{0,1},{1,0},{2,3},{3,2},{4,5},{5,4},{6,7},{7,6},{8,9},{9,8},{10,11... | collective-permute-start | bytes 393224 | tf_op jit(solution)/shard_map/ppermute | solution.py:310
  6.9 1.7 %fusion.3.pixels = bf16[256,4352]{1,0:T(8,128)(2,1)S(1)} fusion(bf16[128,4096]{1,0:T(8,128)(2,1)} %bitcast.33, bf16[128,4096]{1,0:T(8,128)(2,1)} %bitcast.34), kind=kLoop, calls=%fused_computation.5 | loop fusion | flops 10027008 | bytes 4325376 | tf_op jit(solution)/shard_map/concatenate | solution.py:340
  9.3 3.0 %prepare.1 = (f32[64,256,128]{2,1,0:T(8,128)S(1)}, f32[64,16,128]{2,1,0:T(8,128)S(1)}, f32[64,16,128]{2,1,0:T(8,128)S(1)}, bf16[64,128,128]{2,1,0:T(8,128)(2,1)S...) custom-call(s32[16,16]{1,0:T(8,128)S(1)} %bitcast.31, ...), custom_call_target="tpu_custom_call" | custom-call | tf_op jit(solution)/shard_map/prepare/pallas_call | solution.py:107
  12.3 9.2 %relax.2 = (f32[2,24,512]{2,1,0:T(8,128)S(1)}, f32[2,24,512]{2,1,0:T(8,128)S(1)}, f32[2,24,512]{2,1,0:T(8,128)S(1)}) custom-call(bf16[16,4096]{1,0:T(8,128)(2,1)S(1)} %collective-permute-done.outer, bf16[16,4096]{1,0:T(8,128)(2,1)S(1)} %collective-permute-done.1.inner, f32[64,256,128]{2,1,0:T(8,128)S(1)} %get-tuple-element.28.terms_own, ...), custom_call_target="tpu_custom_call" | custom-call | tf_op jit(solution)/shard_map/relax/pallas_call | solution.py:258
  21.5 1.1 %collective-permute-start.2 = (f32[2,24,512]{2,1,0:T(8,128)S(1)}, f32[2,24,512]{2,1,0:T(8,128)S(1)}, u32[]{:S(2)}, u32[]{:S(2)}) collective-permute-start(f32[2,24,512]{2,1,0:T(8,128)S(1)} %get-tuple-element.27), channel_id=1, source_target_pairs={{0,6},{1,7},{2,4},{3,5},{4,2},{5,3},{6,0},{7,1},{8,14},{9,15},{10,... | collective-permute-start | bytes 294920 | tf_op jit(solution)/shard_map/ppermute | solution.py:310
  22.7 1.9 %collective-permute-start.3 = (f32[2,24,512]{2,1,0:T(8,128)S(1)}, f32[2,24,512]{2,1,0:T(8,128)S(1)}, u32[]{:S(2)}, u32[]{:S(2)}) collective-permute-start(f32[2,24,512]{2,1,0:T(8,128)S(1)} %get-tuple-element.26), channel_id=1, source_target_pairs={{0,4},{1,5},{2,6},{3,7},{4,0},{5,1},{6,2},{7,3},{8,12},{9,13},{10,... | collective-permute-start | bytes 294920 | tf_op jit(solution)/shard_map/ppermute | solution.py:310
  24.6 0.5 %collective-permute-start.4 = (f32[2,24,512]{2,1,0:T(8,128)S(1)}, f32[2,24,512]{2,1,0:T(8,128)S(1)}, u32[]{:S(2)}, u32[]{:S(2)}) collective-permute-start(f32[2,24,512]{2,1,0:T(8,128)S(1)} %get-tuple-element.25), channel_id=1, source_target_pairs={{0,2},{1,3},{2,0},{3,1},{4,6},{5,7},{6,4},{7,5},{8,10},{9,11},{10,... | collective-permute-start | bytes 294920 | tf_op jit(solution)/shard_map/ppermute | solution.py:310
  25.1 0.1 maximum_bitcast_fusion
  25.2 3.9 %relax.3 = (f32[1,24,512]{2,1,0:T(8,128)S(1)}, f32[1,24,512]{2,1,0:T(8,128)S(1)}, f32[128,128]{1,0:T(8,128)S(1)}) custom-call(bf16[16,4096]{1,0:T(8,128)(2,1)S(1)} %collective-permute-done.outer, bf16[16,4096]{1,0:T(8,128)(2,1)S(1)} %collective-permute-done.1.inner, f32[64,256,128]{2,1,0:T(8,128)S(1)} %get-tuple-element.28.terms_own, ...), custom_call_target="tpu_custom_call" | custom-call | tf_op jit(solution)/shard_map/relax/pallas_call | solution.py:258
  29.0 0.3 collective-permute-done.3.rest_5_
  29.3 0.1 collective-permute-done.4.rest_6_
  29.4 0.1 collective-permute-start.6
  29.5 0.5 %collective-permute-start.5 = (f32[4,24,512]{2,1,0:T(8,128)S(1)}, f32[4,24,512]{2,1,0:T(8,128)S(1)}, u32[]{:S(2)}, u32[]{:S(2)}) collective-permute-start(f32[4,24,512]{2,1,0:T(8,128)S(1)} %pad_maximum_fusion), channel_id=1, source_target_pairs={{0,1},{1,0},{2,3},{3,2},{4,5},{5,4},{6,7},{7,6},{8,9},{9,8},{10,11... | collective-permute-start | bytes 589832 | tf_op jit(solution)/shard_map/ppermute | solution.py:310
  30.1 0.5 %collective-permute-done.6 = f32[2,512]{1,0:T(2,128)S(1)} collective-permute-done((f32[2,512]{1,0:T(2,128)S(1)}, f32[2,512]{1,0:T(2,128)S(1)}, u32[]{:S(2)}, u32[]{:S(2)}) %collective-permute-start.6) | collective-permute-done | bytes 4128 | tf_op jit(solution)/shard_map/ppermute | solution.py:310
  30.6 0.1 fusion.7.rest_3_
  30.7 3.6 %collective-permute-start.7 = (f32[2,512]{1,0:T(2,128)S(1)}, f32[2,512]{1,0:T(2,128)S(1)}, u32[]{:S(2)}, u32[]{:S(2)}) collective-permute-start(f32[2,512]{1,0:T(2,128)S(1)} %fusion.7.rest_3_), channel_id=1, source_target_pairs={{0,24},{8,16},{16,8},{24,0},{1,25},{9,17},{17,9},{25,1},{2,26},{10... | collective-permute-start | bytes 12296 | tf_op jit(solution)/shard_map/ppermute | solution.py:310
  34.3 0.8 %collective-permute-start.9 = (f32[2,512]{1,0:T(2,128)S(1)}, f32[2,512]{1,0:T(2,128)S(1)}, u32[]{:S(2)}, u32[]{:S(2)}) collective-permute-start(f32[2,512]{1,0:T(2,128)S(1)} %fusion.7.rest_3_), channel_id=1, source_target_pairs={{0,8},{8,0},{16,24},{24,16},{1,9},{9,1},{17,25},{25,17},{2,10},{10... | collective-permute-start | bytes 12296 | tf_op jit(solution)/shard_map/ppermute | solution.py:310
  35.1 1.0 %collective-permute-done.7.rest_0_ = f32[2,512]{1,0:T(2,128)S(1)} collective-permute-done((f32[2,512]{1,0:T(2,128)S(1)}, f32[2,512]{1,0:T(2,128)S(1)}, u32[]{:S(2)}, u32[]{:S(2)}) %collective-permute-start.7) | collective-permute-done | bytes 4128 | tf_op jit(solution)/shard_map/ppermute | solution.py:310
  36.1 2.7 %collective-permute-done.8.rest_1_ = f32[2,512]{1,0:T(2,128)S(1)} collective-permute-done((f32[2,512]{1,0:T(2,128)S(1)}, f32[2,512]{1,0:T(2,128)S(1)}, u32[]{:S(2)}, u32[]{:S(2)}) %collective-permute-start.8) | collective-permute-done | bytes 4128 | tf_op jit(solution)/shard_map/ppermute | solution.py:310
  38.8 0.8 %finish.1 = (f32[128,512]{1,0:T(8,128)}, f32[1,512]{1,0:T(1,128)}) custom-call(f32[1]{0:T(128)} %copy.10.gain, f32[128,128]{1,0:T(8,128)S(1)} %get-tuple-element.29.mask, f32[1,24,512]{2,1,0:T(8,128)S(1)} %get-tuple-element.30.own, f32[4,24,512]{2,1,0:T(8,128)S(1)} %collective-permute-done.5.swapped, f32[2,512]{1,0:T(2,128)S(1)} %collective-permute-done.7.rest_0_, ...), custom_call_target="tpu_custom_call" | custom-call | tf_op jit(solution)/shard_map/finish/pallas_call | solution.py:292
  (20 shorter events, 0.1 us)
Async XLA Ops:
  1.7 7.6 %copy-start = (bf16[1,1,64,128,128]{4,3,2,1,0:T(8,128)(2,1)S(1)}, bf16[1,1,64,128,128]{4,3,2,1,0:T(8,128)(2,1)}, u32[]{:S(2)}) copy-start(bf16[1,1,64,128,128]{4,3,2,1,0:T(8,128)(2,1)} %param.10) | copy-start | bytes 6291460
  1.7 7.6 %copy-start.1 = (s32[1,16,16]{2,1,0:T(8,128)S(1)}, s32[1,16,16]{2,1,0:T(8,128)}, u32[]{:S(2)}) copy-start(s32[1,16,16]{2,1,0:T(8,128)} %param.12) | copy-start | bytes 3076
  1.7 7.6 %copy-start.2 = (bf16[1,16,16]{2,1,0:T(8,128)(2,1)S(1)}, bf16[1,16,16]{2,1,0:T(8,128)(2,1)}, u32[]{:S(2)}) copy-start(bf16[1,16,16]{2,1,0:T(8,128)(2,1)} %param.11) | copy-start | bytes 1540
  1.7 10.6 %collective-permute-start = (bf16[16,4096]{1,0:T(8,128)(2,1)S(1)}, bf16[16,4096]{1,0:T(8,128)(2,1)S(1)}, u32[]{:S(2)}, u32[]{:S(2)}) collective-permute-start(bf16[16,4096]{1,0:T(8,128)(2,1)S(1)} %get-tuple-element.39), channel_id=1, source_target_pairs={{1,2},{3,4},{5,6},{2,1},{4,3},{6,5},{9,10},{11,12},{13,14},{10,9},... | collective-permute-start | bytes 393224 | tf_op jit(solution)/shard_map/ppermute | solution.py:337
  2.5 9.8 %collective-permute-start.1 = (bf16[16,4096]{1,0:T(8,128)(2,1)S(1)}, bf16[16,4096]{1,0:T(8,128)(2,1)S(1)}, u32[]{:S(2)}, u32[]{:S(2)}) collective-permute-start(bf16[16,4096]{1,0:T(8,128)(2,1)S(1)} %get-tuple-element.38), channel_id=1, source_target_pairs={{0,1},{1,0},{2,3},{3,2},{4,5},{5,4},{6,7},{7,6},{8,9},{9,8},{10,11... | collective-permute-start | bytes 393224 | tf_op jit(solution)/shard_map/ppermute | solution.py:310
  8.6 3.8 %copy-start.3 = (s32[1,16]{1,0:T(1,128)S(1)}, s32[1,16]{1,0:T(1,128)}, u32[]{:S(2)}) copy-start(s32[1,16]{1,0:T(1,128)} %sky.3) | copy-start | bytes 196
  8.6 3.8 %copy-start.4 = (s32[1,128]{1,0:T(1,128)S(1)}, s32[1,128]{1,0:T(1,128)}, u32[]{:S(2)}) copy-start(s32[1,128]{1,0:T(1,128)} %mask.3) | copy-start | bytes 1540
  21.5 7.5 %collective-permute-start.2 = (f32[2,24,512]{2,1,0:T(8,128)S(1)}, f32[2,24,512]{2,1,0:T(8,128)S(1)}, u32[]{:S(2)}, u32[]{:S(2)}) collective-permute-start(f32[2,24,512]{2,1,0:T(8,128)S(1)} %get-tuple-element.27), channel_id=1, source_target_pairs={{0,6},{1,7},{2,4},{3,5},{4,2},{5,3},{6,0},{7,1},{8,14},{9,15},{10,... | collective-permute-start | bytes 294920 | tf_op jit(solution)/shard_map/ppermute | solution.py:310
  22.7 6.7 %collective-permute-start.3 = (f32[2,24,512]{2,1,0:T(8,128)S(1)}, f32[2,24,512]{2,1,0:T(8,128)S(1)}, u32[]{:S(2)}, u32[]{:S(2)}) collective-permute-start(f32[2,24,512]{2,1,0:T(8,128)S(1)} %get-tuple-element.26), channel_id=1, source_target_pairs={{0,4},{1,5},{2,6},{3,7},{4,0},{5,1},{6,2},{7,3},{8,12},{9,13},{10,... | collective-permute-start | bytes 294920 | tf_op jit(solution)/shard_map/ppermute | solution.py:310
  24.6 4.8 %collective-permute-start.4 = (f32[2,24,512]{2,1,0:T(8,128)S(1)}, f32[2,24,512]{2,1,0:T(8,128)S(1)}, u32[]{:S(2)}, u32[]{:S(2)}) collective-permute-start(f32[2,24,512]{2,1,0:T(8,128)S(1)} %get-tuple-element.25), channel_id=1, source_target_pairs={{0,2},{1,3},{2,0},{3,1},{4,6},{5,7},{6,4},{7,5},{8,10},{9,11},{10,... | collective-permute-start | bytes 294920 | tf_op jit(solution)/shard_map/ppermute | solution.py:310
  29.4 1.2 %collective-permute-start.6 = (f32[2,512]{1,0:T(2,128)S(1)}, f32[2,512]{1,0:T(2,128)S(1)}, u32[]{:S(2)}, u32[]{:S(2)}) collective-permute-start(f32[2,512]{1,0:T(2,128)S(1)} %fusion.4), channel_id=1, source_target_pairs={{0,1},{1,0},{2,3},{3,2},{4,5},{5,4},{6,7},{7,6},{8,9},{9,8},{10,11... | collective-permute-start | bytes 12296 | tf_op jit(solution)/shard_map/ppermute | solution.py:310
  29.5 9.3 %collective-permute-start.5 = (f32[4,24,512]{2,1,0:T(8,128)S(1)}, f32[4,24,512]{2,1,0:T(8,128)S(1)}, u32[]{:S(2)}, u32[]{:S(2)}) collective-permute-start(f32[4,24,512]{2,1,0:T(8,128)S(1)} %pad_maximum_fusion), channel_id=1, source_target_pairs={{0,1},{1,0},{2,3},{3,2},{4,5},{5,4},{6,7},{7,6},{8,9},{9,8},{10,11... | collective-permute-start | bytes 589832 | tf_op jit(solution)/shard_map/ppermute | solution.py:310
  30.7 5.4 %collective-permute-start.7 = (f32[2,512]{1,0:T(2,128)S(1)}, f32[2,512]{1,0:T(2,128)S(1)}, u32[]{:S(2)}, u32[]{:S(2)}) collective-permute-start(f32[2,512]{1,0:T(2,128)S(1)} %fusion.7.rest_3_), channel_id=1, source_target_pairs={{0,24},{8,16},{16,8},{24,0},{1,25},{9,17},{17,9},{25,1},{2,26},{10... | collective-permute-start | bytes 12296 | tf_op jit(solution)/shard_map/ppermute | solution.py:310
  34.3 4.5 %collective-permute-start.8 = (f32[2,512]{1,0:T(2,128)S(1)}, f32[2,512]{1,0:T(2,128)S(1)}, u32[]{:S(2)}, u32[]{:S(2)}) collective-permute-start(f32[2,512]{1,0:T(2,128)S(1)} %fusion.7.rest_3_), channel_id=1, source_target_pairs={{0,16},{8,24},{16,0},{24,8},{1,17},{9,25},{17,1},{25,9},{2,18},{10... | collective-permute-start | bytes 12296 | tf_op jit(solution)/shard_map/ppermute | solution.py:310
  34.3 4.5 %collective-permute-start.9 = (f32[2,512]{1,0:T(2,128)S(1)}, f32[2,512]{1,0:T(2,128)S(1)}, u32[]{:S(2)}, u32[]{:S(2)}) collective-permute-start(f32[2,512]{1,0:T(2,128)S(1)} %fusion.7.rest_3_), channel_id=1, source_target_pairs={{0,8},{8,0},{16,24},{24,16},{1,9},{9,1},{17,25},{25,17},{2,10},{10... | collective-permute-start | bytes 12296 | tf_op jit(solution)/shard_map/ppermute | solution.py:310
